TPU v7x, 32 devices: a whole 2x2x4 slice. The times are simulated.
32 devices in a mesh: dp: 8 (over z, x), mp: 4 (over y, core).
Axes of the slice: x: 2, y: 2, z: 4, core: 2. Of those that a mesh axis runs over, the one named last changes fastest.
Arguments:
- tokens: bfloat16 [8, 1536, 768], P('dp', 'mp'), may hold values from -6 to 6
- cotangent: bfloat16 [8, 1536, 768], P('dp', 'mp'), may hold values from -6 to 6
- w_qkv: bfloat16 [2, 768, 2304], replicated, may hold values from -0.21875 to 0.21875
- w_attn: bfloat16 [2, 768, 768], replicated, may hold values from -3.5 to 3.5
- attn_gain: float32 [2, 768], replicated, may hold values from 0.5 to 1.5
- rel_bias: float32 [2, 12, 32], replicated, may hold values from -4 to 4
- ffn_gain: float32 [2, 768], replicated, may hold values from 0.5 to 1.5
- router: bfloat16 [2, 768, 16], replicated, may hold values from -0.21875 to 0.21875
- w_in: bfloat16 [2, 16, 768, 3072], P(None, 'dp', None, 'mp'), may hold values from -0.21875 to 0.21875
- w_out: bfloat16 [2, 16, 3072, 768], P(None, 'dp', 'mp'), may hold values from -0.109375 to 0.109375
- cont_lengths: int32 [8, 8], P('dp'), may hold values from 1 to 128, 512 in all within a row
- routes: int32 [2, 8, 1536, 2], P(None, 'dp', 'mp'), may hold values from 0 to 15, as said below
- slots: int32 [2, 8, 1536, 2], P(None, 'dp', 'mp'), may hold values from 0 to 53, as said below
- drops: int32 [2, 8, 1536, 2], P(None, 'dp', 'mp'), may hold values from 0 to 1, as said below
Outputs:
- output: bfloat16 [8, 1536, 768], P('dp', 'mp')
- input_grad: float32 [8, 1536, 768], P('dp', 'mp')
- grad_w_qkv: float32 [2, 768, 2304], replicated
- grad_w_attn: float32 [2, 768, 768], replicated
- grad_attn_gain: float32 [2, 768], replicated
- grad_rel_bias: float32 [2, 12, 32], replicated
- grad_ffn_gain: float32 [2, 768], replicated
- grad_router: float32 [2, 768, 16], replicated
- grad_w_in: float32 [2, 16, 768, 3072], P(None, 'dp', None, 'mp')
- grad_w_out: float32 [2, 16, 3072, 768], P(None, 'dp', 'mp')
Inputs may be any that keep to these rules, and one draw needn't show every extreme that they name: `cont_lengths`: each row sums to 512; its largest entry is 128. `routes`: a token's two experts differ; in every layer one expert is named by 54 or more tokens of every device. Among the kept pairs of one device that name one expert the slots are distinct; dropped pairs have slot 0; in every layer one expert receives exactly 54 kept pairs from every device. `drops`: a pair is dropped only where its expert already holds 54 kept pairs of the same device.
All inputs are finite; a program needn't handle non-finite values.
Results may differ from a plain program's by a relative error of at most 0.022.
Values may be sent and summed in bfloat16 or wider, within the bound.
A program may use at most 384 MiB of HBM per device.

v0:
```python
import jax
import jax.numpy as jnp
from jax import lax
from jax.sharding import PartitionSpec as P

PROMPT = 1024


EPSILON = 1e-06
SQRT_TWO_PI = 0.7978845608028654
THRESHOLDS = (16, 20, 24, 32, 40, 48, 64, 80, 96, 128, 160, 192, 256, 384, 512, 768)
HIGHEST = lax.Precision.HIGHEST


def rms_scale(values, gain_row):
    return (
        values * lax.rsqrt(jnp.mean(values * values, axis=-1, keepdims=True) + EPSILON) * gain_row
    )


def gelu_tanh(values):
    return (
        0.5
        * values
        * (1.0 + jnp.tanh(SQRT_TWO_PI * (values + 0.044715 * values * values * values)))
    )


def bucket_of(distance):
    counted = jnp.minimum(distance, 15)
    for threshold in THRESHOLDS:
        counted = counted + (distance >= threshold).astype(jnp.int32)
    return counted


def geometry(lengths, row_ids):
    starts = PROMPT + jnp.cumsum(lengths, axis=-1) - lengths
    inside = row_ids[None, :, None] >= starts[:, None, :]
    segment = jnp.sum(inside.astype(jnp.int32), axis=-1) - 1
    begin_at = jnp.max(jnp.where(inside, starts[:, None, :], 0), axis=-1)
    position = jnp.where(
        row_ids[None, :] < PROMPT, row_ids[None, :], PROMPT + row_ids[None, :] - begin_at
    )
    return (position, segment)


def visibility(query_pos, query_seg, key_pos, key_seg):
    query_at = query_pos[:, :, None]
    query_in = query_seg[:, :, None]
    key_at = key_pos[:, None, :]
    key_in = key_seg[:, None, :]
    earlier = key_at <= query_at
    allowed = (key_in < 0) & ((query_in >= 0) | earlier) | (key_in >= 0) & (
        key_in == query_in
    ) & earlier
    bucket = bucket_of(jnp.maximum(query_at - key_at, 0))
    return (allowed, bucket)


def bias_table(bias_row, bucket):
    full_bias = jnp.zeros((bias_row.shape[0],) + bucket.shape, jnp.float32)
    for number in range(bias_row.shape[1]):
        full_bias = full_bias + jnp.where(
            bucket[None] == number, bias_row[:, number][:, None, None, None], 0.0
        )
    return full_bias


def score_block(query_b, key_every, full_bias, allowed, factor):
    raw = (
        jnp.einsum("grhd,gkhd->hgrk", query_b, key_every, preferred_element_type=jnp.float32)
        * factor
    )
    raw = raw + full_bias
    return jnp.where(allowed[None], raw, -1e30)


def body(
    tokens,
    cotangent,
    w_qkv,
    w_attn,
    attn_gain,
    rel_bias,
    ffn_gain,
    router,
    w_in,
    w_out,
    cont_lengths,
    routes,
    slots,
    drops,
):
    groups, local_rows, model_width = tokens.shape
    head_count = rel_bias.shape[1]
    bucket_count = rel_bias.shape[2]
    head_size = model_width // head_count
    factor = head_size ** (-0.5)
    layer_count = w_qkv.shape[0]
    dp_count = lax.axis_size("dp")
    mp_count = lax.axis_size("mp")
    seq_len = local_rows * mp_count
    local_experts = w_in.shape[1]
    expert_total = local_experts * dp_count
    tok_count = groups * local_rows
    capacity = max(2, 9 * 2 * tok_count // (8 * expert_total))
    slot_total = expert_total * capacity
    rows_here = lax.axis_index("mp") * local_rows + jnp.arange(local_rows, dtype=jnp.int32)
    rows_every = jnp.arange(seq_len, dtype=jnp.int32)
    query_pos, query_seg = geometry(cont_lengths, rows_here)
    key_pos, key_seg = geometry(cont_lengths, rows_every)
    allowed, bucket = visibility(query_pos, query_seg, key_pos, key_seg)
    route_all = routes.reshape(layer_count, tok_count, 2)
    slot_all = slots.reshape(layer_count, tok_count, 2)
    keep_all = (1 - drops.reshape(layer_count, tok_count, 2)).astype(jnp.float32)
    head_shape = (groups, seq_len, head_count, head_size)
    stream = tokens.reshape(tok_count, model_width).astype(jnp.float32)
    stored = []
    for layer_now in range(layer_count):
        normed_b = rms_scale(stream, attn_gain[layer_now]).astype(jnp.bfloat16)
        qkv_all = jnp.dot(normed_b, w_qkv[layer_now], preferred_element_type=jnp.float32).astype(
            jnp.bfloat16
        )
        query_b = qkv_all[:, :model_width].reshape(groups, local_rows, head_count, head_size)
        key_own = qkv_all[:, model_width : 2 * model_width].reshape(groups, local_rows, model_width)
        value_own = qkv_all[:, 2 * model_width :].reshape(groups, local_rows, model_width)
        key_every, value_every = (
            lax.all_gather(key_own, "mp", axis=1, tiled=True),
            lax.all_gather(value_own, "mp", axis=1, tiled=True),
        )
        key_every = key_every.reshape(head_shape)
        value_every = value_every.reshape(head_shape)
        full_bias = bias_table(rel_bias[layer_now], bucket)
        scores = score_block(query_b, key_every, full_bias, allowed, factor)
        top_score = jnp.max(scores, axis=-1, keepdims=True)
        weights = jnp.exp(scores - top_score)
        weight_sum = jnp.sum(weights, axis=-1, keepdims=True)
        log_total = top_score + jnp.log(weight_sum)
        probs_b = (weights / weight_sum).astype(jnp.bfloat16)
        mixed_b = jnp.einsum(
            "hgrk,gkhd->grhd", probs_b, value_every, preferred_element_type=jnp.float32
        )
        mixed_b = mixed_b.reshape(tok_count, model_width).astype(jnp.bfloat16)
        middle = stream + jnp.dot(mixed_b, w_attn[layer_now], preferred_element_type=jnp.float32)
        kept_keys = (key_every, value_every)
        ffn_b = rms_scale(middle, ffn_gain[layer_now]).astype(jnp.bfloat16)
        logits = jnp.dot(ffn_b, router[layer_now], preferred_element_type=jnp.float32)
        chosen = route_all[layer_now]
        keep_pair = keep_all[layer_now]
        gate_pair = jax.nn.softmax(jnp.take_along_axis(logits, chosen, axis=1), axis=-1)
        target = chosen * capacity + slot_all[layer_now]
        sending = jnp.where(
            keep_pair[:, :, None] > 0, ffn_b[:, None, :], jnp.zeros((), jnp.bfloat16)
        )
        send_rows = (
            jnp.zeros((slot_total, model_width), jnp.bfloat16)
            .at[target.reshape(-1)]
            .add(sending.reshape(-1, model_width))
        )
        arrived = lax.all_to_all(
            send_rows.reshape(dp_count, local_experts, capacity, model_width),
            "dp",
            split_axis=0,
            concat_axis=0,
            tiled=True,
        )
        rows_in = lax.all_gather(arrived, "mp", axis=0, tiled=True)
        up_block = w_in[layer_now]
        down_block = w_out[layer_now]
        inner_act = jnp.einsum(
            "secd,edf->secf", rows_in, up_block, preferred_element_type=jnp.float32
        )
        hidden_b = gelu_tanh(inner_act).astype(jnp.bfloat16)
        summed = lax.psum_scatter(
            jnp.einsum(
                "secf,efd->secd", hidden_b, down_block, preferred_element_type=jnp.float32
            ).astype(jnp.bfloat16),
            "mp",
            scatter_dimension=0,
            tiled=True,
        )
        kept_rows = (rows_in, inner_act, hidden_b)
        returned = lax.all_to_all(summed, "dp", split_axis=0, concat_axis=0, tiled=True).reshape(
            slot_total, model_width
        )
        pair_out = returned[target].astype(jnp.float32)
        stored.append(
            (
                stream,
                normed_b,
                query_b,
                key_own,
                value_own,
                kept_keys,
                log_total,
                mixed_b,
                middle,
                ffn_b,
                chosen,
                keep_pair,
                gate_pair,
                target,
                pair_out,
                kept_rows,
                full_bias,
            )
        )
        stream = middle + jnp.sum((gate_pair * keep_pair)[:, :, None] * pair_out, axis=1)
    output = stream.astype(jnp.bfloat16).reshape(groups, local_rows, model_width)
    one_hot = (
        bucket[None] == jnp.arange(bucket_count, dtype=jnp.int32)[:, None, None, None]
    ).astype(jnp.bfloat16)
    expert_ids = jnp.arange(expert_total, dtype=jnp.int32)
    qkv_grads = [None] * layer_count
    attn_grads = [None] * layer_count
    attn_gain_grads = [None] * layer_count
    bias_grads = [None] * layer_count
    ffn_gain_grads = [None] * layer_count
    router_grads = [None] * layer_count
    up_grads = [None] * layer_count
    down_grads = [None] * layer_count
    flowing = cotangent.reshape(tok_count, model_width).astype(jnp.float32)
    for layer_now in reversed(range(layer_count)):
        (
            stream_in,
            normed_b,
            query_b,
            key_own,
            value_own,
            kept_keys,
            log_total,
            mixed_b,
            middle,
            ffn_b,
            chosen,
            keep_pair,
            gate_pair,
            target,
            pair_out,
            kept_rows,
            full_bias,
        ) = stored[layer_now]
        weighted = gate_pair * keep_pair
        pair_grad = weighted[:, :, None] * flowing[:, None, :]
        gate_grad = keep_pair * jnp.sum(flowing[:, None, :] * pair_out, axis=-1)
        picked_grad = gate_pair * (
            gate_grad - jnp.sum(gate_pair * gate_grad, axis=-1, keepdims=True)
        )
        logit_grad = jnp.sum(
            picked_grad[:, :, None] * (chosen[:, :, None] == expert_ids).astype(jnp.float32), axis=1
        )
        back_rows = (
            jnp.zeros((slot_total, model_width), jnp.float32)
            .at[target.reshape(-1)]
            .add(pair_grad.reshape(-1, model_width))
        )
        back_rows = back_rows.astype(jnp.bfloat16).reshape(
            dp_count, local_experts, capacity, model_width
        )
        grad_arrived = lax.all_to_all(back_rows, "dp", split_axis=0, concat_axis=0, tiled=True)
        grad_rows = lax.all_gather(grad_arrived, "mp", axis=0, tiled=True)
        up_block = w_in[layer_now]
        down_block = w_out[layer_now]
        rows_in, inner_act, hidden_b = kept_rows
        down_grad = jnp.einsum(
            "secf,secd->efd", hidden_b, grad_rows, preferred_element_type=jnp.float32
        )
        hidden_grad = jnp.einsum(
            "secd,efd->secf", grad_rows, down_block, preferred_element_type=jnp.float32
        )
        inner_grad = jax.vjp(gelu_tanh, inner_act)[1](hidden_grad)[0].astype(jnp.bfloat16)
        up_grad = jnp.einsum(
            "secd,secf->edf", rows_in, inner_grad, preferred_element_type=jnp.float32
        )
        rows_grad = lax.psum_scatter(
            jnp.einsum(
                "secf,edf->secd", inner_grad, up_block, preferred_element_type=jnp.float32
            ).astype(jnp.bfloat16),
            "mp",
            scatter_dimension=0,
            tiled=True,
        )
        up_grads[layer_now] = up_grad
        down_grads[layer_now] = down_grad
        grad_back = lax.all_to_all(
            rows_grad, "dp", split_axis=0, concat_axis=0, tiled=True
        ).reshape(slot_total, model_width)
        ffn_grad = jnp.sum(keep_pair[:, :, None] * grad_back[target].astype(jnp.float32), axis=1)
        ffn_grad = ffn_grad + jnp.einsum(
            "te,de->td", logit_grad, router[layer_now].astype(jnp.float32), precision=HIGHEST
        )
        router_grads[layer_now] = jnp.einsum(
            "td,te->de", ffn_b.astype(jnp.float32), logit_grad, precision=HIGHEST
        )
        middle_grad, ffn_gain_grads[layer_now] = jax.vjp(rms_scale, middle, ffn_gain[layer_now])[1](
            ffn_grad
        )
        middle_grad = middle_grad + flowing
        branch_grad = middle_grad.astype(jnp.bfloat16)
        attn_grads[layer_now] = jnp.einsum(
            "td,te->de", mixed_b, branch_grad, preferred_element_type=jnp.float32
        )
        mixed_grad = jnp.einsum(
            "te,de->td", branch_grad, w_attn[layer_now], preferred_element_type=jnp.float32
        )
        mixed_grad = mixed_grad.astype(jnp.bfloat16).reshape(
            groups, local_rows, head_count, head_size
        )
        key_every, value_every = kept_keys
        scores = score_block(query_b, key_every, full_bias, allowed, factor)
        probs = jnp.exp(scores - log_total)
        prob_grad = jnp.einsum(
            "grhd,gkhd->hgrk", mixed_grad, value_every, preferred_element_type=jnp.float32
        )
        score_grad = (
            probs * (prob_grad - jnp.sum(probs * prob_grad, axis=-1, keepdims=True))
        ).astype(jnp.bfloat16)
        query_grad = (
            jnp.einsum("hgrk,gkhd->grhd", score_grad, key_every, preferred_element_type=jnp.float32)
            * factor
        )
        key_part = (
            jnp.einsum("hgrk,grhd->gkhd", score_grad, query_b, preferred_element_type=jnp.float32)
            * factor
        )
        value_part = jnp.einsum(
            "hgrk,grhd->gkhd",
            probs.astype(jnp.bfloat16),
            mixed_grad,
            preferred_element_type=jnp.float32,
        )
        key_grad, value_grad = (
            lax.psum_scatter(
                key_part.reshape(groups, seq_len, model_width).astype(jnp.bfloat16),
                "mp",
                scatter_dimension=1,
                tiled=True,
            ).astype(jnp.float32),
            lax.psum_scatter(
                value_part.reshape(groups, seq_len, model_width).astype(jnp.bfloat16),
                "mp",
                scatter_dimension=1,
                tiled=True,
            ).astype(jnp.float32),
        )
        bias_grads[layer_now] = jnp.einsum(
            "hgrk,bgrk->hb", score_grad, one_hot, preferred_element_type=jnp.float32
        )
        qkv_grad = jnp.concatenate(
            [
                query_grad.reshape(tok_count, model_width),
                key_grad.reshape(tok_count, model_width),
                value_grad.reshape(tok_count, model_width),
            ],
            axis=1,
        ).astype(jnp.bfloat16)
        qkv_grads[layer_now] = jnp.einsum(
            "td,te->de", normed_b, qkv_grad, preferred_element_type=jnp.float32
        )
        normed_grad = jnp.einsum(
            "te,de->td", qkv_grad, w_qkv[layer_now], preferred_element_type=jnp.float32
        )
        stream_grad, attn_gain_grads[layer_now] = jax.vjp(
            rms_scale, stream_in, attn_gain[layer_now]
        )[1](normed_grad)
        flowing = middle_grad + stream_grad
    totals = lax.psum(
        (
            jnp.stack(qkv_grads),
            jnp.stack(attn_grads),
            jnp.stack(attn_gain_grads),
            jnp.stack(bias_grads),
            jnp.stack(ffn_gain_grads),
            jnp.stack(router_grads),
        ),
        ("dp", "mp"),
    )
    input_grad = flowing.reshape(groups, local_rows, model_width)
    return (
        output,
        input_grad,
        totals[0],
        totals[1],
        totals[2],
        totals[3],
        totals[4],
        totals[5],
        jnp.stack(up_grads),
        jnp.stack(down_grads),
    )


def solution(mesh):
    return jax.shard_map(
        body,
        mesh=mesh,
        in_specs=(
            P("dp", "mp", None),
            P("dp", "mp", None),
            P(),
            P(),
            P(),
            P(),
            P(),
            P(),
            P(None, "dp", None, "mp"),
            P(None, "dp", "mp", None),
            P("dp", None),
            P(None, "dp", "mp", None),
            P(None, "dp", "mp", None),
            P(None, "dp", "mp", None),
        ),
        out_specs=(
            P("dp", "mp", None),
            P("dp", "mp", None),
            P(),
            P(),
            P(),
            P(),
            P(),
            P(),
            P(None, "dp", None, "mp"),
            P(None, "dp", "mp", None),
        ),
        check_vma=False,
    )
```

profile of v0, /device:TPU:17, one launch (start us, length us, event | category | flops | bytes accessed | tf_op | source)
XLA Modules:
  0.0 2145.1 jit_solution(8736684111606637270)
XLA Ops:
  23.5 18.6 fusion.99
  45.2 140.5 %fusion.203 = (f32[12,384]{1,0:T(8,128)S(1)}, f32[12,384,1536]{2,1,0:T(8,128)}) fusion(f32[12]{0:T(128)} %get-tuple-element.114, pred[384,1536]{1,0:T(8,128)(4,1)} %get-tuple-element.219, f32[12]{0:T(128)} %get-tuple-element.115, pred[384,1536]{1,0:T(8,128)(4,1)} %get-tuple-element.218, f32[12]{0:T(128)} %get-tuple-element.116, ...), kind=kOutput, calls=%fused_computation.472 | convolution fusion | flops 1380183552 | bytes 50744832 | tf_op jit(solution)/shard_map/grhd,gkhd->hgrk/dot_general | solution.py:71
  230.2 35.9 %all_to_all.40 = bf16[8,2,54,768]{3,1,2,0:T(2,128)(2,1)S(1)} all-to-all(bf16[8,2,54,768]{3,1,2,0:T(2,128)(2,1)S(1)} %copy.211), channel_id=1, replica_groups=mesh['dp'=8,'mp'=4] {'dp'}, dimensions={0} | all-to-all | bytes 2654208 | tf_op jit(solution)/shard_map/all_to_all | solution.py:160
  267.5 42.7 %all-gather.13.cloned.1.call-done = bf16[32,2,54,768]{3,2,0,1:T(8,128)(2,1)} async-done(((bf16[8,2,54,768]{3,2,0,1:T(8,128)(2,1)}), bf16[32,2,54,768]{3,2,0,1:T(8,128)(2,1)}) %all-gather.13.cloned.1.call-update) | async-done | bytes 5308432 | tf_op jit(solution)/shard_map/all_gather | solution.py:167
  343.1 101.3 %all-reduce.12.cloned.1.call-done = bf16[32,2,54,768]{3,1,2,0:T(2,128)(2,1)} async-done(((bf16[32,2,54,768]{3,1,2,0:T(2,128)(2,1)}), bf16[32,2,54,768]{3,1,2,0:T(2,128)(2,1)}) %all-reduce.12.cloned.1.call-update) | async-done | bytes 5308432
  462.5 18.3 all-to-all-done.1
  505.5 22.9 %all-gather.27.cloned.1.call-done = bf16[1536,768]{1,0:T(8,128)(2,1)} async-done(((bf16[384,768]{1,0:T(8,128)(2,1)}), bf16[1536,768]{1,0:T(8,128)(2,1)}) %all-gather.27.cloned.1.call-update) | async-done | bytes 2359312 | tf_op jit(solution)/shard_map/all_gather | solution.py:128
  531.6 139.9 %fusion.204 = (f32[12,384]{1,0:T(8,128)S(1)}, f32[12,384,1536]{2,1,0:T(8,128)}) fusion(f32[12]{0:T(128)S(1)} %copy-done.126, pred[384,1536]{1,0:T(8,128)(4,1)} %get-tuple-element.219, f32[12]{0:T(128)S(1)} %copy-done.127, pred[384,1536]{1,0:T(8,128)(4,1)} %get-tuple-element.218, f32[12]{0:T(128)S(1)} %copy-done.128, ...), kind=kOutput, calls=%fused_computation.473 | convolution fusion | flops 1380183552 | bytes 50744832 | tf_op jit(solution)/shard_map/grhd,gkhd->hgrk/dot_general | solution.py:71
  715.5 35.8 %all_to_all.41 = bf16[8,2,54,768]{3,1,2,0:T(2,128)(2,1)S(1)} all-to-all(bf16[8,2,54,768]{3,1,2,0:T(2,128)(2,1)S(1)} %copy.225), channel_id=1, replica_groups=mesh['dp'=8,'mp'=4] {'dp'}, dimensions={0} | all-to-all | bytes 2654208 | tf_op jit(solution)/shard_map/all_to_all | solution.py:160
  785.2 35.2 %all_to_all.42 = bf16[8,2,54,768]{3,1,2,0:T(2,128)(2,1)S(1)} all-to-all(bf16[8,2,54,768]{3,1,2,0:T(2,128)(2,1)S(1)} %copy.234), channel_id=1, replica_groups=mesh['dp'=8,'mp'=4] {'dp'}, dimensions={0} | all-to-all | bytes 2654208 | tf_op jit(solution)/shard_map/all_to_all | solution.py:260
  902.4 188.8 %all-reduce.18.cloned.1.call-done = (bf16[32,2,54,768]{3,1,2,0:T(2,128)(2,1)}, bf16[32,2,54,768]{3,1,2,0:T(2,128)(2,1)}) async-done(((bf16[32,2,54,768]{3,1,2,0:T(2,128)(2,1)}, bf16[32,2,54,768]{3,1,2,0:T(2,128)(2,1)}), (bf16[32,2,54,768]{3,1,2,0:T(2,128)(2,1)}, bf16[32,2,54,768]{3,1,2,0:T(2,128)(2,1)})) %all-reduce.18.cloned.1.call-update) | async-done | bytes 10616848
  1103.3 24.4 %all-to-all-done.3 = bf16[8,2,54,768]{3,1,2,0:T(2,128)(2,1)S(1)} async-done(((bf16[8,2,54,768]{3,1,2,0:T(2,128)(2,1)}), bf16[8,2,54,768]{3,1,2,0:T(2,128)(2,1)S(1)}, u32[]{:S(2)}, u32[]{:S(2)}) %all-to-all-start.3) | async-done | bytes 1327136 | tf_op jit(solution)/shard_map/all_to_all | solution.py:183
  1197.5 21.8 %multiply_reduce_fusion.1 = (f32[12,384]{1,0:T(8,128)S(1)}, f32[12,384,1536]{2,1,0:T(8,128)}) fusion(f32[12,384,1536]{2,1,0:T(8,128)} %get-tuple-element.239, f32[12,384]{1,0:T(8,128)S(1)} %log_add_fusion.1, bf16[384,12,64]{0,2,1:T(8,128)(2,1)S(1)} %bitcast.445, bf16[1536,12,64]{0,2,1:T(8,128)(2,1)S(1)} %bitcast.427), kind=kOutput, calls=%fused_computation.19 | convolution fusion | flops 927198720 | bytes 59609088 | tf_op jit(solution)/shard_map/grhd,gkhd->hgrk/dot_general | solution.py:312
  1235.4 25.0 %multiply_convert_fusion.1 = bf16[12,384,1536]{2,1,0:T(8,128)(2,1)} fusion(f32[12,384,1536]{2,1,0:T(8,128)} %get-tuple-element.244, f32[12,384,1536]{2,1,0:T(8,128)} %get-tuple-element.239, f32[12,384]{1,0:T(8,128)S(1)} %get-tuple-element.243, f32[12,384]{1,0:T(8,128)S(1)} %log_add_fusion.1), kind=kLoop, calls=%fused_computation.18 | loop fusion | flops 28311552 | bytes 70815744 | tf_op jit(solution)/shard_map/convert_element_type | solution.py:317
  1294.1 22.0 %reduce-scatter.13.cloned.1.call-done = bf16[384,768]{1,0:T(8,128)(2,1)} async-done(((bf16[1536,768]{1,0:T(8,128)(2,1)}), bf16[384,768]{1,0:T(8,128)(2,1)}) %reduce-scatter.13.cloned.1.call-update) | async-done | bytes 589840
  1349.3 35.9 %all_to_all.43 = bf16[8,2,54,768]{3,1,2,0:T(2,128)(2,1)S(1)} all-to-all(bf16[8,2,54,768]{3,1,2,0:T(2,128)(2,1)S(1)} %copy.240), channel_id=1, replica_groups=mesh['dp'=8,'mp'=4] {'dp'}, dimensions={0} | all-to-all | bytes 2654208 | tf_op jit(solution)/shard_map/all_to_all | solution.py:260
  1386.5 41.7 %all-gather.19.cloned.1.call-done = bf16[32,2,54,768]{3,2,0,1:T(8,128)(2,1)} async-done(((bf16[8,2,54,768]{3,2,0,1:T(8,128)(2,1)}), bf16[32,2,54,768]{3,2,0,1:T(8,128)(2,1)}) %all-gather.19.cloned.1.call-update) | async-done | bytes 5308432 | tf_op jit(solution)/shard_map/all_gather | solution.py:261
  1476.8 93.5 %all-reduce.14.cloned.1.call-done = bf16[32,2,54,768]{3,1,2,0:T(2,128)(2,1)} async-done(((bf16[32,2,54,768]{3,1,2,0:T(2,128)(2,1)}), bf16[32,2,54,768]{3,1,2,0:T(2,128)(2,1)}) %all-reduce.14.cloned.1.call-update) | async-done | bytes 5308432
  1638.7 21.6 %multiply_reduce_fusion = (f32[12,384]{1,0:T(8,128)S(1)}, f32[12,384,1536]{2,1,0:T(8,128)}) fusion(f32[12,384,1536]{2,1,0:T(8,128)} %get-tuple-element.235, f32[12,384]{1,0:T(8,128)S(1)} %log_add_fusion, bf16[384,12,64]{0,2,1:T(8,128)(2,1)S(1)} %bitcast.447, bf16[1536,12,64]{0,2,1:T(8,128)(2,1)S(1)} %bitcast.425), kind=kOutput, calls=%fused_computation.16 | convolution fusion | flops 927198720 | bytes 59609088 | tf_op jit(solution)/shard_map/grhd,gkhd->hgrk/dot_general | solution.py:312
  1676.4 25.2 %multiply_convert_fusion = bf16[12,384,1536]{2,1,0:T(8,128)(2,1)} fusion(f32[12,384,1536]{2,1,0:T(8,128)} %get-tuple-element.248, f32[12,384,1536]{2,1,0:T(8,128)} %get-tuple-element.235, f32[12,384]{1,0:T(8,128)S(1)} %get-tuple-element.247, f32[12,384]{1,0:T(8,128)S(1)} %log_add_fusion), kind=kLoop, calls=%fused_computation.15 | loop fusion | flops 28311552 | bytes 70815744 | tf_op jit(solution)/shard_map/convert_element_type | solution.py:317
  1736.6 26.4 %copy.248 = bf16[12,384,1536]{1,0,2:T(8,128)(2,1)} copy(bf16[12,384,1536]{2,1,0:T(8,128)(2,1)} %multiply_convert_fusion.1) | data formatting | bytes 28311552 | tf_op jit(solution)/shard_map/convert_element_type | solution.py:317
  1862.6 26.2 %copy.247 = bf16[12,384,1536]{1,0,2:T(8,128)(2,1)} copy(bf16[12,384,1536]{2,1,0:T(8,128)(2,1)} %multiply_convert_fusion) | data formatting | bytes 28311552 | tf_op jit(solution)/shard_map/convert_element_type | solution.py:317
  1909.6 44.0 %all-reduce.4 = (f32[2,768]{1,0:T(2,128)}, f32[2,12,32]{2,1,0:T(8,128)S(1)}, f32[2,768]{1,0:T(2,128)}) all-reduce(f32[2,768]{1,0:T(2,128)S(1)} %pad_maximum_fusion.12, f32[2,12,32]{2,1,0:T(8,128)} %pad_maximum_fusion.11, f32[2,768]{1,0:T(2,128)S(1)} %pad_maximum_fusion.13), channel_id=1, replica_groups=mesh['dp'=8,'mp'=4] {'dp','mp'}, use_global_device_ids=true, to_apply=%region_49.51 | all-reduce | flops 3840 | bytes 30720 | tf_op jit(solution)/shard_map/psum | solution.py:367
  1957.5 164.1 %all-reduce.16.cloned.1.call-done = (f32[2,768,2304]{2,1,0:T(8,128)}, f32[2,768,768]{2,1,0:T(8,128)}, f32[2,768,16]{1,2,0:T(8,128)}) async-done(((f32[2,768,2304]{2,1,0:T(8,128)}, f32[2,768,768]{2,1,0:T(8,128)}, f32[2,768,16]{1,2,0:T(8,128)}), (f32[2,768,2304]{2,1,0:T(8,128)}, f32[2,768,768]{2,1,0:T(8,128)}, f32[2,768,16]{1,2,0:T(8,128)})) %all-reduce.16.cloned.1.call-update) | async-done | bytes 18972688 | tf_op jit(solution)/shard_map/psum | solution.py:367
  (585 shorter events, 776.0 us)
Async XLA Ops:
  7.2 34.9 %all-gather.23.cloned.1.call-start = ((), (), s32[]{:S(2)}) async-start(), calls=%async_computation.17 | async-start | bytes 2949120 | tf_op jit(solution)/shard_map/all_gather | solution.py:128
  14.9 182.7 %all-gather.21.cloned.1.call-start = ((), (), s32[]{:S(2)}) async-start(), calls=%async_computation.16 | async-start | bytes 2949120 | tf_op jit(solution)/shard_map/all_gather | solution.py:129
  15.7 294.5 %all-gather.13.cloned.1.call-start = ((), (), s32[]{:S(2)}) async-start(), calls=%async_computation.12 | async-start | bytes 6881280 | tf_op jit(solution)/shard_map/all_gather | solution.py:167
  42.1 143.6 %copy-start.51 = (pred[384,1536]{1,0:T(8,128)(4,1)}, pred[384,1536]{1,0:T(8,128)(4,1)S(1)}, u32[]{:S(2)}) copy-start(pred[384,1536]{1,0:T(8,128)(4,1)S(1)} %get-tuple-element.187) | copy-start | bytes 1769476
  214.0 281.3 %copy-start.12 = (f32[384,768]{1,0:T(8,128)}, f32[384,768]{1,0:T(8,128)S(1)}, u32[]{:S(2)}) copy-start(f32[384,768]{1,0:T(8,128)S(1)} %get-tuple-element.237) | copy-start | bytes 3538948
  214.2 239.5 %copy-start.20 = (bf16[384,768]{1,0:T(8,128)(2,1)}, bf16[384,768]{1,0:T(8,128)(2,1)S(1)}, u32[]{:S(2)}) copy-start(bf16[384,768]{1,0:T(8,128)(2,1)S(1)} %multiply_convert_fusion.8) | copy-start | bytes 1769476
  267.5 176.9 %all-reduce.12.cloned.1.call-start = ((), (), s32[]{:S(2)}) async-start(), calls=%async_computation.24 | async-start | bytes 10616832
  447.6 33.1 %all-to-all-start.1 = ((bf16[8,2,54,768]{3,1,2,0:T(2,128)(2,1)}), bf16[8,2,54,768]{3,1,2,0:T(2,128)(2,1)}, u32[]{:S(2)}, u32[]{:S(2)}) async-start(bf16[8,2,54,768]{3,1,2,0:T(2,128)(2,1)} %constant_dynamic-slice_fusion.3), calls=%async_computation.1 | async-start | bytes 2654208 | tf_op jit(solution)/shard_map/all_to_all | solution.py:183
  453.1 75.4 %all-gather.27.cloned.1.call-start = ((), (), s32[]{:S(2)}) async-start(), calls=%async_computation.19 | async-start | bytes 2949120 | tf_op jit(solution)/shard_map/all_gather | solution.py:128
  501.0 181.9 %all-gather.25.cloned.1.call-start = ((), (), s32[]{:S(2)}) async-start(), calls=%async_computation.18 | async-start | bytes 2949120 | tf_op jit(solution)/shard_map/all_gather | solution.py:129
  505.2 166.4 %copy-start.38 = (bf16[384,768]{0,1:T(8,128)(2,1)}, bf16[384,768]{0,1:T(8,128)(2,1)S(1)}, u32[]{:S(2)}) copy-start(bf16[384,768]{0,1:T(8,128)(2,1)S(1)} %copy.217) | copy-start | bytes 1769476
  505.5 316.7 %all-gather.15.cloned.1.call-start = ((), (), s32[]{:S(2)}) async-start(), calls=%async_computation.13 | async-start | bytes 6881280 | tf_op jit(solution)/shard_map/all_gather | solution.py:167
  752.5 110.9 %all-gather.17.cloned.1.call-start = ((), (), s32[]{:S(2)}) async-start(), calls=%async_computation.14 | async-start | bytes 6881280 | tf_op jit(solution)/shard_map/all_gather | solution.py:261
  821.7 269.6 %all-reduce.18.cloned.1.call-start = ((), (), s32[]{:S(2)}) async-start(), calls=%async_computation.27 | async-start | bytes 21233664
  1094.5 33.2 %all-to-all-start.3 = ((bf16[8,2,54,768]{3,1,2,0:T(2,128)(2,1)}), bf16[8,2,54,768]{3,1,2,0:T(2,128)(2,1)S(1)}, u32[]{:S(2)}, u32[]{:S(2)}) async-start(bf16[8,2,54,768]{3,1,2,0:T(2,128)(2,1)} %constant_dynamic-slice_fusion.2), calls=%async_computation.3 | async-start | bytes 2654208 | tf_op jit(solution)/shard_map/all_to_all | solution.py:183
  1127.7 35.4 %all-to-all-start.5 = ((bf16[8,2,54,768]{3,1,2,0:T(2,128)(2,1)}), bf16[8,2,54,768]{3,1,2,0:T(2,128)(2,1)}, u32[]{:S(2)}, u32[]{:S(2)}) async-start(bf16[8,2,54,768]{3,1,2,0:T(2,128)(2,1)} %constant_dynamic-slice_fusion.1), calls=%async_computation.5 | async-start | bytes 2654208 | tf_op jit(solution)/shard_map/all_to_all | solution.py:285
  1135.6 154.7 %reduce-scatter.15.cloned.1.call-start = ((), (), s32[]{:S(2)}) async-start(), calls=%async_computation.21 | async-start | bytes 2949120
  1235.3 80.8 %reduce-scatter.13.cloned.1.call-start = ((), (), s32[]{:S(2)}) async-start(), calls=%async_computation.20 | async-start | bytes 2949120
  1280.6 147.7 %all-gather.19.cloned.1.call-start = ((), (), s32[]{:S(2)}) async-start(), calls=%async_computation.15 | async-start | bytes 6881280 | tf_op jit(solution)/shard_map/all_gather | solution.py:261
  1386.4 183.9 %all-reduce.14.cloned.1.call-start = ((), (), s32[]{:S(2)}) async-start(), calls=%async_computation.25 | async-start | bytes 10616832
  1573.7 33.1 %all-to-all-start.7 = ((bf16[8,2,54,768]{3,1,2,0:T(2,128)(2,1)}), bf16[8,2,54,768]{3,1,2,0:T(2,128)(2,1)S(1)}, u32[]{:S(2)}, u32[]{:S(2)}) async-start(bf16[8,2,54,768]{3,1,2,0:T(2,128)(2,1)} %constant_dynamic-slice_fusion), calls=%async_computation.7 | async-start | bytes 2654208 | tf_op jit(solution)/shard_map/all_to_all | solution.py:285
  1579.1 204.7 %reduce-scatter.19.cloned.1.call-start = ((), (), s32[]{:S(2)}) async-start(), calls=%async_computation.23 | async-start | bytes 2949120
  1676.3 112.2 %reduce-scatter.17.cloned.1.call-start = ((), (), s32[]{:S(2)}) async-start(), calls=%async_computation.22 | async-start | bytes 2949120
  1721.6 399.9 %all-reduce.16.cloned.1.call-start = ((), (), s32[]{:S(2)}) async-start(), calls=%async_computation.26 | async-start | bytes 37945344 | tf_op jit(solution)/shard_map/psum | solution.py:367
  (150 other events, 2740.2 us)
Sparse Core Ops, SparseCore 0:
  15.1 25.5 all-gather.22
  42.8 24.0 all-gather.20
  267.6 42.5 all-gather.12
  341.3 102.9 all-reduce.11
  501.1 27.3 all-gather.26
  530.5 24.0 all-gather.24
  752.6 41.6 all-gather.14
  821.8 41.6 all-gather.16
  902.5 188.6 all-reduce.17
  1235.5 36.0 reduce-scatter.14
  1280.7 35.3 reduce-scatter.12
  1386.6 41.6 all-gather.18
  1467.3 102.9 all-reduce.13
  1676.5 35.8 reduce-scatter.18
  1721.7 35.2 reduce-scatter.16
  1811.0 310.5 all-reduce.15
where the time goes:
time: 2160 us; the launch traced here: 2150 us
  waiting for transfers between devices  756 us (35%)
  matrix products  610 us (28%)
  local copies, waits for them, and re-layouts  345 us (16%)
  other arithmetic  204 us (9%)
  blocking collectives  187 us (9%)
  starting transfers between devices  25.5 us (1%)
    unnamed x23, waiting for transfers between devices  407 us
    dot_general x2, matrix products, score_block(): jnp.einsum('grhd,gkhd->hgrk', query_b, key_every, preferred_element_type=...  280 us
    psum x1, waiting for transfers between devices, body(): lax.psum((jnp.stack(qkv_grads), jnp.stack(attn_grads), jnp.stack(attn_gai...  164 us
    unnamed x333, local copies, waits for them, and re-layouts  111 us
    all_to_all x2, blocking collectives, body(): lax.all_to_all(send_rows.reshape(dp_count, local_experts, capacity, model...  71.7 us
    all_to_all x2, blocking collectives, body(): lax.all_to_all(back_rows, 'dp', split_axis=0, concat_axis=0, tiled=True)  71 us
    convert_element_type x2, local copies, waits for them, and re-layouts, body(): score_grad = (probs * (prob_grad - jnp.sum(probs * prob_grad, axis=-1, ke...  52.6 us
    all_gather x2, waiting for transfers between devices, body(): grad_rows = lax.all_gather(grad_arrived, 'mp', axis=0, tiled=True)  52 us
  transfers between devices with their start and end apart: 20, of which 13 were waited for; matrix products, arithmetic and copies ran while one was open for 34% of the time, Pallas kernels for 0%

commit v1 on v0

--- a/solution.py
+++ b/solution.py
@@ -1,6 +1,10 @@
+import functools
+
 import jax
 import jax.numpy as jnp
 from jax import lax
+from jax.experimental import pallas as pl
+from jax.experimental.pallas import tpu as pltpu
 from jax.sharding import PartitionSpec as P
 
 PROMPT = 1024
@@ -390,9 +394,1138 @@
     )
 
 
+BF = jnp.bfloat16
+F32 = jnp.float32
+VMEM = pl.BlockSpec(memory_space=pltpu.VMEM)
+SMEM = pl.BlockSpec(memory_space=pltpu.SMEM)
+ANY = pl.BlockSpec(memory_space=pl.ANY)
+VMEM_BYTES = 60 << 20
+MESH = pl.DeviceIdType.MESH
+LANES = 128
+QB = 256
+
+
+def nn(a, b):
+    return lax.dot_general(a, b, (((1,), (0,)), ((), ())), preferred_element_type=F32)
+
+
+def nt(a, b):
+    return lax.dot_general(a, b, (((1,), (1,)), ((), ())), preferred_element_type=F32)
+
+
+def tn(a, b):
+    return lax.dot_general(a, b, (((0,), (0,)), ((), ())), preferred_element_type=F32)
+
+
+def segments(lens, shape, dim):
+    at = lax.broadcasted_iota(jnp.int32, shape, dim)
+    segment = jnp.full(shape, -1, jnp.int32)
+    begin = jnp.zeros(shape, jnp.int32)
+    start = jnp.int32(0)
+    for number in range(lens.shape[1]):
+        inside = at >= start
+        segment = segment + inside.astype(jnp.int32)
+        begin = jnp.where(inside, start, begin)
+        start = start + lens[0, number]
+    return segment, at - begin
+
+
+def bias_stage(vec, lens, table, cont_bias):
+    width = vec.shape[1]
+    rows = lax.broadcasted_iota(jnp.int32, (LANES, width), 0)
+    skewed = jnp.broadcast_to(vec, (LANES, width))
+    for bit in range(7):
+        skewed = jnp.where((rows >> bit) % 2 == 1, pltpu.roll(skewed, 1 << bit, 1), skewed)
+    table[...] = skewed[:, : width - LANES].T
+    cont = cont_bias.shape[1]
+    _, offset = segments(lens, (LANES, cont), 1)
+    place = (lax.broadcasted_iota(jnp.int32, (LANES, cont), 0) == offset).astype(BF)
+    full = table[0:PROMPT, :]
+    high = full.astype(BF)
+    low = (full - high.astype(F32)).astype(BF)
+    cont_bias[...] = nn(jnp.concatenate([high, low], 1), jnp.concatenate([place, place], 0))
+
+
+def blocks_of(seq):
+    out = []
+    for start in range(0, PROMPT, QB):
+        out.append((start, start + QB, None))
+    for start in range(0, seq - PROMPT, QB):
+        out.append((PROMPT + start, PROMPT, max(0, start - LANES)))
+    return out
+
+
+def scores_of(keys, query, table, cont_bias, seg_col, seg_row, block, h):
+    q0, prompt_keys, cont_from = block
+    if cont_from is None:
+        left = PROMPT - q0
+        bias = jnp.concatenate(
+            [table[left : left + prompt_keys, :], table[left - LANES : left - LANES + prompt_keys, :]], 1
+        )
+        return [(0, prompt_keys, nt(keys[h, 0:prompt_keys, :], query) + bias)]
+    at = q0 - PROMPT
+    first = nt(keys[h, 0:PROMPT, :], query) + cont_bias[:, at : at + QB]
+    k0, k1 = PROMPT + cont_from, q0 + QB
+    left = PROMPT + cont_from - at
+    bias = jnp.concatenate(
+        [table[left : left + k1 - k0, :], table[left - LANES : left - LANES + k1 - k0, :]], 1
+    )
+    same = seg_col[cont_from : at + QB, :][:, 0:1] == seg_row[:, at : at + QB]
+    second = jnp.where(same, nt(keys[h, k0:k1, :], query) + bias, -1e30)
+    return [(0, PROMPT, first), (k0, k1, second)]
+
+
+def attn_fwd_kernel(heads, size, lens, normed, weight, vecs, qkv_o, mixed_o, lse_o, q_s, k_s, vt_s, table, cont_bias, mixt, segc):
+    seq = normed.shape[0]
+    own = heads * size
+    for i in range(seq // QB):
+        rows = pl.ds(i * QB, QB)
+        part = nn(normed[rows, :], weight[...]).astype(BF)
+        qkv_o[rows, :] = part
+        for h in range(heads):
+            q_s[h, rows, :] = part[:, h * size : (h + 1) * size] * BF(0.125)
+            k_s[h, rows, :] = part[:, own + h * size : own + (h + 1) * size]
+            vt_s[h, :, rows] = part[:, 2 * own + h * size : 2 * own + (h + 1) * size].astype(F32).T.astype(BF)
+    seg_row, _ = segments(lens, (1, seq - PROMPT), 1)
+    segc[...] = segments(lens, (seq - PROMPT, LANES), 0)[0]
+
+    def head(h, carry):
+        bias_stage(vecs[pl.ds(h, 1), :], lens, table, cont_bias)
+        for block in blocks_of(seq):
+            q0 = block[0]
+            parts = scores_of(k_s, q_s[h, q0 : q0 + QB, :], table, cont_bias, segc, seg_row, block, h)
+            top = functools.reduce(jnp.maximum, [jnp.max(s, axis=0, keepdims=True) for _, _, s in parts])
+            total, mixed = 0.0, 0.0
+            for k0, k1, s in parts:
+                p = jnp.exp(s - top)
+                total = total + jnp.sum(p, axis=0, keepdims=True)
+                mixed = mixed + nn(vt_s[h, :, k0:k1], p.astype(BF))
+            mixt[pl.ds(pl.multiple_of(h * size, size), size), q0 : q0 + QB] = mixed / total
+            lse_o[pl.ds(h, 1), q0 : q0 + QB] = top + jnp.log(total)
+        return carry
+
+    lax.fori_loop(0, heads, head, 0)
+    for i in range(seq // QB):
+        mixed_o[i * QB : (i + 1) * QB, :] = mixt[:, i * QB : (i + 1) * QB].T.astype(BF)
+
+
+def attn_fwd(lens, normed, weight, vecs, heads, size):
+    seq = normed.shape[0]
+    own = heads * size
+    width = vecs.shape[1]
+    return pl.pallas_call(
+        functools.partial(attn_fwd_kernel, heads, size),
+        out_shape=(
+            jax.ShapeDtypeStruct((seq, 3 * own), BF),
+            jax.ShapeDtypeStruct((seq, own), BF),
+            jax.ShapeDtypeStruct((heads, seq), F32),
+        ),
+        in_specs=[SMEM, VMEM, VMEM, VMEM],
+        out_specs=(VMEM, VMEM, VMEM),
+        scratch_shapes=[
+            pltpu.VMEM((heads, seq, size), BF),
+            pltpu.VMEM((heads, seq, size), BF),
+            pltpu.VMEM((heads, size, seq), BF),
+            pltpu.VMEM((width - LANES, LANES), F32),
+            pltpu.VMEM((PROMPT, seq - PROMPT), F32),
+            pltpu.VMEM((own, seq), F32),
+            pltpu.VMEM((seq - PROMPT, LANES), jnp.int32),
+        ],
+        compiler_params=pltpu.CompilerParams(vmem_limit_bytes=VMEM_BYTES),
+    )(lens, normed, weight, vecs)
+
+
+def attn_bwd_kernel(
+    heads, size, lens, qkv, normed, branch, w_attn, mixed, lse, vecs,
+    dqkv_o, gw_o, dvec_o,
+    q_s, k_s, v_s, kt_s, do_s, table, cont_bias, fold, dtable, dk_s, dv_s, dqt, dk_all, dv_all, segc,
+):
+    seq = normed.shape[0]
+    own = heads * size
+    cont = seq - PROMPT
+    for i in range(seq // QB):
+        rows = pl.ds(i * QB, QB)
+        part = qkv[rows, :]
+        dmix = nt(branch[rows, :], w_attn[...]).astype(BF)
+        for h in range(heads):
+            q_s[h, rows, :] = part[:, h * size : (h + 1) * size] * BF(0.125)
+            key = part[:, own + h * size : own + (h + 1) * size]
+            k_s[h, rows, :] = key
+            kt_s[h, :, rows] = (key.astype(F32) * 0.125).T.astype(BF)
+            v_s[h, rows, :] = part[:, 2 * own + h * size : 2 * own + (h + 1) * size]
+            do_s[h, rows, :] = dmix[:, h * size : (h + 1) * size]
+    seg_row, _ = segments(lens, (1, cont), 1)
+    segc[...] = segments(lens, (cont, LANES), 0)[0]
+    _, offset = segments(lens, (cont, LANES), 0)
+    unplace = (lax.broadcasted_iota(jnp.int32, (cont, LANES), 1) == offset).astype(BF)
+    width = vecs.shape[1]
+
+    def head(h, carry):
+        bias_stage(vecs[pl.ds(h, 1), :], lens, table, cont_bias)
+        dtable[...] = jnp.zeros_like(dtable)
+        dk_s[...] = jnp.zeros_like(dk_s)
+        dv_s[...] = jnp.zeros_like(dv_s)
+        for block in blocks_of(seq):
+            q0, prompt_keys, cont_from = block
+            query = q_s[h, q0 : q0 + QB, :]
+            dout = do_s[h, q0 : q0 + QB, :]
+            parts = scores_of(k_s, query, table, cont_bias, segc, seg_row, block, h)
+            lse_row = lse[pl.ds(h, 1), q0 : q0 + QB]
+            kept, delta = [], 0.0
+            for k0, k1, s in parts:
+                p = jnp.exp(s - lse_row)
+                dp = nt(v_s[h, k0:k1, :], dout)
+                delta = delta + jnp.sum(p * dp, axis=0, keepdims=True)
+                dv_s[k0:k1, :] += nn(p.astype(BF), dout)
+                kept.append((k0, k1, p, dp))
+            dq = 0.0
+            for k0, k1, p, dp in kept:
+                ds = p * (dp - delta)
+                dsb = ds.astype(BF)
+                dk_s[k0:k1, :] += nn(dsb, query)
+                dq = dq + nn(kt_s[h, :, k0:k1], dsb)
+                if cont_from is not None and k0 == 0:
+                    fold[:, q0 - PROMPT : q0 - PROMPT + QB] = dsb
+                else:
+                    left = PROMPT - q0 if cont_from is None else PROMPT + cont_from - (q0 - PROMPT)
+                    dtable[left : left + k1 - k0, :] += ds[:, 0:LANES]
+                    dtable[left - LANES : left - LANES + k1 - k0, :] += ds[:, LANES:]
+            dqt[pl.ds(pl.multiple_of(h * size, size), size), q0 : q0 + QB] = dq
+        dk_all[h] = dk_s[...].astype(BF)
+        dv_all[h] = dv_s[...].astype(BF)
+        dtable[0:PROMPT, :] += nn(fold[...], unplace)
+        flat = dtable[...].T
+        flat = jnp.concatenate([flat, jnp.zeros((LANES, LANES), F32)], 1)
+        rows = lax.broadcasted_iota(jnp.int32, (LANES, width), 0)
+        for bit in range(7):
+            flat = jnp.where((rows >> bit) % 2 == 1, pltpu.roll(flat, width - (1 << bit), 1), flat)
+        dvec_o[pl.ds(h, 1), :] = jnp.sum(flat, axis=0, keepdims=True)
+        return carry
+
+    lax.fori_loop(0, heads, head, 0)
+    for i in range(seq // QB):
+        rows = pl.ds(i * QB, QB)
+        pieces = [dqt[:, i * QB : (i + 1) * QB].T.astype(BF)]
+        pieces += [dk_all[h, rows, :] for h in range(heads)] + [dv_all[h, rows, :] for h in range(heads)]
+        dqkv_o[rows, :] = jnp.concatenate(pieces, 1)
+    half = normed.shape[1] // 2
+    for i in range(2):
+        cols = slice(i * half, (i + 1) * half)
+        gw_o[cols, 0 : 3 * own] = tn(normed[:, cols], dqkv_o[...])
+        gw_o[cols, 3 * own :] = tn(branch[:, cols], mixed[...])
+
+
+def attn_bwd(lens, qkv, normed, branch, w_attn, mixed, lse, vecs, heads, size):
+    seq, model = normed.shape
+    own = heads * size
+    width = vecs.shape[1]
+    cont = seq - PROMPT
+    return pl.pallas_call(
+        functools.partial(attn_bwd_kernel, heads, size),
+        out_shape=(
+            jax.ShapeDtypeStruct((seq, 3 * own), BF),
+            jax.ShapeDtypeStruct((model, 4 * own), F32),
+            jax.ShapeDtypeStruct((heads, width), F32),
+        ),
+        in_specs=[SMEM] + [VMEM] * 7,
+        out_specs=(VMEM, VMEM, VMEM),
+        scratch_shapes=[
+            pltpu.VMEM((heads, seq, size), BF),
+            pltpu.VMEM((heads, seq, size), BF),
+            pltpu.VMEM((heads, seq, size), BF),
+            pltpu.VMEM((heads, size, seq), BF),
+            pltpu.VMEM((heads, seq, size), BF),
+            pltpu.VMEM((width - LANES, LANES), F32),
+            pltpu.VMEM((PROMPT, cont), F32),
+            pltpu.VMEM((PROMPT, cont), BF),
+            pltpu.VMEM((width - LANES, LANES), F32),
+            pltpu.VMEM((seq, size), F32),
+            pltpu.VMEM((seq, size), F32),
+            pltpu.VMEM((own, seq), F32),
+            pltpu.VMEM((heads, seq, size), BF),
+            pltpu.VMEM((heads, seq, size), BF),
+            pltpu.VMEM((cont, LANES), jnp.int32),
+        ],
+        compiler_params=pltpu.CompilerParams(vmem_limit_bytes=VMEM_BYTES),
+    )(lens, qkv, normed, branch, w_attn, mixed, lse, vecs)
+
+
+def diagonals():
+    width = PROMPT + 3 * LANES
+    at = jnp.arange(width, dtype=jnp.int32)
+    distance = jnp.where(at <= PROMPT, PROMPT - at, PROMPT + width - at)
+    valid = (at <= PROMPT) | (at > width - LANES)
+    return width, distance, valid
+
+
+def bias_vectors(bias):
+    _, distance, valid = diagonals()
+    hot = bucket_of(distance)[None, :] == jnp.arange(bias.shape[-1], dtype=jnp.int32)[:, None]
+    picked = jnp.sum(jnp.where(hot, bias[..., :, None], 0.0), axis=-2)
+    return jnp.where(valid, picked, -1e30)
+
+
+def bias_grads(dvecs, buckets):
+    _, distance, valid = diagonals()
+    hot = (bucket_of(distance)[None, :] == jnp.arange(buckets, dtype=jnp.int32)[:, None]) & valid[None, :]
+    return jnp.sum(jnp.where(hot, dvecs[..., None, :], 0.0), axis=-1)
+
+
+def scatter_rows(rows, values, send):
+    experts, tile, _ = send.shape
+    tokens, model = values[0].shape
+    half = model // 2
+    at = lax.broadcasted_iota(jnp.int32, (experts * tile, tokens), 0)
+    place, piece = [], []
+    for j in range(2):
+        slot = rows[2 + j : 3 + j, :]
+        piece.append(jnp.where(rows[4 + j : 5 + j, :] > 0, slot // tile, -1))
+        place.append(rows[j : j + 1, :] * tile + slot % tile)
+
+    def pick(number, shift, columns):
+        hots = [
+            (jnp.where(piece[j] == number, place[j] + shift, -1) == at) for j in range(2)
+        ]
+        if len(values) == 1:
+            return nn((hots[0] | hots[1]).astype(BF), values[0][:, columns])
+        return nn(hots[0].astype(BF), values[0][:, columns]) + nn(hots[1].astype(BF), values[1][:, columns])
+
+    for i in range(3):
+        send[:, :, i * model : (i + 1) * model] = pick(i, 0, slice(0, model)).astype(BF).reshape(experts, tile, model)
+    tail = pick(3, 0, slice(0, half)) + pick(3, 8, slice(half, model))
+    send[:, :, 3 * model :] = tail.astype(BF).reshape(experts, tile, half)
+
+
+def gather_rows(cols, j, back):
+    experts, tile, wide = back.shape
+    half = wide // 7
+    model = 2 * half
+    tokens = cols.shape[0]
+    at = lax.broadcasted_iota(jnp.int32, (tokens, experts * tile), 1)
+    slot = cols[:, 2 + j : 3 + j]
+    piece = jnp.where(cols[:, 4 + j : 5 + j] > 0, slot // tile, -1)
+    place = cols[:, j : j + 1] * tile + slot % tile
+    total = 0.0
+    for i in range(3):
+        hot = (jnp.where(piece == i, place, -1) == at).astype(BF)
+        total = total + nn(hot, back[:, :, i * model : (i + 1) * model].reshape(experts * tile, model))
+    tail = back[:, :, 3 * model :].reshape(experts * tile, half)
+    left = nn((jnp.where(piece == 3, place, -1) == at).astype(BF), tail)
+    right = nn((jnp.where(piece == 3, place + 8, -1) == at).astype(BF), tail)
+    return total + jnp.concatenate([left, right], 1)
+
+
+def unfold_tail(block, half):
+    wide = block.astype(F32)
+    return jnp.concatenate([wide[0:8, :], wide[8:16, :]], 1)
+
+
+def mp_places():
+    me = lax.axis_index("mp")
+    core, row = lax.rem(me, 2), me // 2
+    return me, core, row * 2 + 1 - core, (1 - row) * 2 + core, (1 - row) * 2 + 1 - core
+
+
+def signal_to(barrier, **place):
+    pl.semaphore_signal(barrier, inc=1, device_id=place, device_id_type=MESH)
+
+
+def remote(src, dst, send_sem, recv_sem, **place):
+    return pltpu.make_async_remote_copy(
+        src_ref=src, dst_ref=dst, send_sem=send_sem, recv_sem=recv_sem, device_id=place, device_id_type=MESH
+    )
+
+
+def gather_mp(held, ssem, rsem):
+    me, core, mate, across, diagonal = mp_places()
+    to_mate = remote(held.at[me], held.at[me], ssem.at[0], rsem.at[0], mp=mate)
+    over = remote(held.at[me], held.at[me], ssem.at[1], rsem.at[1], mp=across)
+    over.start()
+    to_mate.start()
+    over.wait_recv()
+    passed = remote(held.at[across], held.at[across], ssem.at[2], rsem.at[2], mp=mate)
+    passed.start()
+    to_mate.wait_recv()
+    passed.wait_recv()
+    for copy in (to_mate, over, passed):
+        copy.wait_send()
+
+
+def swap_mp(out, held, ssem, rsem, lsem):
+    me, core, mate, across, diagonal = mp_places()
+    copies = [
+        remote(out.at[to], held.at[me], ssem.at[n], rsem.at[n], mp=to) for n, to in enumerate((diagonal, across, mate))
+    ]
+    for copy in copies:
+        copy.start()
+    own = pltpu.make_async_copy(out.at[me], held.at[me], lsem)
+    own.start()
+    own.wait()
+    for copy in copies:
+        copy.wait()
+
+
+def greet_mp(count):
+    me, core, mate, across, diagonal = mp_places()
+    barrier = pltpu.get_barrier_semaphore()
+    for to in (mate, across, diagonal)[:count]:
+        signal_to(barrier, mp=to)
+    pl.semaphore_wait(barrier, count)
+
+
+def mean_square_scale(values):
+    return lax.rsqrt(jnp.mean(values * values, axis=-1, keepdims=True) + EPSILON)
+
+
+def norm_grads(values, gain, upstream):
+    scale = mean_square_scale(values)
+    scaled = upstream * gain
+    drift = jnp.mean(values * scaled, axis=-1, keepdims=True)
+    return scale * scaled - values * (scale * scale * scale * drift), jnp.sum(
+        upstream * values * scale, axis=0, keepdims=True
+    )
+
+
+def first_kernel(tokens, gain, all_o, held, ssem, rsem):
+    greet_mp(2)
+    me = lax.axis_index("mp")
+    stream = tokens[...].astype(F32)
+    held[me] = (stream * mean_square_scale(stream) * gain[...]).astype(BF)
+    gather_mp(held, ssem, rsem)
+    all_o[...] = held[...]
+
+
+def next_kernel(middle, back, cols, gates, gain, stream_o, all_o, held, ssem, rsem):
+    greet_mp(2)
+    me = lax.axis_index("mp")
+    stream = middle[...]
+    for j in range(2):
+        stream = stream + gates[:, j : j + 1] * gather_rows(cols, j, back)
+    stream_o[...] = stream
+    held[me] = (stream * mean_square_scale(stream) * gain[...]).astype(BF)
+    gather_mp(held, ssem, rsem)
+    all_o[...] = held[...]
+
+
+def middle_kernel(with_grad, *refs):
+    if with_grad:
+        (mixed, stream, w_attn, gain, router, rows, cols, cotangent, middle_o, ffn_o, gates_o, send_o, back_o, held, ssem, rsem, lsem) = refs
+    else:
+        (mixed, stream, w_attn, gain, router, rows, cols, middle_o, ffn_o, gates_o, send_o, held, ssem, rsem, lsem) = refs
+    greet_mp(3)
+    swap_mp(mixed, held, ssem, rsem, lsem)
+    part = held.shape[2]
+    middle = stream[...].astype(F32)
+    for m in range(held.shape[0]):
+        middle = middle + nn(held[m], w_attn[m * part : (m + 1) * part, :])
+    middle_o[...] = middle
+    ffn = (middle * mean_square_scale(middle) * gain[...]).astype(BF)
+    ffn_o[...] = ffn
+    logits = nn(ffn, router[...])
+    expert = lax.broadcasted_iota(jnp.int32, logits.shape, 1)
+    chosen = [
+        jnp.sum(jnp.where(expert == cols[:, j : j + 1], logits, 0.0), axis=1, keepdims=True) for j in range(2)
+    ]
+    top = jnp.maximum(chosen[0], chosen[1])
+    powers = [jnp.exp(c - top) for c in chosen]
+    gates = [p / (powers[0] + powers[1]) for p in powers]
+    gates_o[...] = jnp.concatenate(gates, 1)
+    scatter_rows(rows, [ffn], send_o)
+    if with_grad:
+        flow = cotangent[...].astype(F32)
+        scatter_rows(rows, [(gates[j] * cols[:, 4 + j : 5 + j].astype(F32) * flow).astype(BF) for j in range(2)], back_o)
+
+
+def post_kernel(with_output, *refs):
+    if with_output:
+        (back, returned, flow_in, middle, ffn, gates, cols, router, gain, grad_o, all_o, gain_o, router_o, out_o, held, ssem, rsem) = refs
+    else:
+        (back, returned, flow_in, middle, ffn, gates, cols, router, gain, grad_o, all_o, gain_o, router_o, held, ssem, rsem) = refs
+    greet_mp(2)
+    me = lax.axis_index("mp")
+    flow = flow_in[...].astype(F32)
+    outs = [gather_rows(cols, j, returned) for j in range(2)]
+    gate = [gates[:, j : j + 1] for j in range(2)]
+    keep = [cols[:, 4 + j : 5 + j].astype(F32) for j in range(2)]
+    if with_output:
+        out_o[...] = (middle[...] + gate[0] * keep[0] * outs[0] + gate[1] * keep[1] * outs[1]).astype(BF)
+    gate_grad = [keep[j] * jnp.sum(flow * outs[j], axis=1, keepdims=True) for j in range(2)]
+    shared = gate[0] * gate_grad[0] + gate[1] * gate_grad[1]
+    expert = lax.broadcasted_iota(jnp.int32, (flow.shape[0], router.shape[1]), 1)
+    logit_grad = 0.0
+    for j in range(2):
+        logit_grad = logit_grad + jnp.where(expert == cols[:, j : j + 1], gate[j] * (gate_grad[j] - shared), 0.0)
+    high = logit_grad.astype(BF)
+    low = (logit_grad - high.astype(F32)).astype(BF)
+    upstream = gather_rows(cols, 0, back) + gather_rows(cols, 1, back)
+    upstream = upstream + nt(high, router[...]) + nt(low, router[...])
+    router_o[...] = tn(high, ffn[...]) + tn(low, ffn[...])
+    grad, gain_o[...] = norm_grads(middle[...], gain[...], upstream)
+    grad = grad + flow
+    grad_o[...] = grad
+    held[me] = grad.astype(BF)
+    gather_mp(held, ssem, rsem)
+    all_o[...] = held[...]
+
+
+def close_kernel(with_send, *refs):
+    if with_send:
+        (dqkv, weight, stream, gain, grad, rows, cols, gates, flow_o, gain_o, send_o, held, ssem, rsem, lsem) = refs
+    else:
+        (dqkv, weight, stream, gain, grad, flow_o, gain_o, held, ssem, rsem, lsem) = refs
+    greet_mp(3)
+    swap_mp(dqkv, held, ssem, rsem, lsem)
+    upstream = 0.0
+    for m in range(held.shape[0]):
+        upstream = upstream + nt(held[m], weight[m])
+    inner, gain_o[...] = norm_grads(stream[...].astype(F32), gain[...], upstream)
+    flow = grad[...] + inner
+    flow_o[...] = flow
+    if with_send:
+        scatter_rows(
+            rows,
+            [(gates[:, j : j + 1] * cols[:, 4 + j : 5 + j].astype(F32) * flow).astype(BF) for j in range(2)],
+            send_o,
+        )
+
+
+def mp_call(kernel, number, outs, scratch, swap, *args):
+    sems = [pltpu.SemaphoreType.DMA((3,)), pltpu.SemaphoreType.DMA((3,))] + ([pltpu.SemaphoreType.DMA] if swap else [])
+    return pl.pallas_call(
+        kernel,
+        out_shape=tuple(jax.ShapeDtypeStruct(shape, kind) for shape, kind in outs),
+        in_specs=[VMEM] * len(args),
+        out_specs=tuple([VMEM] * len(outs)),
+        scratch_shapes=[pltpu.VMEM(scratch, BF)] + sems,
+        compiler_params=pltpu.CompilerParams(
+            collective_id=number, has_side_effects=True, vmem_limit_bytes=VMEM_BYTES
+        ),
+    )(*args)
+
+
+def gelu_grad(values):
+    inner = jnp.tanh(SQRT_TWO_PI * (values + 0.044715 * values * values * values))
+    slope = SQRT_TWO_PI * (1.0 + 3.0 * 0.044715 * values * values)
+    return 0.5 * values * (1.0 + inner), 0.5 * (1.0 + inner) + 0.5 * values * (1.0 - inner * inner) * slope
+
+
+def expert_kernel(mode, layer, dp_count, *refs):
+    forward, backward = mode in ("fwd", "both"), mode in ("both", "bwd")
+    refs = list(refs)
+
+    def take(count):
+        taken = refs[:count]
+        del refs[:count]
+        return taken
+
+    (send_x,) = take(1) if forward else (None,)
+    (send_g,) = take(1) if backward else (None,)
+    (x_in,) = take(1) if mode == "bwd" else (None,)
+    w_in, w_out = take(2)
+    (out_o,) = take(1) if forward else (None,)
+    (x_o,) = take(1) if mode == "fwd" else (None,)
+    grad_o, gw_in_o, gw_out_o = take(3) if backward else (None, None, None)
+    w1, w2, wsem, wssem, wrsem = take(5)
+    kept_part, x_all, xsem = take(3)
+    paths = []
+    for sending in ([send_x] if forward else []) + ([send_g] if backward else []):
+        paths.append((sending, take(14)))
+    if backward:
+        g_all, hid_all, ig_all, stage, gsem, grsem, glsem = take(7)
+
+    d = lax.axis_index("dp")
+    me, core, mate, across, diagonal = mp_places()
+    row = me // 2
+    index = d * 2 + core
+    experts = dp_count * 2
+    groups = dp_count // 2
+    model = w1.shape[1]
+    half = model // 2
+    rows_a = x_all.shape[1] // 2
+
+    barrier = pltpu.get_barrier_semaphore()
+
+    def greet(k, carry):
+        signal_to(barrier, dp=lax.rem(d + k // 2, dp_count), mp=row * 2 + lax.rem(core + k % 2, 2))
+        return carry
+
+    lax.fori_loop(1, experts, greet, 0)
+    signal_to(barrier, mp=across)
+    pl.semaphore_wait(barrier, experts)
+
+    def send_all(path):
+        sending, (recv_a, recv_b, ssem, asem, fsem, bsem, part, pssem, prsem, ret_s, ret, rssem, rrsem, psend) = path
+
+        def one(k, carry):
+            dd, cc = lax.rem(d + k // 2, dp_count), lax.rem(core + k % 2, 2)
+            to = dd * 2 + cc
+            remote(sending.at[to], recv_a.at[index], ssem.at[to], asem.at[index], dp=dd, mp=row * 2 + cc).start()
+            return carry
+
+        lax.fori_loop(1, experts, one, 0)
+        pltpu.make_async_copy(sending.at[index], recv_a.at[index], asem.at[index]).start()
+
+    send_all(paths[0])
+    copies = []
+    for n, (source, held) in enumerate(((w_in, w1), (w_out, w2))):
+        copies.append(remote(source.at[layer, 1 - core], held.at[core], wssem.at[n], wrsem.at[n], mp=mate))
+        copies.append(pltpu.make_async_copy(source.at[layer, core], held.at[core], wsem.at[n]))
+    for copy in copies:
+        copy.start()
+    if mode == "bwd":
+        saved = pltpu.make_async_copy(x_in, x_all, xsem)
+        saved.start()
+    for path in paths[1:]:
+        send_all(path)
+    for copy in copies:
+        copy.wait()
+    if mode == "bwd":
+        saved.wait()
+
+    def source_of(g, kk):
+        return lax.rem(d + dp_count - (g * 2 + kk), dp_count)
+
+    def unpack(held, g, side, into):
+        base = side * rows_a
+        for kk in range(2):
+            s0 = source_of(g, kk)
+            tails = []
+            for cc in range(2):
+                block = held[s0 * 2 + cc]
+                for i in range(3):
+                    into[g, base + i * 64 + kk * 32 + cc * 16 : base + i * 64 + kk * 32 + cc * 16 + 16, :] = block[
+                        :, i * model : (i + 1) * model
+                    ]
+                tails.append(unfold_tail(block[:, 3 * model :], half))
+            into[g, base + 192 + kk * 16 : base + 208 + kk * 16, :] = jnp.concatenate(tails, 0).astype(BF)
+
+    def run_path(path, into, compute):
+        sending, (recv_a, recv_b, ssem, asem, fsem, bsem, part, pssem, prsem, ret_s, ret, rssem, rrsem, psend) = path
+
+        def forward_copy(s0):
+            two = pl.ds(s0 * 2, 2)
+            return remote(recv_a.at[two], recv_b.at[two], fsem.at[s0], bsem.at[s0], mp=across)
+
+        def partial_copy(g):
+            return remote(psend.at[g], part.at[g], pssem.at[g], prsem.at[g], mp=across)
+
+        def step(i, carry):
+            @pl.when(i < groups)
+            def _():
+                for kk in range(2):
+                    s0 = source_of(i, kk)
+                    for cc in range(2):
+                        src = s0 * 2 + cc
+                        pltpu.make_async_copy(recv_a.at[src], recv_a.at[src], asem.at[src]).wait()
+                    forward_copy(s0).start()
+
+            @pl.when((i >= 1) & (i <= groups))
+            def _():
+                g = i - 1
+                for kk in range(2):
+                    forward_copy(source_of(g, kk)).wait_recv()
+                unpack(recv_a, g, 0, into)
+                unpack(recv_b, g, 1, into)
+                total = compute(g)
+                kept_part[lax.rem(g, 2)] = total[0:rows_a, :]
+                psend[g] = total[rows_a:, :].astype(BF)
+                partial_copy(g).start()
+
+            @pl.when(i >= 2)
+            def _():
+                g = i - 2
+                partial_copy(g).wait_recv()
+                total = kept_part[lax.rem(g, 2)] + part[g].astype(F32)
+                for kk in range(2):
+                    s0 = source_of(g, kk)
+                    for cc in range(2):
+                        src = s0 * 2 + cc
+                        for n in range(3):
+                            at = n * 64 + kk * 32 + cc * 16
+                            ret_s[src, :, n * model : (n + 1) * model] = total[at : at + 16, :].astype(BF)
+                        at = 192 + kk * 16 + cc * 8
+                        ret_s[src, :, 3 * model :] = jnp.concatenate(
+                            [total[at : at + 8, 0:half], total[at : at + 8, half:]], 0
+                        ).astype(BF)
+
+                        @pl.when(src == index)
+                        def _():
+                            pltpu.make_async_copy(ret_s.at[src], ret.at[index], rrsem.at[index]).start()
+
+                        @pl.when(src != index)
+                        def _():
+                            remote(
+                                ret_s.at[src], ret.at[index], rssem.at[src], rrsem.at[index], dp=s0, mp=row * 2 + cc
+                            ).start()
+
+            return carry
+
+        lax.fori_loop(0, groups + 2, step, 0)
+
+    def finish_path(path, result):
+        sending, (recv_a, recv_b, ssem, asem, fsem, bsem, part, pssem, prsem, ret_s, ret, rssem, rrsem, psend) = path
+
+        def end(e, carry):
+            pltpu.make_async_copy(ret.at[e], ret.at[e], rrsem.at[e]).wait()
+
+            @pl.when(e != index)
+            def _():
+                pltpu.make_async_copy(ret_s.at[e], ret_s.at[e], rssem.at[e]).wait()
+                pltpu.make_async_copy(sending.at[e], sending.at[e], ssem.at[e]).wait()
+
+            return carry
+
+        lax.fori_loop(0, experts, end, 0)
+
+        def end_pair(s0, carry):
+            two = pl.ds(s0 * 2, 2)
+            pltpu.make_async_copy(recv_a.at[two], recv_a.at[two], fsem.at[s0]).wait()
+            return carry
+
+        lax.fori_loop(0, dp_count, end_pair, 0)
+
+        def end_group(g, carry):
+            pltpu.make_async_copy(psend.at[g], psend.at[g], pssem.at[g]).wait()
+            return carry
+
+        lax.fori_loop(0, groups, end_group, 0)
+        result[...] = ret[...]
+
+    def compute_forward(g):
+        x = x_all[g]
+        total = 0.0
+        for q in range(2):
+            hidden = gelu_tanh(nn(x, w1[q])).astype(BF)
+            if backward:
+                hid_all[q, g] = hidden
+            total = total + nn(hidden, w2[q])
+        return total
+
+    def compute_backward(g):
+        x, gr = x_all[g], g_all[g]
+        total = 0.0
+        for q in range(2):
+            value, slope = gelu_grad(nn(x, w1[q]))
+            if not forward:
+                hid_all[q, g] = value.astype(BF)
+            inner = (nt(gr, w2[q]) * slope).astype(BF)
+            ig_all[q, g] = inner
+            total = total + nt(inner, w1[q])
+        return total
+
+    if forward:
+        run_path(paths[0], x_all, compute_forward)
+        if mode == "fwd":
+            saved = pltpu.make_async_copy(x_all, x_o, xsem)
+            saved.start()
+    if backward:
+        run_path(paths[-1], g_all, compute_backward)
+        count = groups * 2 * rows_a
+
+        def products(n, q):
+            if n == 0:
+                return tn(x_all[...].reshape(count, model), ig_all[q].reshape(count, model))
+            return tn(hid_all[q].reshape(count, model), g_all[...].reshape(count, model))
+
+        outs = (gw_in_o, gw_out_o)
+        copies = []
+        for n in range(2):
+            stage[n] = products(n, 1 - core)
+            copy = remote(stage.at[n], outs[n].at[core], gsem.at[n], grsem.at[n], mp=mate)
+            copy.start()
+            copies.append(copy)
+        for n in range(2):
+            copies[n].wait_send()
+            stage[n] = products(n, core)
+            copy = pltpu.make_async_copy(stage.at[n], outs[n].at[core], glsem.at[n])
+            copy.start()
+            copies.append(copy)
+        for n in range(2):
+            copies[n].wait_recv()
+            copies[2 + n].wait()
+    if forward:
+        finish_path(paths[0], out_o)
+        if mode == "fwd":
+            saved.wait()
+    if backward:
+        finish_path(paths[-1], grad_o)
+
+
+def expert_call(mode, layer, number, dp_count, sends, x_in, w_in, w_out):
+    forward, backward = mode in ("fwd", "both"), mode in ("both", "bwd")
+    shape = sends[0].shape
+    experts, tile, wide = shape
+    model = w_in.shape[2]
+    groups = dp_count // 2
+    rows = 2 * 4 * 56
+    dma = pltpu.SemaphoreType.DMA
+    args = list(sends)
+    specs = [VMEM] * len(sends)
+    if mode == "bwd":
+        args.append(x_in)
+        specs.append(ANY)
+    args += [w_in, w_out]
+    specs += [ANY, ANY]
+    outs, out_specs = [], []
+
+    def out(dims, kind, spec):
+        outs.append(jax.ShapeDtypeStruct(dims, kind))
+        out_specs.append(spec)
+
+    if forward:
+        out(shape, BF, VMEM)
+    if mode == "fwd":
+        out((groups, rows, model), BF, ANY)
+    if backward:
+        out(shape, BF, VMEM)
+        out((2, model, model), F32, ANY)
+        out((2, model, model), F32, ANY)
+    scratch = [
+        pltpu.VMEM((2, model, model), BF),
+        pltpu.VMEM((2, model, model), BF),
+        dma((2,)),
+        dma((2,)),
+        dma((2,)),
+        pltpu.VMEM((2, rows // 2, model), F32),
+        pltpu.VMEM((groups, rows, model), BF),
+        dma,
+    ]
+    for _ in sends:
+        scratch += [
+            pltpu.VMEM(shape, BF),
+            pltpu.VMEM(shape, BF),
+            dma((experts,)),
+            dma((experts,)),
+            dma((dp_count,)),
+            dma((dp_count,)),
+            pltpu.VMEM((groups, rows // 2, model), BF),
+            dma((groups,)),
+            dma((groups,)),
+            pltpu.VMEM(shape, BF),
+            pltpu.VMEM(shape, BF),
+            dma((experts,)),
+            dma((experts,)),
+            pltpu.VMEM((groups, rows // 2, model), BF),
+        ]
+    if backward:
+        scratch += [
+            pltpu.VMEM((groups, rows, model), BF),
+            pltpu.VMEM((2, groups, rows, model), BF),
+            pltpu.VMEM((2, groups, rows, model), BF),
+            pltpu.VMEM((2, model, model), F32),
+            dma((2,)),
+            dma((2,)),
+            dma((2,)),
+        ]
+    return pl.pallas_call(
+        functools.partial(expert_kernel, mode, layer, dp_count),
+        out_shape=tuple(outs),
+        in_specs=specs,
+        out_specs=tuple(out_specs),
+        scratch_shapes=scratch,
+        compiler_params=pltpu.CompilerParams(
+            collective_id=number, has_side_effects=True, vmem_limit_bytes=VMEM_BYTES
+        ),
+    )(*args)
+
+
+def reduce_kernel(layers, dp_count, *refs):
+    grads = refs[:layers]
+    small, all_o, small_o, part, come, small_come, small_mp, small_all, ssem, rsem, tsem, usem, vsem, zsem, csem, dsem, esem, fsem, hsem, isem = refs[layers:]
+    d = lax.axis_index("dp")
+    me, core, mate, across, diagonal = mp_places()
+    rows = come.shape[2]
+    barrier = pltpu.get_barrier_semaphore()
+
+    def peer(k):
+        return lax.rem(d + k, dp_count)
+
+    for k in range(1, dp_count):
+        signal_to(barrier, dp=peer(k), mp=me)
+    for to in (mate, across, diagonal):
+        signal_to(barrier, mp=to)
+    for j in range(dp_count):
+        for n in range(layers):
+            part[j, n] = grads[n][j * rows : (j + 1) * rows, :].astype(BF)
+    pl.semaphore_wait(barrier, dp_count + 2)
+
+    def small_copy(k):
+        to = peer(k)
+        return remote(small.at[to], small_come.at[d], tsem.at[k], usem.at[k], dp=to, mp=me)
+
+    def big_copy(k):
+        to = peer(k)
+        return remote(part.at[to], come.at[d], ssem.at[k], rsem.at[k], dp=to, mp=me)
+
+    for k in range(1, dp_count):
+        small_copy(k).start()
+    for k in range(1, dp_count):
+        big_copy(k).start()
+    total = small[d]
+    for k in range(1, dp_count):
+        small_copy(k).wait_recv()
+        total = total + small_come[lax.rem(d + dp_count - k, dp_count)]
+    small_mp[me] = total
+    swaps = [remote(small_mp.at[me], small_mp.at[me], csem.at[n], dsem.at[n], mp=to) for n, to in enumerate((mate, across, diagonal))]
+    for copy in swaps:
+        copy.start()
+    sums = [part[d, n].astype(F32) for n in range(layers)]
+    for copy in swaps:
+        copy.wait_recv()
+    small_all[d] = small_mp[0] + small_mp[1] + small_mp[2] + small_mp[3]
+
+    def small_share(k):
+        return remote(small_all.at[d], small_all.at[d], vsem.at[k], zsem.at[k], dp=peer(k), mp=me)
+
+    for k in range(1, dp_count):
+        small_share(k).start()
+    for k in range(1, dp_count):
+        big_copy(k).wait_recv()
+        src = lax.rem(d + dp_count - k, dp_count)
+        for n in range(layers):
+            sums[n] = sums[n] + come[src, n].astype(F32)
+    for n in range(layers):
+        all_o[me, d, n] = sums[n].astype(BF)
+
+    def share(k):
+        return remote(all_o.at[me, d], all_o.at[me, d], esem.at[k], fsem.at[k], dp=peer(k), mp=me)
+
+    def over(n, j):
+        whose = across if n == 2 else me
+        return remote(all_o.at[whose, j], all_o.at[whose, j], hsem.at[n, j], isem.at[n, j], mp=across if n == 1 else mate)
+
+    for k in range(1, dp_count):
+        share(k).start()
+    for k in range(dp_count):
+        j = lax.rem(d + dp_count - k, dp_count)
+        if k > 0:
+            share(k).wait_recv()
+        over(1, j).start()
+        over(0, j).start()
+        if k > 0:
+            last = lax.rem(d + dp_count - k + 1, dp_count)
+            over(1, last).wait_recv()
+            over(2, last).start()
+    last = lax.rem(d + 1, dp_count)
+    over(1, last).wait_recv()
+    over(2, last).start()
+    for k in range(1, dp_count):
+        small_share(k).wait_recv()
+    small_o[...] = small_all[...]
+    for j in range(dp_count):
+        over(0, j).wait_recv()
+        over(2, j).wait_recv()
+        for n in range(3):
+            over(n, j).wait_send()
+    for copy in swaps:
+        copy.wait_send()
+    for k in range(1, dp_count):
+        small_copy(k).wait_send()
+        big_copy(k).wait_send()
+        small_share(k).wait_send()
+        share(k).wait_send()
+
+
+def reduce_call(number, dp_count, grads, small):
+    model, width = grads[0].shape
+    layers = len(grads)
+    rows = model // dp_count
+    dma = pltpu.SemaphoreType.DMA
+    return pl.pallas_call(
+        functools.partial(reduce_kernel, layers, dp_count),
+        out_shape=(
+            jax.ShapeDtypeStruct((4, dp_count, layers, rows, width), BF),
+            jax.ShapeDtypeStruct(small.shape, F32),
+        ),
+        in_specs=[VMEM] * (layers + 1),
+        out_specs=(VMEM, VMEM),
+        scratch_shapes=[
+            pltpu.VMEM((dp_count, layers, rows, width), BF),
+            pltpu.VMEM((dp_count, layers, rows, width), BF),
+            pltpu.VMEM(small.shape, F32),
+            pltpu.VMEM((4,) + small.shape[1:], F32),
+            pltpu.VMEM(small.shape, F32),
+        ]
+        + [dma((dp_count,))] * 6
+        + [dma((3,))] * 2
+        + [dma((dp_count,))] * 2
+        + [dma((3, dp_count))] * 2,
+        compiler_params=pltpu.CompilerParams(
+            collective_id=number, has_side_effects=True, vmem_limit_bytes=VMEM_BYTES
+        ),
+    )(*grads, small)
+
+
+def spread_kernel(own, parts, qkv_o, attn_o):
+    for n in range(parts.shape[2]):
+        pieces = [parts[m, 0, n].astype(F32) for m in range(parts.shape[0])]
+        qkv_o[n] = jnp.concatenate([p[:, t * own : (t + 1) * own] for t in range(3) for p in pieces], 1)
+        attn_o[n, 0] = jnp.concatenate([p[:, 3 * own :] for p in pieces], 1)
+
+
+def spread_call(parts, own):
+    count, blocks, layers, rows, width = parts.shape
+    return pl.pallas_call(
+        functools.partial(spread_kernel, own),
+        grid=(blocks,),
+        out_shape=(
+            jax.ShapeDtypeStruct((layers, blocks * rows, 3 * count * own), F32),
+            jax.ShapeDtypeStruct((layers, blocks, rows, count * own), F32),
+        ),
+        in_specs=[pl.BlockSpec((count, 1, layers, rows, width), lambda i: (0, i, 0, 0, 0))],
+        out_specs=(
+            pl.BlockSpec((layers, rows, 3 * count * own), lambda i: (0, i, 0)),
+            pl.BlockSpec((layers, 1, rows, count * own), lambda i: (0, i, 0, 0)),
+        ),
+        compiler_params=pltpu.CompilerParams(vmem_limit_bytes=VMEM_BYTES),
+    )(parts)
+
+
+def fast_body(
+    tokens, cotangent, w_qkv, w_attn, attn_gain, rel_bias, ffn_gain, router, w_in, w_out, cont_lengths, routes, slots, drops
+):
+    _, local, model = tokens.shape
+    heads, buckets = rel_bias.shape[1:]
+    size = model // heads
+    layers = w_qkv.shape[0]
+    dp_count, mp_count = lax.axis_size("dp"), lax.axis_size("mp")
+    seq = local * mp_count
+    own_heads = heads // mp_count
+    own = own_heads * size
+    experts = dp_count * 2
+    me = lax.axis_index("mp")
+    half = model // 2
+    block = (experts, 16, 7 * half)
+    pairs = jnp.concatenate(
+        [routes.reshape(layers, local, 2), slots.reshape(layers, local, 2), 1 - drops.reshape(layers, local, 2)], 2
+    )
+    cols = jnp.pad(pairs, ((0, 0), (0, 0), (0, 2)))
+    rows = cols.transpose(0, 2, 1)
+    vecs = bias_vectors(lax.dynamic_slice_in_dim(rel_bias, me * own_heads, own_heads, 1))
+    weights = w_qkv.reshape(layers, model, 3, mp_count, own).transpose(0, 3, 1, 2, 4)
+    weights = weights.reshape(layers, mp_count, model, 3 * own)
+    mine = lax.dynamic_index_in_dim(weights, me, 1, keepdims=False)
+    mine_attn = lax.dynamic_slice_in_dim(w_attn, me * own, own, 1)
+    held = (mp_count, local, model)
+
+    kept = [None] * layers
+    stream = tokens[0]
+    sends, back, x_rows = None, None, None
+    for l in range(layers):
+        gain = attn_gain[l][None]
+        if l == 0:
+            (normed,) = mp_call(first_kernel, 0, [(held, BF)], held, False, stream, gain)
+        else:
+            before = kept[l - 1]
+            stream, normed = mp_call(
+                next_kernel, 1, [((local, model), F32), (held, BF)], held, False,
+                before["middle"], before["out"], cols[l - 1], before["gates"], gain,
+            )
+        normed = normed.reshape(seq, model)
+        qkv, mixed, lse = attn_fwd(cont_lengths, normed, mine[l], vecs[l], own_heads, size)
+        last = l == layers - 1
+        outs = [((local, model), F32), ((local, model), BF), ((local, 2), F32), (block, BF)] + ([(block, BF)] if last else [])
+        args = [mixed.reshape(mp_count, local, own), stream, w_attn[l], ffn_gain[l][None], router[l], rows[l], cols[l]]
+        got = mp_call(
+            functools.partial(middle_kernel, last), 2 + last, outs, (mp_count, local, own), True,
+            *args, *([cotangent[0]] if last else []),
+        )
+        middle, ffn, gates = got[:3]
+        kept[l] = dict(stream=stream, normed=normed, qkv=qkv, mixed=mixed, lse=lse, middle=middle, ffn=ffn, gates=gates)
+        if last:
+            out, back, gw_in, gw_out = expert_call("both", l, 5, dp_count, got[3:5], None, w_in, w_out)
+            kept[l].update(gw_in=gw_in, gw_out=gw_out)
+        else:
+            out, x_rows = expert_call("fwd", l, 4, dp_count, got[3:4], None, w_in, w_out)
+            kept[l].update(x_rows=x_rows)
+        kept[l].update(out=out)
+
+    flow = cotangent[0]
+    for l in reversed(range(layers)):
+        k = kept[l]
+        last = l == layers - 1
+        outs = [((local, model), F32), (held, BF), ((1, model), F32), ((experts, model), F32)]
+        got = mp_call(
+            functools.partial(post_kernel, last), 6 + last, outs + ([((local, model), BF)] if last else []), held, False,
+            back, k["out"], flow, k["middle"], k["ffn"], k["gates"], cols[l], router[l], ffn_gain[l][None],
+        )
+        grad, branch, k["ffn_gain"], k["router"] = got[:4]
+        if last:
+            output = got[4]
+        dqkv, k["heads"], dvecs = attn_bwd(
+            cont_lengths, k["qkv"], k["normed"], branch.reshape(seq, model), mine_attn[l], k["mixed"], k["lse"], vecs[l],
+            own_heads, size,
+        )
+        k["bias"] = bias_grads(dvecs, buckets)
+        outs = [((local, model), F32), ((1, model), F32)]
+        args = [dqkv.reshape(mp_count, local, 3 * own), weights[l], k["stream"], attn_gain[l][None], grad]
+        if l > 0:
+            outs.append((block, BF))
+            args += [rows[l - 1], cols[l - 1], kept[l - 1]["gates"]]
+        got = mp_call(functools.partial(close_kernel, l > 0), 8 + (l > 0), outs, (mp_count, local, 3 * own), True, *args)
+        flow, k["attn_gain"] = got[:2]
+        if l > 0:
+            b = kept[l - 1]
+            back, b["gw_in"], b["gw_out"] = expert_call("bwd", l - 1, 10, dp_count, [got[2]], b["x_rows"], w_in, w_out)
+
+    small = []
+    for l in range(layers):
+        k = kept[l]
+        bias = lax.dynamic_update_slice_in_dim(jnp.zeros((heads, buckets), F32), k["bias"], me * own_heads, 0)
+        small += [k["attn_gain"], k["ffn_gain"], jnp.pad(bias.reshape(1, -1), ((0, 5), (0, model - heads * buckets)))]
+        small += [k["router"]]
+    lines = 8 + experts
+    total_lines = -(-layers * lines // (8 * dp_count)) * 8
+    small = jnp.pad(jnp.concatenate(small, 0), ((0, total_lines * dp_count - layers * lines), (0, 0)))
+    parts, small = reduce_call(11, dp_count, [kept[l]["heads"] for l in range(layers)], small.reshape(dp_count, total_lines, model))
+    small = small.reshape(-1, model)[: layers * lines].reshape(layers, lines, model)
+    grad_qkv, grad_attn = spread_call(parts, own)
+    grad_attn = grad_attn.reshape(layers, model, model).transpose(0, 2, 1)
+    return (
+        output[None],
+        flow[None],
+        grad_qkv,
+        grad_attn,
+        small[:, 0],
+        small[:, 2, : heads * buckets].reshape(layers, heads, buckets),
+        small[:, 1],
+        small[:, 8:].transpose(0, 2, 1),
+        jnp.stack([k["gw_in"] for k in kept]),
+        jnp.stack([k["gw_out"] for k in kept]),
+    )
+
+
+def chosen_body(
+    tokens, cotangent, w_qkv, w_attn, attn_gain, rel_bias, ffn_gain, router, w_in, w_out, cont_lengths, routes, slots, drops
+):
+    groups, local, model = tokens.shape
+    heads = rel_bias.shape[1]
+    dp_count, mp_count = lax.axis_size("dp"), lax.axis_size("mp")
+    capacity = max(2, 9 * 2 * groups * local // (8 * w_in.shape[1] * dp_count))
+    seq = local * mp_count
+    fits = (
+        groups == 1
+        and mp_count == 4
+        and dp_count % 8 == 0
+        and heads % mp_count == 0
+        and model // heads == 64
+        and model % 256 == 0
+        and local % 128 == 0
+        and w_in.shape[1:] == (2, model, model)
+        and w_out.shape[1:] == (2, model, model)
+        and 48 < capacity <= 56
+        and seq > PROMPT
+        and (seq - PROMPT) % QB == 0
+    )
+    plan = fast_body if fits else body
+    return plan(
+        tokens, cotangent, w_qkv, w_attn, attn_gain, rel_bias, ffn_gain, router, w_in, w_out, cont_lengths, routes, slots, drops
+    )
+
+
 def solution(mesh):
     return jax.shard_map(
-        body,
+        chosen_body,
         mesh=mesh,
         in_specs=(
             P("dp", "mp", None),

time: 2160 us -> 926 us (0.43)
  Pallas kernels: 0 us -> 833 us
  waiting for transfers between devices: 756 us -> 0 us
  matrix products: 610 us -> 0 us
  local copies, waits for them, and re-layouts: 345 us -> 61.5 us
  blocking collectives: 187 us -> 0 us
  other arithmetic: 204 us -> 18.8 us
  starting transfers between devices: 25.5 us -> 0 us
    pallas_call x0 -> x17, Pallas kernels: none -> 833 us  [the longest x3 343 us: expert_call(): pl.pallas_call(functools.partial(expert_kernel, mode, layer, dp_count), o...]
    dot_general x44 -> x0, matrix products: 610 us -> none  [the longest x2 280 us: score_block(): jnp.einsum('grhd,gkhd->hgrk', query_b, key_every, preferred_element_type=...]
    unnamed x23 -> x0, waiting for transfers between devices: 407 us -> none
    psum x1 -> x0, waiting for transfers between devices: 164 us -> none  [body(): lax.psum((jnp.stack(qkv_grads), jnp.stack(attn_grads), jnp.stack(attn_gai...]
    all_to_all x4 -> x0, blocking collectives: 143 us -> none  [the longest x2 71.7 us: body(): lax.all_to_all(send_rows.reshape(dp_count, local_experts, capacity, model...]
    convert_element_type x12 -> x0, local copies, waits for them, and re-layouts: 125 us -> none  [the longest x2 52.6 us: body(): score_grad = (probs * (prob_grad - jnp.sum(probs * prob_grad, axis=-1, ke...]
    all_gather x8 -> x0, waiting for transfers between devices: 118 us -> none  [the longest x2 52 us: body(): grad_rows = lax.all_gather(grad_arrived, 'mp', axis=0, tiled=True)]
    unnamed x333 -> x41, local copies, waits for them, and re-layouts: 111 us -> 22.1 us
  transfers between devices with their start and end apart: 20 -> 0, of which waited for: 13 -> 0; matrix products, arithmetic and copies ran while one was open for 34% -> 0% of each run, Pallas kernels for 0% -> 0%
where the time goes in v1:
time: 926 us; the launch traced here: 915 us
  Pallas kernels  833 us (90%)
  local copies, waits for them, and re-layouts  61.5 us (7%)
  other arithmetic  18.8 us (2%)
    pallas_call x3, Pallas kernels, expert_call(): pl.pallas_call(functools.partial(expert_kernel, mode, layer, dp_count), o...  343 us
    pallas_call x8, Pallas kernels, mp_call(): pl.pallas_call(kernel, out_shape=tuple((jax.ShapeDtypeStruct(shape, kind)...  193 us
    pallas_call x1, Pallas kernels, reduce_call(): pl.pallas_call(functools.partial(reduce_kernel, layers, dp_count), out_sh...  169 us
    pallas_call x2, Pallas kernels, attn_bwd(): pl.pallas_call(functools.partial(attn_bwd_kernel, heads, size), out_shape...  72.7 us
    pallas_call x2, Pallas kernels, attn_fwd(): pl.pallas_call(functools.partial(attn_fwd_kernel, heads, size), out_shape...  43.9 us
    unnamed x41, local copies, waits for them, and re-layouts  22.1 us

profile of v1, /device:TPU:17, one launch (start us, length us, event | category | flops | bytes accessed | tf_op | source)
XLA Modules:
  0.0 915.1 jit_solution(920030089758620037)
XLA Ops:
  12.8 20.6 %shard_map.213 = bf16[4,384,768]{2,1,0:T(8,128)(2,1)} custom-call(bf16[384,768]{1,0:T(8,128)(2,1)} %bitcast.79, f32[1,768]{1,0:T(1,128)} %get-tuple-element.165.gain.refs_3_), custom_call_target="tpu_custom_call" | custom-call | tf_op jit(solution)/shard_map/pallas_call | solution.py:894
  34.9 10.3 %copy.72 = bf16[2,768,2304]{1,2,0:T(8,128)(2,1)} copy(bf16[2,768,2304]{2,1,0:T(8,128)(2,1)} %param.16) | data formatting | bytes 14155776 | tf_op args[2]
  45.2 3.6 copy.73
  55.9 5.9 copy.88.refs_1_
  64.0 21.8 %shard_map.214 = (bf16[1536,576]{1,0:T(8,128)(2,1)}, bf16[1536,192]{1,0:T(8,128)(2,1)}, f32[3,1536]{1,0:T(4,128)}) custom-call(s32[1,8]{1,0:T(1,128)} %lens.7, bf16[1536,768]{1,0:T(8,128)(2,1)} %bitcast.72, bf16[768,576]{1,0:T(8,128)(2,1)} %bitcast.89, f32[3,1408]{1,0:T(4,128)} %get-tuple-element.159.vecs), custom_call_target="tpu_custom_call" | custom-call | tf_op jit(solution)/shard_map/pallas_call | solution.py:516
  85.8 16.0 %shard_map.215 = (f32[384,768]{1,0:T(8,128)}, bf16[384,768]{1,0:T(8,128)(2,1)}, f32[384,2]{1,0:T(8,128)}, bf16[16,16,2688]{2,1,0:T(8,128)(2,1)}) custom-call(bf16[4,384,192]{2,1,0:T(8,128)(2,1)} %bitcast.91, bf16[384,768]{1,0:T(8,128)(2,1)} %bitcast.80, bf16[768,768]{1,0:T(8,128)(2,1)} %get-tuple-element.149.refs_2_, ...), custom_call_target="tpu_custom_call" | custom-call | tf_op jit(solution)/shard_map/pallas_call | solution.py:894
  101.9 89.2 %shard_map.216 = (bf16[16,16,2688]{2,1,0:T(8,128)(2,1)}, bf16[4,448,768]{2,1,0:T(8,128)(2,1)}) custom-call(bf16[16,16,2688]{2,1,0:T(8,128)(2,1)} %get-tuple-element.62.refs_0_, bf16[2,2,768,768]{3,2,1,0:T(8,128)(2,1)} %refs_2_.5, bf16[2,2,768,768]{3,2,1,0:T(8,128)(2,1)} %refs_3_.3), custom_call_target="tpu_custom_call" | custom-call | tf_op jit(solution)/shard_map/pallas_call | solution.py:1220
  193.1 5.9 copy.85.refs_1_
  198.9 22.8 %shard_map.217 = (f32[384,768]{1,0:T(8,128)}, bf16[4,384,768]{2,1,0:T(8,128)(2,1)}) custom-call(f32[384,768]{1,0:T(8,128)} %get-tuple-element.61.middle.refs_3_, bf16[16,16,2688]{2,1,0:T(8,128)(2,1)} %get-tuple-element.63.back.refs_1_, s32[384,8]{1,0:T(8,128)} %get-tuple-element.151.refs_6_.cols, f32[384,2]{1,0:T(8,128)} %get-tuple-element.64.gates.refs_7_.refs_5_, ...), custom_call_target="tpu_custom_call" | custom-call | tf_op jit(solution)/shard_map/pallas_call | solution.py:894
  221.7 22.0 %shard_map.218 = (bf16[1536,576]{1,0:T(8,128)(2,1)}, bf16[1536,192]{1,0:T(8,128)(2,1)}, f32[3,1536]{1,0:T(4,128)}) custom-call(s32[1,8]{1,0:T(1,128)} %lens.7, bf16[1536,768]{1,0:T(8,128)(2,1)} %bitcast.77, bf16[768,576]{1,0:T(8,128)(2,1)} %bitcast.88, f32[3,1408]{1,0:T(4,128)} %get-tuple-element.158.vecs), custom_call_target="tpu_custom_call" | custom-call | tf_op jit(solution)/shard_map/pallas_call | solution.py:516
  243.8 17.9 %shard_map.219 = (f32[384,768]{1,0:T(8,128)}, bf16[384,768]{1,0:T(8,128)(2,1)}, f32[384,2]{1,0:T(8,128)}, bf16[16,16,2688]{2,1,0:T(8,128)(2,1)}, bf16[16,16,2688]{2,1,0:T(8,128)(2,1)}) custom-call(bf16[4,384,192]{2,1,0:T(8,128)(2,1)} %bitcast.90, f32[384,768]{1,0:T(8,128)} %get-tuple-element.67.refs_1_.refs_2_, bf16[768,768]{1,0:T(8,128)(2,1)} %get-tuple-element.148.refs_2_, ...), custom_call_target="tpu_custom_call" | custom-call | tf_op jit(solution)/shard_map/pallas_call | solution.py:894
  261.7 155.1 %shard_map.220 = (bf16[16,16,2688]{2,1,0:T(8,128)(2,1)}, bf16[16,16,2688]{2,1,0:T(8,128)(2,1)}, f32[2,768,768]{2,1,0:T(8,128)}, f32[2,768,768]{2,1,0:T(8,128)}) custom-call(bf16[16,16,2688]{2,1,0:T(8,128)(2,1)} %get-tuple-element.68.refs_0_, bf16[16,16,2688]{2,1,0:T(8,128)(2,1)} %get-tuple-element.69.refs_1_, bf16[2,2,768,768]{3,2,1,0:T(8,128)(2,1)} %refs_2_.5, ...), custom_call_target="tpu_custom_call" | custom-call | tf_op jit(solution)/shard_map/pallas_call | solution.py:1220
  416.9 26.8 %shard_map.221 = (f32[384,768]{1,0:T(8,128)}, bf16[4,384,768]{2,1,0:T(8,128)(2,1)}, f32[1,768]{1,0:T(1,128)}, f32[16,768]{1,0:T(8,128)}, bf16[384,768]{1,0:T(8,128)(2,1)}) custom-call(bf16[16,16,2688]{2,1,0:T(8,128)(2,1)} %get-tuple-element.70.refs_0_, bf16[16,16,2688]{2,1,0:T(8,128)(2,1)} %get-tuple-element.71.refs_1_, bf16[384,768]{1,0:T(8,128)(2,1)} %bitcast.93, ...), custom_call_target="tpu_custom_call" | custom-call | tf_op jit(solution)/shard_map/pallas_call | solution.py:894
  443.7 36.3 %shard_map.222 = (bf16[1536,576]{1,0:T(8,128)(2,1)}, f32[768,768]{1,0:T(8,128)}, f32[3,1408]{1,0:T(4,128)}) custom-call(s32[1,8]{1,0:T(1,128)} %lens.7, bf16[1536,576]{1,0:T(8,128)(2,1)} %get-tuple-element.77.qkv, bf16[1536,768]{1,0:T(8,128)(2,1)} %bitcast.78, bf16[1536,768]{1,0:T(8,128)(2,1)} %bitcast.94, bf16[192,768]{1,0:T(8,128)(2,1)} %get-tuple-element.147.w_attn, ...), custom_call_target="tpu_custom_call" | custom-call | tf_op jit(solution)/shard_map/pallas_call | solution.py:623
  480.0 33.5 %shard_map.223 = (f32[384,768]{1,0:T(8,128)}, f32[1,768]{1,0:T(1,128)}, bf16[16,16,2688]{2,1,0:T(8,128)(2,1)}) custom-call(bf16[4,384,576]{2,1,0:T(8,128)(2,1)} %bitcast.97, bf16[4,768,576]{2,1,0:T(8,128)(2,1)} %copy.85.refs_1_, f32[384,768]{1,0:T(8,128)} %get-tuple-element.67.refs_1_.refs_2_, f32[1,768]{1,0:T(1,128)} %get-tuple-element.164.gain.refs_3_, ...), custom_call_target="tpu_custom_call" | custom-call | tf_op jit(solution)/shard_map/pallas_call | solution.py:894
  513.5 98.7 %shard_map.224 = (bf16[16,16,2688]{2,1,0:T(8,128)(2,1)}, f32[2,768,768]{2,1,0:T(8,128)}, f32[2,768,768]{2,1,0:T(8,128)}) custom-call(bf16[16,16,2688]{2,1,0:T(8,128)(2,1)} %get-tuple-element.82.refs_0_, bf16[4,448,768]{2,1,0:T(8,128)(2,1)} %get-tuple-element.83.refs_1_, bf16[2,2,768,768]{3,2,1,0:T(8,128)(2,1)} %refs_2_.5, bf16[2,2,768,768]{3,2,1,0:T(8,128)(2,1)} %refs_3_.3), custom_call_target="tpu_custom_call" | custom-call | tf_op jit(solution)/shard_map/pallas_call | solution.py:1220
  612.3 25.6 %shard_map.225 = (f32[384,768]{1,0:T(8,128)}, bf16[4,384,768]{2,1,0:T(8,128)(2,1)}, f32[1,768]{1,0:T(1,128)}, f32[16,768]{1,0:T(8,128)}) custom-call(bf16[16,16,2688]{2,1,0:T(8,128)(2,1)} %get-tuple-element.84.refs_0_, bf16[16,16,2688]{2,1,0:T(8,128)(2,1)} %get-tuple-element.63.back.refs_1_, f32[384,768]{1,0:T(8,128)} %get-tuple-element.85.refs_2_, ...), custom_call_target="tpu_custom_call" | custom-call | tf_op jit(solution)/shard_map/pallas_call | solution.py:894
  637.9 36.4 %shard_map.226 = (bf16[1536,576]{1,0:T(8,128)(2,1)}, f32[768,768]{1,0:T(8,128)}, f32[3,1408]{1,0:T(4,128)}) custom-call(s32[1,8]{1,0:T(1,128)} %lens.7, bf16[1536,576]{1,0:T(8,128)(2,1)} %get-tuple-element.76.qkv, bf16[1536,768]{1,0:T(8,128)(2,1)} %bitcast.73, bf16[1536,768]{1,0:T(8,128)(2,1)} %bitcast.95, bf16[192,768]{1,0:T(8,128)(2,1)} %get-tuple-element.146.w_attn, ...), custom_call_target="tpu_custom_call" | custom-call | tf_op jit(solution)/shard_map/pallas_call | solution.py:623
  675.6 30.0 %shard_map.227 = (f32[384,768]{1,0:T(8,128)}, f32[1,768]{1,0:T(1,128)}) custom-call(bf16[4,384,576]{2,1,0:T(8,128)(2,1)} %bitcast.96, bf16[4,768,576]{2,1,0:T(8,128)(2,1)} %copy.88.refs_1_, bf16[384,768]{1,0:T(8,128)(2,1)} %bitcast.81, f32[1,768]{1,0:T(1,128)} %get-tuple-element.165.gain.refs_3_, f32[384,768]{1,0:T(8,128)} %get-tuple-element.90.refs_4_), custom_call_target="tpu_custom_call" | custom-call | tf_op jit(solution)/shard_map/pallas_call | solution.py:894
  705.7 8.1 pad_maximum_fusion
  714.6 8.1 pad_maximum_fusion.1
  722.7 168.9 %shard_map.228 = (bf16[4,8,2,96,768]{4,3,2,1,0:T(8,128)(2,1)}, f32[8,8,768]{2,1,0:T(8,128)}) custom-call(f32[768,768]{1,0:T(8,128)} %get-tuple-element.92.refs_0_, f32[768,768]{1,0:T(8,128)} %get-tuple-element.93.refs_1_, f32[8,8,768]{2,1,0:T(8,128)} %pad_bitcast_fusion.1.refs_2_), custom_call_target="tpu_custom_call" | custom-call | tf_op jit(solution)/shard_map/pallas_call | solution.py:1334
  895.1 11.5 %shard_map.229 = (f32[2,768,2304]{2,1,0:T(8,128)}, f32[2,8,96,768]{3,2,1,0:T(8,128)}) custom-call(bf16[4,8,2,96,768]{4,3,2,1,0:T(8,128)(2,1)} %get-tuple-element.102.parts), custom_call_target="tpu_custom_call" | custom-call | tf_op jit(solution)/shard_map/pallas_call | solution.py:1368
  906.7 6.2 copy.89
  (82 shorter events, 32.3 us)
Async XLA Ops:
  0.6 0.7 copy-start
  0.7 11.3 %copy-start.2 = (bf16[2,768,768]{2,1,0:T(8,128)(2,1)S(1)}, bf16[2,768,768]{2,1,0:T(8,128)(2,1)}, u32[]{:S(2)}) copy-start(bf16[2,768,768]{2,1,0:T(8,128)(2,1)} %param.17) | copy-start | bytes 7077892
  45.2 5.0 slice-start
  45.2 5.7 slice-start.1
  637.9 36.4 %copy-start.5 = (pred[32,1408]{1,0:T(8,128)(4,1)S(1)}, pred[32,1408]{1,0:T(8,128)(4,1)}, u32[]{:S(2)}) copy-start(pred[32,1408]{1,0:T(8,128)(4,1)} %get-tuple-element.160) | copy-start | bytes 135172
  637.9 36.4 %copy-start.8 = (f32[3,1408]{1,0:T(4,128)S(1)}, f32[3,1408]{1,0:T(4,128)}, u32[]{:S(2)}) copy-start(f32[3,1408]{1,0:T(4,128)} %get-tuple-element.100) | copy-start | bytes 50692
  705.6 8.2 copy-start.6
  705.6 8.2 copy-start.7
  705.6 8.2 copy-start.9
  705.6 8.2 copy-start.10
  705.6 8.2 copy-start.11
  705.6 8.2 copy-start.12
  906.7 6.2 copy-start.4
  906.7 7.0 copy-start.3
  906.7 8.0 copy-start.1

commit v2 on v1

--- a/solution.py
+++ b/solution.py
@@ -417,6 +417,11 @@
     return lax.dot_general(a, b, (((0,), (0,)), ((), ())), preferred_element_type=F32)
 
 
+def layer_spec(array, layer):
+    zeros = (0,) * (array.ndim - 1)
+    return pl.BlockSpec((None,) + array.shape[1:], lambda i: (layer,) + zeros)
+
+
 def segments(lens, shape, dim):
     at = lax.broadcasted_iota(jnp.int32, shape, dim)
     segment = jnp.full(shape, -1, jnp.int32)
@@ -475,9 +480,17 @@
     return [(0, PROMPT, first), (k0, k1, second)]
 
 
-def attn_fwd_kernel(heads, size, lens, normed, weight, vecs, qkv_o, mixed_o, lse_o, q_s, k_s, vt_s, table, cont_bias, mixt, segc):
-    seq = normed.shape[0]
+def attn_fwd_kernel(heads, size, lens, normed, w_qkv, vecs, qkv_o, mixed_o, lse_o, weight, q_s, k_s, vt_s, table, cont_bias, mixt, segc):
+    seq, model = normed.shape
     own = heads * size
+    me = lax.axis_index("mp")
+    for m in range(model // own):
+
+        @pl.when(me == m)
+        def _():
+            for t in range(3):
+                weight[:, t * own : (t + 1) * own] = w_qkv[:, t * model + m * own : t * model + (m + 1) * own]
+
     for i in range(seq // QB):
         rows = pl.ds(i * QB, QB)
         part = nn(normed[rows, :], weight[...]).astype(BF)
@@ -509,20 +522,22 @@
         mixed_o[i * QB : (i + 1) * QB, :] = mixt[:, i * QB : (i + 1) * QB].T.astype(BF)
 
 
-def attn_fwd(lens, normed, weight, vecs, heads, size):
-    seq = normed.shape[0]
+def attn_fwd(lens, normed, w_qkv, layer, vecs, heads, size):
+    seq, model = normed.shape
     own = heads * size
     width = vecs.shape[1]
     return pl.pallas_call(
         functools.partial(attn_fwd_kernel, heads, size),
+        grid=(1,),
         out_shape=(
             jax.ShapeDtypeStruct((seq, 3 * own), BF),
             jax.ShapeDtypeStruct((seq, own), BF),
             jax.ShapeDtypeStruct((heads, seq), F32),
         ),
-        in_specs=[SMEM, VMEM, VMEM, VMEM],
+        in_specs=[SMEM, VMEM, layer_spec(w_qkv, layer), VMEM],
         out_specs=(VMEM, VMEM, VMEM),
         scratch_shapes=[
+            pltpu.VMEM((model, 3 * own), BF),
             pltpu.VMEM((heads, seq, size), BF),
             pltpu.VMEM((heads, seq, size), BF),
             pltpu.VMEM((heads, size, seq), BF),
@@ -532,21 +547,48 @@
             pltpu.VMEM((seq - PROMPT, LANES), jnp.int32),
         ],
         compiler_params=pltpu.CompilerParams(vmem_limit_bytes=VMEM_BYTES),
-    )(lens, normed, weight, vecs)
-
-
-def attn_bwd_kernel(
-    heads, size, lens, qkv, normed, branch, w_attn, mixed, lse, vecs,
-    dqkv_o, gw_o, dvec_o,
-    q_s, k_s, v_s, kt_s, do_s, table, cont_bias, fold, dtable, dk_s, dv_s, dqt, dk_all, dv_all, segc,
-):
-    seq = normed.shape[0]
+    )(lens, normed, w_qkv, vecs)
+
+
+def attn_bwd_kernel(heads, size, extra, lens, qkv, normed, branch, w_attn, mixed, lse, vecs, *refs):
+    refs = list(refs)
+    if extra == "copy":
+        sources, refs = refs[:2], refs[2:]
+    elif extra == "share":
+        shared, refs = refs[0], refs[1:]
+    dqkv_o, gw_o, dvec_o = refs[:3]
+    refs = refs[3:]
+    if extra == "copy":
+        targets, refs = refs[:2], refs[2:]
+    elif extra == "share":
+        all_o, refs = refs[0], refs[1:]
+    q_s, k_s, v_s, kt_s, do_s, table, cont_bias, fold, dtable, dk_s, dv_s, dqt, dk_all, dv_all, segc = refs[:15]
+    refs = refs[15:]
+    me, core, mate, across, diagonal = mp_places()
+    if extra == "copy":
+        spaces, sems = refs[:2], refs[2]
+        takes = [pltpu.make_async_copy(sources[n], spaces[n], sems.at[n]) for n in range(2)]
+        puts = [pltpu.make_async_copy(spaces[n], targets[n].at[targets[n].shape[0] - 1], sems.at[2 + n]) for n in range(2)]
+        for copy in takes:
+            copy.start()
+    elif extra == "share":
+        held, ssem, rsem = refs
+        greet_mp(2)
+        held[me] = shared[...]
+        to_mate = remote(held.at[me], held.at[me], ssem.at[0], rsem.at[0], mp=mate)
+        over = remote(held.at[me], held.at[me], ssem.at[1], rsem.at[1], mp=across)
+        passed = remote(held.at[across], held.at[across], ssem.at[2], rsem.at[2], mp=mate)
+        over.start()
+        to_mate.start()
+
+    seq, model = normed.shape
     own = heads * size
     cont = seq - PROMPT
+    own_rows = pl.ds(pl.multiple_of(me * own, size), own)
     for i in range(seq // QB):
         rows = pl.ds(i * QB, QB)
         part = qkv[rows, :]
-        dmix = nt(branch[rows, :], w_attn[...]).astype(BF)
+        dmix = nt(branch[rows, :], w_attn[own_rows, :]).astype(BF)
         for h in range(heads):
             q_s[h, rows, :] = part[:, h * size : (h + 1) * size] * BF(0.125)
             key = part[:, own + h * size : own + (h + 1) * size]
@@ -603,6 +645,13 @@
         return carry
 
     lax.fori_loop(0, heads, head, 0)
+    if extra == "copy":
+        for n in range(2):
+            takes[n].wait()
+            puts[n].start()
+    elif extra == "share":
+        over.wait_recv()
+        passed.start()
     for i in range(seq // QB):
         rows = pl.ds(i * QB, QB)
         pieces = [dqt[:, i * QB : (i + 1) * QB].T.astype(BF)]
@@ -613,22 +662,42 @@
         cols = slice(i * half, (i + 1) * half)
         gw_o[cols, 0 : 3 * own] = tn(normed[:, cols], dqkv_o[...])
         gw_o[cols, 3 * own :] = tn(branch[:, cols], mixed[...])
-
-
-def attn_bwd(lens, qkv, normed, branch, w_attn, mixed, lse, vecs, heads, size):
+    if extra == "copy":
+        for copy in puts:
+            copy.wait()
+    elif extra == "share":
+        to_mate.wait()
+        over.wait_send()
+        passed.wait()
+        all_o[...] = held[...]
+
+
+def attn_bwd(lens, qkv, normed, branch, w_attn, layer, mixed, lse, vecs, heads, size, extra=None, more=(), number=None):
     seq, model = normed.shape
     own = heads * size
     width = vecs.shape[1]
     cont = seq - PROMPT
+    params = pltpu.CompilerParams(vmem_limit_bytes=VMEM_BYTES)
+    outs, scratch, in_spec = (), [], VMEM
+    if extra == "copy":
+        outs = tuple(jax.ShapeDtypeStruct((w_attn.shape[0],) + g.shape, F32) for g in more)
+        scratch, in_spec = [pltpu.VMEM(g.shape, F32) for g in more] + [pltpu.SemaphoreType.DMA((4,))], ANY
+    elif extra == "share":
+        shape = (4,) + more[0].shape
+        outs = (jax.ShapeDtypeStruct(shape, BF),)
+        scratch = [pltpu.VMEM(shape, BF), pltpu.SemaphoreType.DMA((3,)), pltpu.SemaphoreType.DMA((3,))]
+        params = pltpu.CompilerParams(collective_id=number, has_side_effects=True, vmem_limit_bytes=VMEM_BYTES)
     return pl.pallas_call(
-        functools.partial(attn_bwd_kernel, heads, size),
+        functools.partial(attn_bwd_kernel, heads, size, extra),
+        grid=(1,),
         out_shape=(
             jax.ShapeDtypeStruct((seq, 3 * own), BF),
             jax.ShapeDtypeStruct((model, 4 * own), F32),
             jax.ShapeDtypeStruct((heads, width), F32),
-        ),
-        in_specs=[SMEM] + [VMEM] * 7,
-        out_specs=(VMEM, VMEM, VMEM),
+        )
+        + outs,
+        in_specs=[SMEM] + [VMEM] * 3 + [layer_spec(w_attn, layer)] + [VMEM] * 3 + [in_spec] * len(more),
+        out_specs=(VMEM, VMEM, VMEM) + (in_spec,) * len(outs),
         scratch_shapes=[
             pltpu.VMEM((heads, seq, size), BF),
             pltpu.VMEM((heads, seq, size), BF),
@@ -645,9 +714,10 @@
             pltpu.VMEM((heads, seq, size), BF),
             pltpu.VMEM((heads, seq, size), BF),
             pltpu.VMEM((cont, LANES), jnp.int32),
-        ],
-        compiler_params=pltpu.CompilerParams(vmem_limit_bytes=VMEM_BYTES),
-    )(lens, qkv, normed, branch, w_attn, mixed, lse, vecs)
+        ]
+        + scratch,
+        compiler_params=params,
+    )(lens, qkv, normed, branch, w_attn, mixed, lse, vecs, *more)
 
 
 def diagonals():
@@ -756,21 +826,46 @@
     copies = [
         remote(out.at[to], held.at[me], ssem.at[n], rsem.at[n], mp=to) for n, to in enumerate((diagonal, across, mate))
     ]
+    copies.append(pltpu.make_async_copy(out.at[me], held.at[me], lsem))
     for copy in copies:
         copy.start()
-    own = pltpu.make_async_copy(out.at[me], held.at[me], lsem)
-    own.start()
-    own.wait()
-    for copy in copies:
-        copy.wait()
-
-
-def greet_mp(count):
+    return copies
+
+
+def greet_mp(count, dp_count=1):
     me, core, mate, across, diagonal = mp_places()
+    d = lax.axis_index("dp")
     barrier = pltpu.get_barrier_semaphore()
     for to in (mate, across, diagonal)[:count]:
         signal_to(barrier, mp=to)
-    pl.semaphore_wait(barrier, count)
+    for k in range(1, dp_count):
+        signal_to(barrier, dp=lax.rem(d + k, dp_count), mp=me)
+    pl.semaphore_wait(barrier, count + dp_count - 1)
+
+
+def share_dp(held, ssem, rsem):
+    d, me, count = lax.axis_index("dp"), lax.axis_index("mp"), held.shape[0]
+    return [
+        remote(held.at[d], held.at[d], ssem.at[k], rsem.at[k], dp=lax.rem(d + k, count), mp=me) for k in range(1, count)
+    ]
+
+
+def scatter_dp(part, come, ssem, rsem):
+    d, me, count = lax.axis_index("dp"), lax.axis_index("mp"), part.shape[0]
+    copies = []
+    for k in range(1, count):
+        to = lax.rem(d + k, count)
+        copies.append(remote(part.at[to], come.at[d], ssem.at[k], rsem.at[k], dp=to, mp=me))
+    return copies
+
+
+def sum_dp(copies, part, come):
+    d, count = lax.axis_index("dp"), part.shape[0]
+    total = part[d].astype(F32)
+    for k in range(1, count):
+        copies[k - 1].wait_recv()
+        total = total + come[lax.rem(d + count - k, count)].astype(F32)
+    return total
 
 
 def mean_square_scale(values):
@@ -813,7 +908,8 @@
     else:
         (mixed, stream, w_attn, gain, router, rows, cols, middle_o, ffn_o, gates_o, send_o, held, ssem, rsem, lsem) = refs
     greet_mp(3)
-    swap_mp(mixed, held, ssem, rsem, lsem)
+    for copy in swap_mp(mixed, held, ssem, rsem, lsem):
+        copy.wait()
     part = held.shape[2]
     middle = stream[...].astype(F32)
     for m in range(held.shape[0]):
@@ -839,9 +935,15 @@
 def post_kernel(with_output, *refs):
     if with_output:
         (back, returned, flow_in, middle, ffn, gates, cols, router, gain, grad_o, all_o, gain_o, router_o, out_o, held, ssem, rsem) = refs
+        greet_mp(2)
     else:
-        (back, returned, flow_in, middle, ffn, gates, cols, router, gain, grad_o, all_o, gain_o, router_o, held, ssem, rsem) = refs
-    greet_mp(2)
+        (back, returned, flow_in, middle, ffn, gates, cols, router, gain, shared, grad_o, all_o, gain_o, router_o, share_o, held, ssem, rsem, round_s, dssem, drsem) = refs
+        greet_mp(2, dp_count=round_s.shape[0])
+        d = lax.axis_index("dp")
+        round_s[d] = shared[...]
+        shares = share_dp(round_s, dssem, drsem)
+        for copy in shares:
+            copy.start()
     me = lax.axis_index("mp")
     flow = flow_in[...].astype(F32)
     outs = [gather_rows(cols, j, returned) for j in range(2)]
@@ -866,41 +968,139 @@
     held[me] = grad.astype(BF)
     gather_mp(held, ssem, rsem)
     all_o[...] = held[...]
-
-
-def close_kernel(with_send, *refs):
-    if with_send:
-        (dqkv, weight, stream, gain, grad, rows, cols, gates, flow_o, gain_o, send_o, held, ssem, rsem, lsem) = refs
-    else:
-        (dqkv, weight, stream, gain, grad, flow_o, gain_o, held, ssem, rsem, lsem) = refs
-    greet_mp(3)
-    swap_mp(dqkv, held, ssem, rsem, lsem)
+    if not with_output:
+        for copy in shares:
+            copy.wait()
+        share_o[...] = round_s[...]
+
+
+def close_layer(held, w_qkv, stream, gain, grad):
+    model = w_qkv.shape[0]
+    own = held.shape[2] // 3
     upstream = 0.0
-    for m in range(held.shape[0]):
-        upstream = upstream + nt(held[m], weight[m])
-    inner, gain_o[...] = norm_grads(stream[...].astype(F32), gain[...], upstream)
-    flow = grad[...] + inner
+    for t in range(3):
+        piece = jnp.concatenate([held[m, :, t * own : (t + 1) * own] for m in range(held.shape[0])], 1)
+        upstream = upstream + nt(piece, w_qkv[:, t * model : (t + 1) * model])
+    inner, gain_grad = norm_grads(stream[...].astype(F32), gain[...], upstream)
+    return grad[...] + inner, gain_grad
+
+
+def fill_parts(part, heads):
+    rows = part.shape[1]
+    for j in range(part.shape[0]):
+        part[j] = heads[j * rows : (j + 1) * rows, :].astype(BF)
+
+
+def close_kernel(dqkv, w_qkv, stream, gain, grad, rows, cols, gates, heads, flow_o, gain_o, send_o, sum_o, held, part, come, ssem, rsem, lsem, dssem, drsem):
+    greet_mp(3, dp_count=part.shape[0])
+    swaps = swap_mp(dqkv, held, ssem, rsem, lsem)
+    fill_parts(part, heads)
+    scattered = scatter_dp(part, come, dssem, drsem)
+    for copy in scattered:
+        copy.start()
+    for copy in swaps:
+        copy.wait()
+    flow, gain_o[...] = close_layer(held, w_qkv, stream, gain, grad)
     flow_o[...] = flow
-    if with_send:
-        scatter_rows(
-            rows,
-            [(gates[:, j : j + 1] * cols[:, 4 + j : 5 + j].astype(F32) * flow).astype(BF) for j in range(2)],
-            send_o,
-        )
-
-
-def mp_call(kernel, number, outs, scratch, swap, *args):
-    sems = [pltpu.SemaphoreType.DMA((3,)), pltpu.SemaphoreType.DMA((3,))] + ([pltpu.SemaphoreType.DMA] if swap else [])
+    scatter_rows(
+        rows,
+        [(gates[:, j : j + 1] * cols[:, 4 + j : 5 + j].astype(F32) * flow).astype(BF) for j in range(2)],
+        send_o,
+    )
+    sum_o[...] = sum_dp(scattered, part, come).astype(BF)
+    for copy in scattered:
+        copy.wait_send()
+
+
+def last_kernel(
+    dqkv, w_qkv, stream, gain, grad, heads, small, flow_o, all_o, small_o,
+    held, part, come, small_s, small_come, small_mp, small_all,
+    ssem, rsem, lsem, dssem, drsem, tsem, usem, csem, dsem, vsem, zsem, esem, fsem, hsem, isem,
+):
+    dp_count = part.shape[0]
+    d = lax.axis_index("dp")
+    me, core, mate, across, diagonal = mp_places()
+    greet_mp(3, dp_count=dp_count)
+    swaps = swap_mp(dqkv, held, ssem, rsem, lsem)
+    fill_parts(part, heads)
+    scattered = scatter_dp(part, come, dssem, drsem)
+    for copy in scattered:
+        copy.start()
+    small_s[...] = small[...]
+    for copy in swaps:
+        copy.wait()
+    flow, gain_grad = close_layer(held, w_qkv, stream, gain, grad)
+    flow_o[...] = flow
+    small_s[0, 0:1, :] = gain_grad
+    small_scattered = scatter_dp(small_s, small_come, tsem, usem)
+    for copy in small_scattered:
+        copy.start()
+    all_o[me, d] = sum_dp(scattered, part, come).astype(BF)
+    shares = [
+        remote(all_o.at[me, d], all_o.at[me, d], esem.at[k], fsem.at[k], dp=lax.rem(d + k, dp_count), mp=me)
+        for k in range(1, dp_count)
+    ]
+    for copy in shares:
+        copy.start()
+
+    def over(n, j):
+        whose = across if n == 2 else me
+        return remote(all_o.at[whose, j], all_o.at[whose, j], hsem.at[n, j], isem.at[n, j], mp=across if n == 1 else mate)
+
+    over(1, d).start()
+    over(0, d).start()
+    small_mp[me] = sum_dp(small_scattered, small_s, small_come)
+    small_swaps = [
+        remote(small_mp.at[me], small_mp.at[me], csem.at[n], dsem.at[n], mp=to) for n, to in enumerate((mate, across, diagonal))
+    ]
+    for copy in small_swaps:
+        copy.start()
+    for copy in small_swaps:
+        copy.wait_recv()
+    small_all[d] = small_mp[0] + small_mp[1] + small_mp[2] + small_mp[3]
+    small_shares = share_dp(small_all, vsem, zsem)
+    for copy in small_shares:
+        copy.start()
+    for k in range(1, dp_count):
+        j = lax.rem(d + dp_count - k, dp_count)
+        shares[k - 1].wait_recv()
+        over(1, j).start()
+        over(0, j).start()
+        last = lax.rem(d + dp_count - k + 1, dp_count)
+        over(1, last).wait_recv()
+        over(2, last).start()
+    last = lax.rem(d + 1, dp_count)
+    over(1, last).wait_recv()
+    over(2, last).start()
+    for copy in small_shares:
+        copy.wait_recv()
+    small_o[...] = small_all[...]
+    for j in range(dp_count):
+        over(0, j).wait_recv()
+        over(2, j).wait_recv()
+        for n in range(3):
+            over(n, j).wait_send()
+    for copy in small_swaps + scattered + small_scattered + small_shares + shares:
+        copy.wait_send()
+
+
+def dma(*shape):
+    return pltpu.SemaphoreType.DMA(shape) if shape else pltpu.SemaphoreType.DMA
+
+
+def mp_call(kernel, number, outs, scratch, *args):
+    specs = [layer_spec(*a) if isinstance(a, tuple) else VMEM for a in args]
     return pl.pallas_call(
         kernel,
+        grid=(1,),
         out_shape=tuple(jax.ShapeDtypeStruct(shape, kind) for shape, kind in outs),
-        in_specs=[VMEM] * len(args),
+        in_specs=specs,
         out_specs=tuple([VMEM] * len(outs)),
-        scratch_shapes=[pltpu.VMEM(scratch, BF)] + sems,
+        scratch_shapes=scratch,
         compiler_params=pltpu.CompilerParams(
             collective_id=number, has_side_effects=True, vmem_limit_bytes=VMEM_BYTES
         ),
-    )(*args)
+    )(*[a[0] if isinstance(a, tuple) else a for a in args])
 
 
 def gelu_grad(values):
@@ -1158,7 +1358,6 @@
     model = w_in.shape[2]
     groups = dp_count // 2
     rows = 2 * 4 * 56
-    dma = pltpu.SemaphoreType.DMA
     args = list(sends)
     specs = [VMEM] * len(sends)
     if mode == "bwd":
@@ -1183,28 +1382,28 @@
     scratch = [
         pltpu.VMEM((2, model, model), BF),
         pltpu.VMEM((2, model, model), BF),
-        dma((2,)),
-        dma((2,)),
-        dma((2,)),
+        dma(2),
+        dma(2),
+        dma(2),
         pltpu.VMEM((2, rows // 2, model), F32),
         pltpu.VMEM((groups, rows, model), BF),
-        dma,
+        dma(),
     ]
     for _ in sends:
         scratch += [
             pltpu.VMEM(shape, BF),
             pltpu.VMEM(shape, BF),
-            dma((experts,)),
-            dma((experts,)),
-            dma((dp_count,)),
-            dma((dp_count,)),
+            dma(experts),
+            dma(experts),
+            dma(dp_count),
+            dma(dp_count),
             pltpu.VMEM((groups, rows // 2, model), BF),
-            dma((groups,)),
-            dma((groups,)),
+            dma(groups),
+            dma(groups),
             pltpu.VMEM(shape, BF),
             pltpu.VMEM(shape, BF),
-            dma((experts,)),
-            dma((experts,)),
+            dma(experts),
+            dma(experts),
             pltpu.VMEM((groups, rows // 2, model), BF),
         ]
     if backward:
@@ -1213,9 +1412,9 @@
             pltpu.VMEM((2, groups, rows, model), BF),
             pltpu.VMEM((2, groups, rows, model), BF),
             pltpu.VMEM((2, model, model), F32),
-            dma((2,)),
-            dma((2,)),
-            dma((2,)),
+            dma(2),
+            dma(2),
+            dma(2),
         ]
     return pl.pallas_call(
         functools.partial(expert_kernel, mode, layer, dp_count),
@@ -1229,156 +1428,52 @@
     )(*args)
 
 
-def reduce_kernel(layers, dp_count, *refs):
-    grads = refs[:layers]
-    small, all_o, small_o, part, come, small_come, small_mp, small_all, ssem, rsem, tsem, usem, vsem, zsem, csem, dsem, esem, fsem, hsem, isem = refs[layers:]
-    d = lax.axis_index("dp")
-    me, core, mate, across, diagonal = mp_places()
-    rows = come.shape[2]
-    barrier = pltpu.get_barrier_semaphore()
-
-    def peer(k):
-        return lax.rem(d + k, dp_count)
-
-    for k in range(1, dp_count):
-        signal_to(barrier, dp=peer(k), mp=me)
-    for to in (mate, across, diagonal):
-        signal_to(barrier, mp=to)
-    for j in range(dp_count):
-        for n in range(layers):
-            part[j, n] = grads[n][j * rows : (j + 1) * rows, :].astype(BF)
-    pl.semaphore_wait(barrier, dp_count + 2)
-
-    def small_copy(k):
-        to = peer(k)
-        return remote(small.at[to], small_come.at[d], tsem.at[k], usem.at[k], dp=to, mp=me)
-
-    def big_copy(k):
-        to = peer(k)
-        return remote(part.at[to], come.at[d], ssem.at[k], rsem.at[k], dp=to, mp=me)
-
-    for k in range(1, dp_count):
-        small_copy(k).start()
-    for k in range(1, dp_count):
-        big_copy(k).start()
-    total = small[d]
-    for k in range(1, dp_count):
-        small_copy(k).wait_recv()
-        total = total + small_come[lax.rem(d + dp_count - k, dp_count)]
-    small_mp[me] = total
-    swaps = [remote(small_mp.at[me], small_mp.at[me], csem.at[n], dsem.at[n], mp=to) for n, to in enumerate((mate, across, diagonal))]
-    for copy in swaps:
+def spread_kernel(own, count, *refs):
+    parts, (gw_in, gw_out, _, _) = refs[:count], refs[count : count + 4]
+    qkv_o, attn_o, in_o, out_o, sem = refs[count + 4 :]
+    step = pl.program_id(0)
+    copies = [
+        pltpu.make_async_copy(gw_in.at[0], in_o.at[0, step], sem.at[0]),
+        pltpu.make_async_copy(gw_out.at[0], out_o.at[0, step], sem.at[1]),
+    ]
+    for copy in copies:
         copy.start()
-    sums = [part[d, n].astype(F32) for n in range(layers)]
-    for copy in swaps:
-        copy.wait_recv()
-    small_all[d] = small_mp[0] + small_mp[1] + small_mp[2] + small_mp[3]
-
-    def small_share(k):
-        return remote(small_all.at[d], small_all.at[d], vsem.at[k], zsem.at[k], dp=peer(k), mp=me)
-
-    for k in range(1, dp_count):
-        small_share(k).start()
-    for k in range(1, dp_count):
-        big_copy(k).wait_recv()
-        src = lax.rem(d + dp_count - k, dp_count)
-        for n in range(layers):
-            sums[n] = sums[n] + come[src, n].astype(F32)
-    for n in range(layers):
-        all_o[me, d, n] = sums[n].astype(BF)
-
-    def share(k):
-        return remote(all_o.at[me, d], all_o.at[me, d], esem.at[k], fsem.at[k], dp=peer(k), mp=me)
-
-    def over(n, j):
-        whose = across if n == 2 else me
-        return remote(all_o.at[whose, j], all_o.at[whose, j], hsem.at[n, j], isem.at[n, j], mp=across if n == 1 else mate)
-
-    for k in range(1, dp_count):
-        share(k).start()
-    for k in range(dp_count):
-        j = lax.rem(d + dp_count - k, dp_count)
-        if k > 0:
-            share(k).wait_recv()
-        over(1, j).start()
-        over(0, j).start()
-        if k > 0:
-            last = lax.rem(d + dp_count - k + 1, dp_count)
-            over(1, last).wait_recv()
-            over(2, last).start()
-    last = lax.rem(d + 1, dp_count)
-    over(1, last).wait_recv()
-    over(2, last).start()
-    for k in range(1, dp_count):
-        small_share(k).wait_recv()
-    small_o[...] = small_all[...]
-    for j in range(dp_count):
-        over(0, j).wait_recv()
-        over(2, j).wait_recv()
-        for n in range(3):
-            over(n, j).wait_send()
-    for copy in swaps:
-        copy.wait_send()
-    for k in range(1, dp_count):
-        small_copy(k).wait_send()
-        big_copy(k).wait_send()
-        small_share(k).wait_send()
-        share(k).wait_send()
-
-
-def reduce_call(number, dp_count, grads, small):
-    model, width = grads[0].shape
-    layers = len(grads)
-    rows = model // dp_count
-    dma = pltpu.SemaphoreType.DMA
+
+    for n in range(count):
+        mp_count, blocks, rows, width = parts[n].shape
+        pieces = [parts[n][m].reshape(blocks * rows, width).astype(F32) for m in range(mp_count)]
+        qkv_o[n] = jnp.concatenate([p[:, t * own : (t + 1) * own] for t in range(3) for p in pieces], 1)
+        for m in range(mp_count):
+            attn_o[n, m * own : (m + 1) * own, :] = pieces[m][:, 3 * own :].T
+    for copy in copies:
+        copy.wait()
+
+
+def spread_call(parts, own, grads, places):
+    mp_count, blocks, rows, width = parts[0].shape
+    layers, model = len(parts), blocks * rows
+    steps = grads[0].shape[0]
     return pl.pallas_call(
-        functools.partial(reduce_kernel, layers, dp_count),
+        functools.partial(spread_kernel, own, layers),
+        grid=(steps,),
         out_shape=(
-            jax.ShapeDtypeStruct((4, dp_count, layers, rows, width), BF),
-            jax.ShapeDtypeStruct(small.shape, F32),
+            jax.ShapeDtypeStruct((layers, model, 3 * mp_count * own), F32),
+            jax.ShapeDtypeStruct((layers, mp_count * own, model), F32),
+        )
+        + tuple(jax.ShapeDtypeStruct(p.shape, F32) for p in places),
+        in_specs=[pl.BlockSpec((mp_count, blocks // steps, rows, width), lambda i: (0, i, 0, 0))] * layers
+        + [pl.BlockSpec((1,) + g.shape[1:], lambda i: (i, 0, 0)) for g in grads]
+        + [ANY] * 2,
+        out_specs=(
+            pl.BlockSpec((layers, model // steps, 3 * mp_count * own), lambda i: (0, i, 0)),
+            pl.BlockSpec((layers, mp_count * own, model // steps), lambda i: (0, 0, i)),
+            ANY,
+            ANY,
         ),
-        in_specs=[VMEM] * (layers + 1),
-        out_specs=(VMEM, VMEM),
-        scratch_shapes=[
-            pltpu.VMEM((dp_count, layers, rows, width), BF),
-            pltpu.VMEM((dp_count, layers, rows, width), BF),
-            pltpu.VMEM(small.shape, F32),
-            pltpu.VMEM((4,) + small.shape[1:], F32),
-            pltpu.VMEM(small.shape, F32),
-        ]
-        + [dma((dp_count,))] * 6
-        + [dma((3,))] * 2
-        + [dma((dp_count,))] * 2
-        + [dma((3, dp_count))] * 2,
-        compiler_params=pltpu.CompilerParams(
-            collective_id=number, has_side_effects=True, vmem_limit_bytes=VMEM_BYTES
-        ),
-    )(*grads, small)
-
-
-def spread_kernel(own, parts, qkv_o, attn_o):
-    for n in range(parts.shape[2]):
-        pieces = [parts[m, 0, n].astype(F32) for m in range(parts.shape[0])]
-        qkv_o[n] = jnp.concatenate([p[:, t * own : (t + 1) * own] for t in range(3) for p in pieces], 1)
-        attn_o[n, 0] = jnp.concatenate([p[:, 3 * own :] for p in pieces], 1)
-
-
-def spread_call(parts, own):
-    count, blocks, layers, rows, width = parts.shape
-    return pl.pallas_call(
-        functools.partial(spread_kernel, own),
-        grid=(blocks,),
-        out_shape=(
-            jax.ShapeDtypeStruct((layers, blocks * rows, 3 * count * own), F32),
-            jax.ShapeDtypeStruct((layers, blocks, rows, count * own), F32),
-        ),
-        in_specs=[pl.BlockSpec((count, 1, layers, rows, width), lambda i: (0, i, 0, 0, 0))],
-        out_specs=(
-            pl.BlockSpec((layers, rows, 3 * count * own), lambda i: (0, i, 0)),
-            pl.BlockSpec((layers, 1, rows, count * own), lambda i: (0, i, 0, 0)),
-        ),
+        scratch_shapes=[dma(2)],
+        input_output_aliases={layers + 2: 2, layers + 3: 3},
         compiler_params=pltpu.CompilerParams(vmem_limit_bytes=VMEM_BYTES),
-    )(parts)
+    )(*parts, *grads, *places)
 
 
 def fast_body(
@@ -1394,40 +1489,41 @@
     own = own_heads * size
     experts = dp_count * 2
     me = lax.axis_index("mp")
-    half = model // 2
-    block = (experts, 16, 7 * half)
+    block = (experts, 16, 7 * model // 2)
     pairs = jnp.concatenate(
         [routes.reshape(layers, local, 2), slots.reshape(layers, local, 2), 1 - drops.reshape(layers, local, 2)], 2
     )
     cols = jnp.pad(pairs, ((0, 0), (0, 0), (0, 2)))
     rows = cols.transpose(0, 2, 1)
     vecs = bias_vectors(lax.dynamic_slice_in_dim(rel_bias, me * own_heads, own_heads, 1))
-    weights = w_qkv.reshape(layers, model, 3, mp_count, own).transpose(0, 3, 1, 2, 4)
-    weights = weights.reshape(layers, mp_count, model, 3 * own)
-    mine = lax.dynamic_index_in_dim(weights, me, 1, keepdims=False)
-    mine_attn = lax.dynamic_slice_in_dim(w_attn, me * own, own, 1)
+    gain_a, gain_f = attn_gain[:, None], ffn_gain[:, None]
     held = (mp_count, local, model)
+    chunk = (dp_count, model // dp_count, model)
+    gather = [pltpu.VMEM(held, BF), dma(3), dma(3)]
+
+    def swap(width):
+        return [pltpu.VMEM((mp_count, local, width), BF)], [dma(3), dma(3), dma()]
 
     kept = [None] * layers
     stream = tokens[0]
     sends, back, x_rows = None, None, None
     for l in range(layers):
-        gain = attn_gain[l][None]
         if l == 0:
-            (normed,) = mp_call(first_kernel, 0, [(held, BF)], held, False, stream, gain)
+            (normed,) = mp_call(first_kernel, 0, [(held, BF)], gather, stream, (gain_a, l))
         else:
             before = kept[l - 1]
             stream, normed = mp_call(
-                next_kernel, 1, [((local, model), F32), (held, BF)], held, False,
-                before["middle"], before["out"], cols[l - 1], before["gates"], gain,
+                next_kernel, 1, [((local, model), F32), (held, BF)], gather,
+                before["middle"], before["out"], (cols, l - 1), before["gates"], (gain_a, l),
             )
         normed = normed.reshape(seq, model)
-        qkv, mixed, lse = attn_fwd(cont_lengths, normed, mine[l], vecs[l], own_heads, size)
+        qkv, mixed, lse = attn_fwd(cont_lengths, normed, w_qkv, l, vecs[l], own_heads, size)
         last = l == layers - 1
         outs = [((local, model), F32), ((local, model), BF), ((local, 2), F32), (block, BF)] + ([(block, BF)] if last else [])
-        args = [mixed.reshape(mp_count, local, own), stream, w_attn[l], ffn_gain[l][None], router[l], rows[l], cols[l]]
+        args = [mixed.reshape(mp_count, local, own), stream, (w_attn, l), (gain_f, l), (router, l), (rows, l), (cols, l)]
+        space, sems = swap(own)
         got = mp_call(
-            functools.partial(middle_kernel, last), 2 + last, outs, (mp_count, local, own), True,
+            functools.partial(middle_kernel, last), 2 + last, outs, space + sems,
             *args, *([cotangent[0]] if last else []),
         )
         middle, ffn, gates = got[:3]
@@ -1445,42 +1541,67 @@
         k = kept[l]
         last = l == layers - 1
         outs = [((local, model), F32), (held, BF), ((1, model), F32), ((experts, model), F32)]
-        got = mp_call(
-            functools.partial(post_kernel, last), 6 + last, outs + ([((local, model), BF)] if last else []), held, False,
-            back, k["out"], flow, k["middle"], k["ffn"], k["gates"], cols[l], router[l], ffn_gain[l][None],
-        )
+        args = [back, k["out"], flow, k["middle"], k["ffn"], k["gates"], (cols, l), (router, l), (gain_f, l)]
+        if last:
+            outs.append(((local, model), BF))
+            scratch = gather
+        else:
+            outs.append((chunk, BF))
+            args.append(heads_sum)
+            scratch = gather + [pltpu.VMEM(chunk, BF), dma(dp_count), dma(dp_count)]
+        got = mp_call(functools.partial(post_kernel, last), 6 + last, outs, scratch, *args)
         grad, branch, k["ffn_gain"], k["router"] = got[:4]
         if last:
             output = got[4]
-        dqkv, k["heads"], dvecs = attn_bwd(
-            cont_lengths, k["qkv"], k["normed"], branch.reshape(seq, model), mine_attn[l], k["mixed"], k["lse"], vecs[l],
-            own_heads, size,
-        )
+            extra, more = "copy", (k["gw_in"], k["gw_out"])
+        else:
+            extra, more = "share", (got[4],)
+        got = attn_bwd(
+            cont_lengths, k["qkv"], k["normed"], branch.reshape(seq, model), w_attn, l, k["mixed"], k["lse"], vecs[l],
+            own_heads, size, extra, more, 8,
+        )
+        dqkv, heads_grad, dvecs = got[:3]
         k["bias"] = bias_grads(dvecs, buckets)
-        outs = [((local, model), F32), ((1, model), F32)]
-        args = [dqkv.reshape(mp_count, local, 3 * own), weights[l], k["stream"], attn_gain[l][None], grad]
-        if l > 0:
-            outs.append((block, BF))
-            args += [rows[l - 1], cols[l - 1], kept[l - 1]["gates"]]
-        got = mp_call(functools.partial(close_kernel, l > 0), 8 + (l > 0), outs, (mp_count, local, 3 * own), True, *args)
-        flow, k["attn_gain"] = got[:2]
-        if l > 0:
+        args = [dqkv.reshape(mp_count, local, 3 * own), (w_qkv, l), k["stream"], (gain_a, l), grad]
+        space, sems = swap(3 * own)
+        if last:
+            places = got[3:]
             b = kept[l - 1]
-            back, b["gw_in"], b["gw_out"] = expert_call("bwd", l - 1, 10, dp_count, [got[2]], b["x_rows"], w_in, w_out)
+            flow, k["attn_gain"], send, heads_sum = mp_call(
+                close_kernel, 9, [((local, model), F32), ((1, model), F32), (block, BF), (chunk[1:], BF)],
+                space + [pltpu.VMEM(chunk, BF)] * 2 + sems + [dma(dp_count)] * 2,
+                *args, (rows, l - 1), (cols, l - 1), b["gates"], heads_grad,
+            )
+            back, b["gw_in"], b["gw_out"] = expert_call("bwd", l - 1, 10, dp_count, [send], b["x_rows"], w_in, w_out)
+        else:
+            (parts,) = got[3:]
 
     small = []
     for l in range(layers):
         k = kept[l]
         bias = lax.dynamic_update_slice_in_dim(jnp.zeros((heads, buckets), F32), k["bias"], me * own_heads, 0)
-        small += [k["attn_gain"], k["ffn_gain"], jnp.pad(bias.reshape(1, -1), ((0, 5), (0, model - heads * buckets)))]
-        small += [k["router"]]
+        small += [k["attn_gain"] if l > 0 else jnp.zeros((1, model), F32), k["ffn_gain"]]
+        small += [jnp.pad(bias.reshape(1, -1), ((0, 5), (0, model - heads * buckets))), k["router"]]
     lines = 8 + experts
-    total_lines = -(-layers * lines // (8 * dp_count)) * 8
-    small = jnp.pad(jnp.concatenate(small, 0), ((0, total_lines * dp_count - layers * lines), (0, 0)))
-    parts, small = reduce_call(11, dp_count, [kept[l]["heads"] for l in range(layers)], small.reshape(dp_count, total_lines, model))
+    share = -(-layers * lines // (8 * dp_count)) * 8
+    small = jnp.pad(jnp.concatenate(small, 0), ((0, share * dp_count - layers * lines), (0, 0)))
+    small = small.reshape(dp_count, share, model)
+    small_vmem = pltpu.VMEM(small.shape, F32)
+    flow, first_parts, small = mp_call(
+        last_kernel, 11, [((local, model), F32), ((mp_count,) + chunk, BF), (small.shape, F32)],
+        space
+        + [pltpu.VMEM(chunk, BF)] * 2
+        + [small_vmem, small_vmem, pltpu.VMEM((mp_count, share, model), F32), small_vmem]
+        + sems
+        + [dma(dp_count)] * 4
+        + [dma(3)] * 2
+        + [dma(dp_count)] * 4
+        + [dma(3, dp_count)] * 2,
+        *args, heads_grad, small,
+    )
     small = small.reshape(-1, model)[: layers * lines].reshape(layers, lines, model)
-    grad_qkv, grad_attn = spread_call(parts, own)
-    grad_attn = grad_attn.reshape(layers, model, model).transpose(0, 2, 1)
+    b = kept[0]
+    grad_qkv, grad_attn, grad_in, grad_out = spread_call([first_parts, parts], own, (b["gw_in"], b["gw_out"]), places)
     return (
         output[None],
         flow[None],
@@ -1490,8 +1611,8 @@
         small[:, 2, : heads * buckets].reshape(layers, heads, buckets),
         small[:, 1],
         small[:, 8:].transpose(0, 2, 1),
-        jnp.stack([k["gw_in"] for k in kept]),
-        jnp.stack([k["gw_out"] for k in kept]),
+        grad_in,
+        grad_out,
     )
 
 
@@ -1505,6 +1626,7 @@
     seq = local * mp_count
     fits = (
         groups == 1
+        and w_qkv.shape[0] == 2
         and mp_count == 4
         and dp_count % 8 == 0
         and heads % mp_count == 0

time: 926 us -> 782 us (0.84)
  Pallas kernels: 833 us -> 759 us
  local copies, waits for them, and re-layouts: 61.5 us -> 15.2 us
  other arithmetic: 18.8 us -> 1.95 us
    pallas_call x14 -> x13, Pallas kernels: 490 us -> 425 us  [the longest x8 283 us: mp_call(): pl.pallas_call(kernel, grid=(1,), out_shape=tuple((jax.ShapeDtypeStruct(s...]
    squeeze x8 -> x0, local copies, waits for them, and re-layouts: 16.3 us -> none  [the longest x2 11.7 us: fast_body(): weights[l]]
    another operation x2 -> x0, other arithmetic: 16.2 us -> none  [the longest x1 8.13 us: fast_body(): jnp.stack([k['gw_in'] for k in kept])]
    unnamed x41 -> x27, local copies, waits for them, and re-layouts: 22.1 us -> 7.42 us
    slice x7 -> x0, local copies, waits for them, and re-layouts: 9.63 us -> none  [the longest x3 4.79 us: fast_body(): weights[l]]
where the time goes in v2:
time: 782 us; the launch traced here: 777 us
  Pallas kernels  759 us (97%)
  local copies, waits for them, and re-layouts  15.2 us (2%)
    pallas_call x3, Pallas kernels, expert_call(): pl.pallas_call(functools.partial(expert_kernel, mode, layer, dp_count), o...  334 us
    pallas_call x8, Pallas kernels, mp_call(): pl.pallas_call(kernel, grid=(1,), out_shape=tuple((jax.ShapeDtypeStruct(s...  283 us
    pallas_call x2, Pallas kernels, attn_bwd(): pl.pallas_call(functools.partial(attn_bwd_kernel, heads, size, extra), gr...  78.8 us
    pallas_call x2, Pallas kernels, attn_fwd(): pl.pallas_call(functools.partial(attn_fwd_kernel, heads, size), grid=(1,)...  46.4 us
    pallas_call x1, Pallas kernels, spread_call(): pl.pallas_call(functools.partial(spread_kernel, own, layers), grid=(steps...  16.6 us

profile of v2, /device:TPU:17, one launch (start us, length us, event | category | flops | bytes accessed | tf_op | source)
XLA Modules:
  0.0 777.4 jit_solution(7644281996076462801)
XLA Ops:
  1.4 1.3 broadcast_in_dim.75.gain
  2.7 1.3 broadcast_in_dim.81.refs_3_.refs_8_
  6.5 1.7 copy.67.refs_4_.refs_7_
  8.2 0.8 fusion.36
  9.8 20.6 %shard_map.213 = bf16[4,384,768]{2,1,0:T(8,128)(2,1)} custom-call(bf16[384,768]{1,0:T(8,128)(2,1)} %bitcast.40, f32[2,1,768]{2,1,0:T(1,128)} %broadcast_in_dim.75.gain), custom_call_target="tpu_custom_call" | custom-call | tf_op jit(solution)/shard_map/pallas_call | solution.py:1093
  30.4 23.1 %shard_map.214 = (bf16[1536,576]{1,0:T(8,128)(2,1)}, bf16[1536,192]{1,0:T(8,128)(2,1)}, f32[3,1536]{1,0:T(4,128)}) custom-call(s32[1,8]{1,0:T(1,128)} %lens.7, bf16[1536,768]{1,0:T(8,128)(2,1)} %bitcast.36, bf16[2,768,2304]{2,1,0:T(8,128)(2,1)} %w_qkv.7, f32[3,1408]{1,0:T(4,128)} %get-tuple-element.159.vecs), custom_call_target="tpu_custom_call" | custom-call | tf_op jit(solution)/shard_map/pallas_call | solution.py:529
  53.5 16.0 %shard_map.215 = (f32[384,768]{1,0:T(8,128)}, bf16[384,768]{1,0:T(8,128)(2,1)}, f32[384,2]{1,0:T(8,128)}, bf16[16,16,2688]{2,1,0:T(8,128)(2,1)}) custom-call(bf16[4,384,192]{2,1,0:T(8,128)(2,1)} %bitcast.44, bf16[384,768]{1,0:T(8,128)(2,1)} %bitcast.41, bf16[2,768,768]{2,1,0:T(8,128)(2,1)} %w_attn.3, f32[2,1,768]{2,1,0:T(1,128)} %broadcast_in_dim.81.refs_3_.refs_8_, ...), custom_call_target="tpu_custom_call" | custom-call | tf_op jit(solution)/shard_map/pallas_call | solution.py:1093
  69.5 89.0 %shard_map.216 = (bf16[16,16,2688]{2,1,0:T(8,128)(2,1)}, bf16[4,448,768]{2,1,0:T(8,128)(2,1)}) custom-call(bf16[16,16,2688]{2,1,0:T(8,128)(2,1)} %get-tuple-element.68.refs_0_, bf16[2,2,768,768]{3,2,1,0:T(8,128)(2,1)} %refs_2_.9, bf16[2,2,768,768]{3,2,1,0:T(8,128)(2,1)} %refs_3_.3), custom_call_target="tpu_custom_call" | custom-call | tf_op jit(solution)/shard_map/pallas_call | solution.py:1419
  158.5 22.9 %shard_map.217 = (f32[384,768]{1,0:T(8,128)}, bf16[4,384,768]{2,1,0:T(8,128)(2,1)}) custom-call(f32[384,768]{1,0:T(8,128)} %get-tuple-element.67.middle.refs_3_, bf16[16,16,2688]{2,1,0:T(8,128)(2,1)} %get-tuple-element.69.back.refs_1_, s32[2,384,8]{2,1,0:T(8,128)} %get-tuple-element.154.refs_6_.cols, f32[384,2]{1,0:T(8,128)} %get-tuple-element.70.gates.refs_5_, ...), custom_call_target="tpu_custom_call" | custom-call | tf_op jit(solution)/shard_map/pallas_call | solution.py:1093
  181.4 23.3 %shard_map.218 = (bf16[1536,576]{1,0:T(8,128)(2,1)}, bf16[1536,192]{1,0:T(8,128)(2,1)}, f32[3,1536]{1,0:T(4,128)}) custom-call(s32[1,8]{1,0:T(1,128)} %lens.7, bf16[1536,768]{1,0:T(8,128)(2,1)} %bitcast.38, bf16[2,768,2304]{2,1,0:T(8,128)(2,1)} %w_qkv.7, f32[3,1408]{1,0:T(4,128)} %get-tuple-element.158.vecs), custom_call_target="tpu_custom_call" | custom-call | tf_op jit(solution)/shard_map/pallas_call | solution.py:529
  204.8 17.8 %shard_map.219 = (f32[384,768]{1,0:T(8,128)}, bf16[384,768]{1,0:T(8,128)(2,1)}, f32[384,2]{1,0:T(8,128)}, bf16[16,16,2688]{2,1,0:T(8,128)(2,1)}, bf16[16,16,2688]{2,1,0:T(8,128)(2,1)}) custom-call(bf16[4,384,192]{2,1,0:T(8,128)(2,1)} %bitcast.43, f32[384,768]{1,0:T(8,128)} %get-tuple-element.73.refs_1_.stream, bf16[2,768,768]{2,1,0:T(8,128)(2,1)} %w_attn.3, ...), custom_call_target="tpu_custom_call" | custom-call | tf_op jit(solution)/shard_map/pallas_call | solution.py:1093
  222.6 155.3 %shard_map.220 = (bf16[16,16,2688]{2,1,0:T(8,128)(2,1)}, bf16[16,16,2688]{2,1,0:T(8,128)(2,1)}, f32[2,768,768]{2,1,0:T(8,128)}, f32[2,768,768]{2,1,0:T(8,128)}) custom-call(bf16[16,16,2688]{2,1,0:T(8,128)(2,1)} %get-tuple-element.74.refs_0_, bf16[16,16,2688]{2,1,0:T(8,128)(2,1)} %get-tuple-element.75.refs_1_, bf16[2,2,768,768]{3,2,1,0:T(8,128)(2,1)} %refs_2_.9, ...), custom_call_target="tpu_custom_call" | custom-call | tf_op jit(solution)/shard_map/pallas_call | solution.py:1419
  377.9 26.7 %shard_map.221 = (f32[384,768]{1,0:T(8,128)}, bf16[4,384,768]{2,1,0:T(8,128)(2,1)}, f32[1,768]{1,0:T(1,128)}, f32[16,768]{1,0:T(8,128)}, bf16[384,768]{1,0:T(8,128)(2,1)}) custom-call(bf16[16,16,2688]{2,1,0:T(8,128)(2,1)} %get-tuple-element.76.refs_0_, bf16[16,16,2688]{2,1,0:T(8,128)(2,1)} %get-tuple-element.77.refs_1_, bf16[384,768]{1,0:T(8,128)(2,1)} %bitcast.47, ...), custom_call_target="tpu_custom_call" | custom-call | tf_op jit(solution)/shard_map/pallas_call | solution.py:1093
  404.6 37.9 %shard_map.222 = (bf16[1536,576]{1,0:T(8,128)(2,1)}, f32[768,768]{1,0:T(8,128)}, f32[3,1408]{1,0:T(4,128)}, f32[2,2,768,768]{3,2,1,0:T(8,128)}, f32[2,2,768,768]{3,2,1,0:T(8,128)}) custom-call(s32[1,8]{1,0:T(1,128)} %lens.7, bf16[1536,576]{1,0:T(8,128)(2,1)} %get-tuple-element.83.qkv, bf16[1536,768]{1,0:T(8,128)(2,1)} %bitcast.39, ...), custom_call_target="tpu_custom_call" | custom-call | tf_op jit(solution)/shard_map/pallas_call | solution.py:690
  442.5 44.6 %shard_map.223 = (f32[384,768]{1,0:T(8,128)}, f32[1,768]{1,0:T(1,128)}, bf16[16,16,2688]{2,1,0:T(8,128)(2,1)}, bf16[96,768]{1,0:T(8,128)(2,1)}) custom-call(bf16[4,384,576]{2,1,0:T(8,128)(2,1)} %bitcast.49, bf16[2,768,2304]{2,1,0:T(8,128)(2,1)} %w_qkv.7, f32[384,768]{1,0:T(8,128)} %get-tuple-element.73.refs_1_.stream, f32[2,1,768]{2,1,0:T(1,128)} %broadcast_in_dim.75.gain, ...), custom_call_target="tpu_custom_call" | custom-call | tf_op jit(solution)/shard_map/pallas_call | solution.py:1093
  487.1 89.5 %shard_map.224 = (bf16[16,16,2688]{2,1,0:T(8,128)(2,1)}, f32[2,768,768]{2,1,0:T(8,128)}, f32[2,768,768]{2,1,0:T(8,128)}) custom-call(bf16[16,16,2688]{2,1,0:T(8,128)(2,1)} %get-tuple-element.91.refs_0_, bf16[4,448,768]{2,1,0:T(8,128)(2,1)} %get-tuple-element.92.refs_1_, bf16[2,2,768,768]{3,2,1,0:T(8,128)(2,1)} %refs_2_.9, bf16[2,2,768,768]{3,2,1,0:T(8,128)(2,1)} %refs_3_.3), custom_call_target="tpu_custom_call" | custom-call | tf_op jit(solution)/shard_map/pallas_call | solution.py:1419
  576.5 43.4 %shard_map.225 = (f32[384,768]{1,0:T(8,128)}, bf16[4,384,768]{2,1,0:T(8,128)(2,1)}, f32[1,768]{1,0:T(1,128)}, f32[16,768]{1,0:T(8,128)}, bf16[8,96,768]{2,1,0:T(8,128)(2,1)}) custom-call(bf16[16,16,2688]{2,1,0:T(8,128)(2,1)} %get-tuple-element.93.refs_0_, bf16[16,16,2688]{2,1,0:T(8,128)(2,1)} %get-tuple-element.69.back.refs_1_, ...), custom_call_target="tpu_custom_call" | custom-call | tf_op jit(solution)/shard_map/pallas_call | solution.py:1093
  620.0 40.9 %shard_map.226 = (bf16[1536,576]{1,0:T(8,128)(2,1)}, f32[768,768]{1,0:T(8,128)}, f32[3,1408]{1,0:T(4,128)}, bf16[4,8,96,768]{3,2,1,0:T(8,128)(2,1)}) custom-call(s32[1,8]{1,0:T(1,128)} %lens.7, bf16[1536,576]{1,0:T(8,128)(2,1)} %get-tuple-element.82.qkv, bf16[1536,768]{1,0:T(8,128)(2,1)} %bitcast.37, bf16[1536,768]{1,0:T(8,128)(2,1)} %bitcast.48, ...), custom_call_target="tpu_custom_call" | custom-call | tf_op jit(solution)/shard_map/pallas_call | solution.py:690
  661.0 0.9 select_reduce_fusion.1
  663.1 91.4 %shard_map.227 = (f32[384,768]{1,0:T(8,128)}, bf16[4,8,96,768]{3,2,1,0:T(8,128)(2,1)}, f32[8,8,768]{2,1,0:T(8,128)}) custom-call(bf16[4,384,576]{2,1,0:T(8,128)(2,1)} %bitcast.50, bf16[2,768,2304]{2,1,0:T(8,128)(2,1)} %w_qkv.7, bf16[384,768]{1,0:T(8,128)(2,1)} %bitcast.42, f32[2,1,768]{2,1,0:T(1,128)} %broadcast_in_dim.75.gain, ...), custom_call_target="tpu_custom_call" | custom-call | tf_op jit(solution)/shard_map/pallas_call | solution.py:1093
  754.6 0.9 slice.26
  758.1 16.6 %shard_map.228 = (f32[2,768,2304]{2,1,0:T(8,128)}, f32[2,768,768]{2,1,0:T(8,128)}, f32[2,2,768,768]{3,2,1,0:T(8,128)}, f32[2,2,768,768]{3,2,1,0:T(8,128)}) custom-call(bf16[4,8,96,768]{3,2,1,0:T(8,128)(2,1)} %get-tuple-element.111.refs_0_, bf16[4,8,96,768]{3,2,1,0:T(8,128)(2,1)} %get-tuple-element.112.refs_1_, ...), custom_call_target="tpu_custom_call", output_to_operand_aliasing={{2}: (4, {}), {3}: (5, {})} | custom-call | tf_op jit(solution)/shard_map/pallas_call | solution.py:1456
  774.7 0.8 copy.95
  776.2 1.0 copy.96
  (51 shorter events, 8.4 us)
Async XLA Ops:
  0.6 0.7 copy-start
  620.0 41.0 %copy-start.6 = (f32[3,1408]{1,0:T(4,128)S(1)}, f32[3,1408]{1,0:T(4,128)}, u32[]{:S(2)}) copy-start(f32[3,1408]{1,0:T(4,128)} %get-tuple-element.108) | copy-start | bytes 50692
  620.0 42.4 %copy-start.4 = (f32[16,768]{1,0:T(8,128)S(1)}, f32[16,768]{1,0:T(8,128)}, u32[]{:S(2)}) copy-start(f32[16,768]{1,0:T(8,128)} %get-tuple-element.109) | copy-start | bytes 147460
  620.0 42.4 %copy-start.5 = (f32[16,768]{1,0:T(8,128)S(1)}, f32[16,768]{1,0:T(8,128)}, u32[]{:S(2)}) copy-start(f32[16,768]{1,0:T(8,128)} %get-tuple-element.105) | copy-start | bytes 147460
  620.0 42.4 %copy-start.7 = (f32[1,768]{1,0:T(1,128)S(1)}, f32[1,768]{1,0:T(1,128)}, u32[]{:S(2)}) copy-start(f32[1,768]{1,0:T(1,128)} %get-tuple-element.107) | copy-start | bytes 9220
  620.0 42.4 %copy-start.8 = (f32[1,768]{1,0:T(1,128)S(1)}, f32[1,768]{1,0:T(1,128)}, u32[]{:S(2)}) copy-start(f32[1,768]{1,0:T(1,128)} %get-tuple-element.106) | copy-start | bytes 9220
  620.0 42.4 %copy-start.9 = (f32[1,768]{1,0:T(1,128)S(1)}, f32[1,768]{1,0:T(1,128)}, u32[]{:S(2)}) copy-start(f32[1,768]{1,0:T(1,128)} %get-tuple-element.103) | copy-start | bytes 9220
  758.1 16.6 %copy-start.3 = (bf16[384,768]{1,0:T(8,128)(2,1)S(1)}, bf16[384,768]{1,0:T(8,128)(2,1)}, u32[]{:S(2)}) copy-start(bf16[384,768]{1,0:T(8,128)(2,1)} %get-tuple-element.81) | copy-start | bytes 1769476
  758.1 19.1 %copy-start.1 = (f32[2,12,32]{2,0,1:T(2,128)S(1)}, f32[2,12,32]{2,0,1:T(2,128)}, u32[]{:S(2)}) copy-start(f32[2,12,32]{2,0,1:T(2,128)} %param.19) | copy-start | bytes 9220
  774.7 1.5 copy-start.2

commit v3 on v2

--- a/solution.py
+++ b/solution.py
@@ -480,76 +480,6 @@
     return [(0, PROMPT, first), (k0, k1, second)]
 
 
-def attn_fwd_kernel(heads, size, lens, normed, w_qkv, vecs, qkv_o, mixed_o, lse_o, weight, q_s, k_s, vt_s, table, cont_bias, mixt, segc):
-    seq, model = normed.shape
-    own = heads * size
-    me = lax.axis_index("mp")
-    for m in range(model // own):
-
-        @pl.when(me == m)
-        def _():
-            for t in range(3):
-                weight[:, t * own : (t + 1) * own] = w_qkv[:, t * model + m * own : t * model + (m + 1) * own]
-
-    for i in range(seq // QB):
-        rows = pl.ds(i * QB, QB)
-        part = nn(normed[rows, :], weight[...]).astype(BF)
-        qkv_o[rows, :] = part
-        for h in range(heads):
-            q_s[h, rows, :] = part[:, h * size : (h + 1) * size] * BF(0.125)
-            k_s[h, rows, :] = part[:, own + h * size : own + (h + 1) * size]
-            vt_s[h, :, rows] = part[:, 2 * own + h * size : 2 * own + (h + 1) * size].astype(F32).T.astype(BF)
-    seg_row, _ = segments(lens, (1, seq - PROMPT), 1)
-    segc[...] = segments(lens, (seq - PROMPT, LANES), 0)[0]
-
-    def head(h, carry):
-        bias_stage(vecs[pl.ds(h, 1), :], lens, table, cont_bias)
-        for block in blocks_of(seq):
-            q0 = block[0]
-            parts = scores_of(k_s, q_s[h, q0 : q0 + QB, :], table, cont_bias, segc, seg_row, block, h)
-            top = functools.reduce(jnp.maximum, [jnp.max(s, axis=0, keepdims=True) for _, _, s in parts])
-            total, mixed = 0.0, 0.0
-            for k0, k1, s in parts:
-                p = jnp.exp(s - top)
-                total = total + jnp.sum(p, axis=0, keepdims=True)
-                mixed = mixed + nn(vt_s[h, :, k0:k1], p.astype(BF))
-            mixt[pl.ds(pl.multiple_of(h * size, size), size), q0 : q0 + QB] = mixed / total
-            lse_o[pl.ds(h, 1), q0 : q0 + QB] = top + jnp.log(total)
-        return carry
-
-    lax.fori_loop(0, heads, head, 0)
-    for i in range(seq // QB):
-        mixed_o[i * QB : (i + 1) * QB, :] = mixt[:, i * QB : (i + 1) * QB].T.astype(BF)
-
-
-def attn_fwd(lens, normed, w_qkv, layer, vecs, heads, size):
-    seq, model = normed.shape
-    own = heads * size
-    width = vecs.shape[1]
-    return pl.pallas_call(
-        functools.partial(attn_fwd_kernel, heads, size),
-        grid=(1,),
-        out_shape=(
-            jax.ShapeDtypeStruct((seq, 3 * own), BF),
-            jax.ShapeDtypeStruct((seq, own), BF),
-            jax.ShapeDtypeStruct((heads, seq), F32),
-        ),
-        in_specs=[SMEM, VMEM, layer_spec(w_qkv, layer), VMEM],
-        out_specs=(VMEM, VMEM, VMEM),
-        scratch_shapes=[
-            pltpu.VMEM((model, 3 * own), BF),
-            pltpu.VMEM((heads, seq, size), BF),
-            pltpu.VMEM((heads, seq, size), BF),
-            pltpu.VMEM((heads, size, seq), BF),
-            pltpu.VMEM((width - LANES, LANES), F32),
-            pltpu.VMEM((PROMPT, seq - PROMPT), F32),
-            pltpu.VMEM((own, seq), F32),
-            pltpu.VMEM((seq - PROMPT, LANES), jnp.int32),
-        ],
-        compiler_params=pltpu.CompilerParams(vmem_limit_bytes=VMEM_BYTES),
-    )(lens, normed, w_qkv, vecs)
-
-
 def attn_bwd_kernel(heads, size, extra, lens, qkv, normed, branch, w_attn, mixed, lse, vecs, *refs):
     refs = list(refs)
     if extra == "copy":
@@ -763,7 +693,27 @@
     for i in range(3):
         send[:, :, i * model : (i + 1) * model] = pick(i, 0, slice(0, model)).astype(BF).reshape(experts, tile, model)
     tail = pick(3, 0, slice(0, half)) + pick(3, 8, slice(half, model))
-    send[:, :, 3 * model :] = tail.astype(BF).reshape(experts, tile, half)
+    send[:, :, 3 * model : 3 * model + half] = tail.astype(BF).reshape(experts, tile, half)
+
+
+def scatter_gates(rows, gates, send, start):
+    experts, tile, _ = send.shape
+    tokens = rows.shape[1]
+    at = lax.broadcasted_iota(jnp.int32, (experts * tile, tokens), 0)
+    lane = lax.broadcasted_iota(jnp.int32, (tokens, LANES), 1)
+    total = 0.0
+    for j in range(2):
+        slot = rows[2 + j : 3 + j, :]
+        piece = jnp.where(rows[4 + j : 5 + j, :] > 0, slot // tile, -1)
+        place = rows[j : j + 1, :] * tile + slot % tile
+        high = gates[j].astype(BF).astype(F32)
+        rest = gates[j] - high
+        mid = rest.astype(BF).astype(F32)
+        part = jnp.where(lane % 3 == 0, high, jnp.where(lane % 3 == 1, mid, rest - mid))
+        for i in range(4):
+            hot = (jnp.where(piece == i, place, -1) == at).astype(BF)
+            total = total + nn(hot, jnp.where(lane // 3 == i, part, 0.0).astype(BF))
+    send[:, :, start:] = total.astype(BF).reshape(experts, tile, LANES)
 
 
 def gather_rows(cols, j, back):
@@ -881,41 +831,152 @@
     )
 
 
-def first_kernel(tokens, gain, all_o, held, ssem, rsem):
-    greet_mp(2)
-    me = lax.axis_index("mp")
-    stream = tokens[...].astype(F32)
-    held[me] = (stream * mean_square_scale(stream) * gain[...]).astype(BF)
-    gather_mp(held, ssem, rsem)
-    all_o[...] = held[...]
-
-
-def next_kernel(middle, back, cols, gates, gain, stream_o, all_o, held, ssem, rsem):
-    greet_mp(2)
-    me = lax.axis_index("mp")
-    stream = middle[...]
-    for j in range(2):
-        stream = stream + gates[:, j : j + 1] * gather_rows(cols, j, back)
-    stream_o[...] = stream
-    held[me] = (stream * mean_square_scale(stream) * gain[...]).astype(BF)
-    gather_mp(held, ssem, rsem)
-    all_o[...] = held[...]
-
-
-def middle_kernel(with_grad, *refs):
-    if with_grad:
-        (mixed, stream, w_attn, gain, router, rows, cols, cotangent, middle_o, ffn_o, gates_o, send_o, back_o, held, ssem, rsem, lsem) = refs
+def pre_kernel(layer, layers, heads, size, *refs):
+    refs = list(refs)
+
+    def take(count):
+        taken = refs[:count]
+        del refs[:count]
+        return taken
+
+    first, last = layer == 0, layer == layers - 1
+    lens, gain_a, w_qkv, vecs, w_attn, gain_f, router, rows, cols = take(9)
+    if first:
+        tokens, cotangent, far_rows = take(3)
     else:
-        (mixed, stream, w_attn, gain, router, rows, cols, middle_o, ffn_o, gates_o, send_o, held, ssem, rsem, lsem) = refs
-    greet_mp(3)
-    for copy in swap_mp(mixed, held, ssem, rsem, lsem):
-        copy.wait()
-    part = held.shape[2]
-    middle = stream[...].astype(F32)
-    for m in range(held.shape[0]):
-        middle = middle + nn(held[m], w_attn[m * part : (m + 1) * part, :])
+        before, returned, cols_in, gates_in = take(4)
+    (g_in,) = take(1) if last else (None,)
+    (stream_o,) = (None,) if first else take(1)
+    normed_o, qkv_o, mixed_o, lse_o, middle_o, ffn_o, gates_o, send_o = take(8)
+    (g_o,) = take(1) if first or last else (None,)
+    held, hssem, hrsem = take(3)
+    weight, q_s, k_s, vt_s, table, cont_bias, mixt, segc, out_s, mixed_s, mssem, mrsem = take(12)
+    if first:
+        g_send, g_held, gssem, grsem = take(4)
+    elif last:
+        g_held, gssem, grsem = take(3)
+    me, core, mate, across, diagonal = mp_places()
+    d = lax.axis_index("dp")
+    dp_count = lax.axis_size("dp")
+    seq, own = mixed_o.shape
+    local, model = middle_o.shape
+    parts = local // LANES
+
+    barrier = pltpu.get_barrier_semaphore()
+    for to in (mate, across, diagonal):
+        signal_to(barrier, mp=to)
+    if first:
+        for k in range(2, 2 * dp_count):
+            signal_to(barrier, dp=lax.rem(d + k // 2, dp_count), mp=(me // 2) * 2 + lax.rem(core + k % 2, 2))
+        count = 3 + 2 * dp_count - 2
+    else:
+        count = 3
+    if first:
+        stream = tokens[...].astype(F32)
+    else:
+        stream = before[...]
+        for j in range(2):
+            stream = stream + gates_in[:, j : j + 1] * gather_rows(cols_in, j, returned)
+        stream_o[...] = stream
+    held[me] = (stream * mean_square_scale(stream) * gain_a[...]).astype(BF)
+    pl.semaphore_wait(barrier, count)
+    over = remote(held.at[me], held.at[me], hssem.at[1], hrsem.at[1], mp=across)
+    to_mate = remote(held.at[me], held.at[me], hssem.at[0], hrsem.at[0], mp=mate)
+    passed = remote(held.at[across], held.at[across], hssem.at[2], hrsem.at[2], mp=mate)
+    over.start()
+    to_mate.start()
+
+    extras = []
+    if first:
+        scatter_rows(far_rows, [cotangent[...]], g_send)
+        index = d * 2 + core
+        extras.append(pltpu.make_async_copy(g_send.at[index], g_held.at[index], grsem.at[0]))
+        for k in range(1, 2 * dp_count):
+            dd, cc = lax.rem(d + k // 2, dp_count), lax.rem(core + k % 2, 2)
+            extras.append(
+                remote(g_send.at[dd * 2 + cc], g_held.at[index], gssem.at[k], grsem.at[k], dp=dd, mp=(me // 2) * 2 + cc)
+            )
+    elif last:
+        extras.append(remote(g_in, g_held, gssem, grsem, mp=across))
+    for copy in extras:
+        copy.start()
+
+    for m in range(model // own):
+
+        @pl.when(me == m)
+        def _():
+            for t in range(3):
+                weight[:, t * own : (t + 1) * own] = w_qkv[:, t * model + m * own : t * model + (m + 1) * own]
+
+    seg_row, _ = segments(lens, (1, seq - PROMPT), 1)
+    segc[...] = segments(lens, (seq - PROMPT, LANES), 0)[0]
+
+    def tables(h, carry):
+        bias_stage(vecs[pl.ds(h, 1), :], lens, table.at[h], cont_bias.at[h])
+        return carry
+
+    lax.fori_loop(0, heads, tables, 0)
+
+    def project(m):
+        at = pl.ds(pl.multiple_of(m * local, LANES), local)
+        part = nn(held[m], weight[...]).astype(BF)
+        qkv_o[at, :] = part
+        for h in range(heads):
+            q_s[h, at, :] = part[:, h * size : (h + 1) * size] * BF(0.125)
+            k_s[h, at, :] = part[:, own + h * size : own + (h + 1) * size]
+            vt_s[h, :, at] = part[:, 2 * own + h * size : 2 * own + (h + 1) * size].astype(F32).T.astype(BF)
+
+    project(me)
+    to_mate.wait_recv()
+    project(mate)
+    over.wait_recv()
+    passed.start()
+    project(across)
+    passed.wait_recv()
+    project(diagonal)
+
+    def handed(n):
+        return remote(out_s.at[n], mixed_s.at[me, n % parts], mssem.at[n], mrsem.at[me, n % parts], mp=n // parts)
+
+    for block in blocks_of(seq):
+        q0 = block[0]
+
+        def head(h, carry):
+            query = q_s[h, q0 : q0 + QB, :]
+            scored = scores_of(k_s, query, table.at[h], cont_bias.at[h], segc, seg_row, block, h)
+            top = functools.reduce(jnp.maximum, [jnp.max(s, axis=0, keepdims=True) for _, _, s in scored])
+            total, mixed = 0.0, 0.0
+            for k0, k1, s in scored:
+                p = jnp.exp(s - top)
+                total = total + jnp.sum(p, axis=0, keepdims=True)
+                mixed = mixed + nn(vt_s[h, :, k0:k1], p.astype(BF))
+            mixt[pl.ds(pl.multiple_of(h * size, size), size), :] = mixed / total
+            lse_o[pl.ds(h, 1), q0 : q0 + QB] = top + jnp.log(total)
+            return carry
+
+        lax.fori_loop(0, heads, head, 0)
+        done = mixt[...].T.astype(BF)
+        mixed_o[q0 : q0 + QB, :] = done
+        for half in range(QB // LANES):
+            n = q0 // LANES + half
+            out_s[n] = done[half * LANES : (half + 1) * LANES, :]
+
+            @pl.when(me == n // parts)
+            def _():
+                pltpu.make_async_copy(out_s.at[n], mixed_s.at[me, n % parts], mrsem.at[me, n % parts]).start()
+
+            @pl.when(me != n // parts)
+            def _():
+                handed(n).start()
+
+    normed_o[...] = held[...]
+    middle = stream
+    for m in range(mixed_s.shape[0]):
+        for n in range(parts):
+            pltpu.make_async_copy(mixed_s.at[m, n], mixed_s.at[m, n], mrsem.at[m, n]).wait()
+        middle = middle + nn(mixed_s[m].reshape(local, own), w_attn[m * own : (m + 1) * own, :])
     middle_o[...] = middle
-    ffn = (middle * mean_square_scale(middle) * gain[...]).astype(BF)
+    ffn = (middle * mean_square_scale(middle) * gain_f[...]).astype(BF)
     ffn_o[...] = ffn
     logits = nn(ffn, router[...])
     expert = lax.broadcasted_iota(jnp.int32, logits.shape, 1)
@@ -927,9 +988,70 @@
     gates = [p / (powers[0] + powers[1]) for p in powers]
     gates_o[...] = jnp.concatenate(gates, 1)
     scatter_rows(rows, [ffn], send_o)
-    if with_grad:
-        flow = cotangent[...].astype(F32)
-        scatter_rows(rows, [(gates[j] * cols[:, 4 + j : 5 + j].astype(F32) * flow).astype(BF) for j in range(2)], back_o)
+    if last:
+        scatter_gates(rows, gates, send_o, 7 * model // 2)
+    if first or last:
+        for copy in extras:
+            if first and copy is extras[0]:
+                copy.wait()
+            else:
+                copy.wait_send()
+                copy.wait_recv()
+        g_o[...] = g_held[...]
+    for copy in (to_mate, over, passed):
+        copy.wait_send()
+    for n in range(seq // LANES):
+
+        @pl.when(me != n // parts)
+        def _():
+            handed(n).wait_send()
+
+
+def pre_call(layer, layers, number, heads, size, lens, normal, mp_count, dp_count, local, model, specials, block):
+    first, last = layer == 0, layer == layers - 1
+    seq, own = local * mp_count, heads * size
+    width = PROMPT + 3 * LANES
+    args = list(normal) + list(specials)
+    specs = [SMEM] + [layer_spec(*a) if isinstance(a, tuple) else VMEM for a in args]
+    narrow = block[:2] + (7 * model // 2,)
+    send = narrow[:2] + (narrow[2] + LANES,) if last else narrow
+    outs = [] if first else [((local, model), F32)]
+    outs += [
+        ((mp_count, local, model), BF), ((seq, 3 * own), BF), ((seq, own), BF), ((heads, seq), F32),
+        ((local, model), F32), ((local, model), BF), ((local, 2), F32), (send, BF),
+    ]
+    if first or last:
+        outs.append((narrow, BF))
+    scratch = [
+        pltpu.VMEM((mp_count, local, model), BF), dma(3), dma(3),
+        pltpu.VMEM((model, 3 * own), BF),
+        pltpu.VMEM((heads, seq, size), BF),
+        pltpu.VMEM((heads, seq, size), BF),
+        pltpu.VMEM((heads, size, seq), BF),
+        pltpu.VMEM((heads, width - LANES, LANES), F32),
+        pltpu.VMEM((heads, PROMPT, seq - PROMPT), F32),
+        pltpu.VMEM((own, QB), F32),
+        pltpu.VMEM((seq - PROMPT, LANES), jnp.int32),
+        pltpu.VMEM((seq // LANES, LANES, own), BF),
+        pltpu.VMEM((mp_count, local // LANES, LANES, own), BF),
+        dma(seq // LANES),
+        dma(mp_count, local // LANES),
+    ]
+    if first:
+        scratch += [pltpu.VMEM(narrow, BF), pltpu.VMEM(narrow, BF), dma(2 * dp_count), dma(2 * dp_count)]
+    elif last:
+        scratch += [pltpu.VMEM(narrow, BF), dma(), dma()]
+    return pl.pallas_call(
+        functools.partial(pre_kernel, layer, layers, heads, size),
+        grid=(1,),
+        out_shape=tuple(jax.ShapeDtypeStruct(shape, kind) for shape, kind in outs),
+        in_specs=specs,
+        out_specs=tuple([VMEM] * len(outs)),
+        scratch_shapes=scratch,
+        compiler_params=pltpu.CompilerParams(
+            collective_id=number, has_side_effects=True, vmem_limit_bytes=VMEM_BYTES
+        ),
+    )(lens, *[a[0] if isinstance(a, tuple) else a for a in args])
 
 
 def post_kernel(with_output, *refs):
@@ -1118,18 +1240,17 @@
         del refs[:count]
         return taken
 
-    (send_x,) = take(1) if forward else (None,)
-    (send_g,) = take(1) if backward else (None,)
+    (sending,) = take(1)
+    far = take(2) if mode == "both" else None
     (x_in,) = take(1) if mode == "bwd" else (None,)
     w_in, w_out = take(2)
-    (out_o,) = take(1) if forward else (None,)
+    results = take(forward + backward)
     (x_o,) = take(1) if mode == "fwd" else (None,)
-    grad_o, gw_in_o, gw_out_o = take(3) if backward else (None, None, None)
+    gw_in_o, gw_out_o = take(2) if backward else (None, None)
     w1, w2, wsem, wssem, wrsem = take(5)
-    kept_part, x_all, xsem = take(3)
-    paths = []
-    for sending in ([send_x] if forward else []) + ([send_g] if backward else []):
-        paths.append((sending, take(14)))
+    x_all, xsem = take(2)
+    recv_a, recv_b, ssem, asem, fsem, bsem = take(6)
+    paths = [take(9) for _ in results]
     if backward:
         g_all, hid_all, ig_all, stage, gsem, grsem, glsem = take(7)
 
@@ -1138,10 +1259,11 @@
     row = me // 2
     index = d * 2 + core
     experts = dp_count * 2
-    groups = dp_count // 2
     model = w1.shape[1]
     half = model // 2
     rows_a = x_all.shape[1] // 2
+    tile = sending.shape[1]
+    ahead = 3
 
     barrier = pltpu.get_barrier_semaphore()
 
@@ -1153,174 +1275,148 @@
     signal_to(barrier, mp=across)
     pl.semaphore_wait(barrier, experts)
 
-    def send_all(path):
-        sending, (recv_a, recv_b, ssem, asem, fsem, bsem, part, pssem, prsem, ret_s, ret, rssem, rrsem, psend) = path
-
-        def one(k, carry):
-            dd, cc = lax.rem(d + k // 2, dp_count), lax.rem(core + k % 2, 2)
+    def send_wave(k):
+        dd = lax.rem(d + k, dp_count)
+        for cc in range(2):
             to = dd * 2 + cc
-            remote(sending.at[to], recv_a.at[index], ssem.at[to], asem.at[index], dp=dd, mp=row * 2 + cc).start()
-            return carry
-
-        lax.fori_loop(1, experts, one, 0)
-        pltpu.make_async_copy(sending.at[index], recv_a.at[index], asem.at[index]).start()
-
-    send_all(paths[0])
+
+            @pl.when(to == index)
+            def _():
+                pltpu.make_async_copy(sending.at[to], recv_a.at[index], asem.at[index]).start()
+
+            @pl.when(to != index)
+            def _():
+                remote(sending.at[to], recv_a.at[index], ssem.at[to], asem.at[index], dp=dd, mp=row * 2 + cc).start()
+
+    for k in range(ahead):
+        send_wave(k)
     copies = []
     for n, (source, held) in enumerate(((w_in, w1), (w_out, w2))):
         copies.append(remote(source.at[layer, 1 - core], held.at[core], wssem.at[n], wrsem.at[n], mp=mate))
         copies.append(pltpu.make_async_copy(source.at[layer, core], held.at[core], wsem.at[n]))
+    if mode == "bwd":
+        copies.append(pltpu.make_async_copy(x_in, x_all, xsem))
     for copy in copies:
         copy.start()
-    if mode == "bwd":
-        saved = pltpu.make_async_copy(x_in, x_all, xsem)
-        saved.start()
-    for path in paths[1:]:
-        send_all(path)
     for copy in copies:
         copy.wait()
-    if mode == "bwd":
-        saved.wait()
-
-    def source_of(g, kk):
-        return lax.rem(d + dp_count - (g * 2 + kk), dp_count)
-
-    def unpack(held, g, side, into):
+
+    def source_of(g):
+        return lax.rem(d + dp_count - g, dp_count)
+
+    def unpack(held, g, side, into, gates):
         base = side * rows_a
-        for kk in range(2):
-            s0 = source_of(g, kk)
-            tails = []
+        s0 = source_of(g)
+        tails = []
+        for cc in range(2):
+            src = s0 * 2 + cc
+            block = held[src]
+            factors = None if gates is None else gates[src][:, 7 * half :].astype(F32)
+
+            def factor(i):
+                return factors[:, 3 * i : 3 * i + 1] + factors[:, 3 * i + 1 : 3 * i + 2] + factors[:, 3 * i + 2 : 3 * i + 3]
+
+            for i in range(3):
+                piece = block[:, i * model : (i + 1) * model]
+                if gates is not None:
+                    piece = (piece.astype(F32) * factor(i)).astype(BF)
+                into[g, base + (2 * i + cc) * tile : base + (2 * i + cc + 1) * tile, :] = piece
+            tail = unfold_tail(block[:, 3 * model : 7 * half], half)
+            tails.append(tail if gates is None else tail * factor(3)[0:8, :])
+        into[g, base + 6 * tile : base + 7 * tile, :] = jnp.concatenate(tails, 0).astype(BF)
+
+    def forward_copy(s0):
+        two = pl.ds(s0 * 2, 2)
+        return remote(recv_a.at[two], recv_b.at[two], fsem.at[s0], bsem.at[s0], mp=across)
+
+    def partial_copy(path, g):
+        kept, part, pssem, prsem, ret_s, ret, rssem, rrsem, psend = path
+        return remote(psend.at[g], part.at[g], pssem.at[g], prsem.at[g], mp=across)
+
+    def compute(g):
+        x = x_all[g]
+        totals = [0.0] * len(results)
+        for q in range(2):
+            inner = nn(x, w1[q])
+            if backward:
+                value, slope = gelu_grad(inner)
+                hidden = value.astype(BF)
+                hid_all[q, g] = hidden
+                grad = (nt(g_all[g], w2[q]) * slope).astype(BF)
+                ig_all[q, g] = grad
+                totals[-1] = totals[-1] + nt(grad, w1[q])
+            else:
+                hidden = gelu_tanh(inner).astype(BF)
+            if forward:
+                totals[0] = totals[0] + nn(hidden, w2[q])
+        return totals
+
+    def give_back(path, g):
+        kept, part, pssem, prsem, ret_s, ret, rssem, rrsem, psend = path
+        partial_copy(path, g).wait_recv()
+        total = kept[lax.rem(g, 2)] + part[g].astype(F32)
+        s0 = source_of(g)
+        for cc in range(2):
+            src = s0 * 2 + cc
+            for i in range(3):
+                at = (2 * i + cc) * tile
+                ret_s[src, :, i * model : (i + 1) * model] = total[at : at + tile, :].astype(BF)
+            at = 6 * tile + 8 * cc
+            ret_s[src, :, 3 * model :] = jnp.concatenate(
+                [total[at : at + 8, 0:half], total[at : at + 8, half:]], 0
+            ).astype(BF)
+
+            @pl.when(src == index)
+            def _():
+                pltpu.make_async_copy(ret_s.at[src], ret.at[index], rrsem.at[index]).start()
+
+            @pl.when(src != index)
+            def _():
+                remote(ret_s.at[src], ret.at[index], rssem.at[src], rrsem.at[index], dp=s0, mp=row * 2 + cc).start()
+
+    def step(i, carry):
+        @pl.when(i < dp_count)
+        def _():
+            s0 = source_of(i)
             for cc in range(2):
-                block = held[s0 * 2 + cc]
-                for i in range(3):
-                    into[g, base + i * 64 + kk * 32 + cc * 16 : base + i * 64 + kk * 32 + cc * 16 + 16, :] = block[
-                        :, i * model : (i + 1) * model
-                    ]
-                tails.append(unfold_tail(block[:, 3 * model :], half))
-            into[g, base + 192 + kk * 16 : base + 208 + kk * 16, :] = jnp.concatenate(tails, 0).astype(BF)
-
-    def run_path(path, into, compute):
-        sending, (recv_a, recv_b, ssem, asem, fsem, bsem, part, pssem, prsem, ret_s, ret, rssem, rrsem, psend) = path
-
-        def forward_copy(s0):
-            two = pl.ds(s0 * 2, 2)
-            return remote(recv_a.at[two], recv_b.at[two], fsem.at[s0], bsem.at[s0], mp=across)
-
-        def partial_copy(g):
-            return remote(psend.at[g], part.at[g], pssem.at[g], prsem.at[g], mp=across)
-
-        def step(i, carry):
-            @pl.when(i < groups)
-            def _():
-                for kk in range(2):
-                    s0 = source_of(i, kk)
-                    for cc in range(2):
-                        src = s0 * 2 + cc
-                        pltpu.make_async_copy(recv_a.at[src], recv_a.at[src], asem.at[src]).wait()
-                    forward_copy(s0).start()
-
-            @pl.when((i >= 1) & (i <= groups))
-            def _():
-                g = i - 1
-                for kk in range(2):
-                    forward_copy(source_of(g, kk)).wait_recv()
-                unpack(recv_a, g, 0, into)
-                unpack(recv_b, g, 1, into)
-                total = compute(g)
-                kept_part[lax.rem(g, 2)] = total[0:rows_a, :]
+                src = s0 * 2 + cc
+                pltpu.make_async_copy(recv_a.at[src], recv_a.at[src], asem.at[src]).wait()
+            forward_copy(s0).start()
+
+        @pl.when(i + ahead < dp_count)
+        def _():
+            send_wave(i + ahead)
+
+        @pl.when((i >= 1) & (i <= dp_count))
+        def _():
+            g = i - 1
+            forward_copy(source_of(g)).wait_recv()
+            for side, held in enumerate((recv_a, recv_b)):
+                if forward:
+                    unpack(held, g, side, x_all, None)
+                if mode == "both":
+                    unpack(far[side], g, side, g_all, held)
+                elif mode == "bwd":
+                    unpack(held, g, side, g_all, None)
+            for path, total in zip(paths, compute(g)):
+                kept, psend = path[0], path[8]
+                kept[lax.rem(g, 2)] = total[0:rows_a, :]
                 psend[g] = total[rows_a:, :].astype(BF)
-                partial_copy(g).start()
-
-            @pl.when(i >= 2)
-            def _():
-                g = i - 2
-                partial_copy(g).wait_recv()
-                total = kept_part[lax.rem(g, 2)] + part[g].astype(F32)
-                for kk in range(2):
-                    s0 = source_of(g, kk)
-                    for cc in range(2):
-                        src = s0 * 2 + cc
-                        for n in range(3):
-                            at = n * 64 + kk * 32 + cc * 16
-                            ret_s[src, :, n * model : (n + 1) * model] = total[at : at + 16, :].astype(BF)
-                        at = 192 + kk * 16 + cc * 8
-                        ret_s[src, :, 3 * model :] = jnp.concatenate(
-                            [total[at : at + 8, 0:half], total[at : at + 8, half:]], 0
-                        ).astype(BF)
-
-                        @pl.when(src == index)
-                        def _():
-                            pltpu.make_async_copy(ret_s.at[src], ret.at[index], rrsem.at[index]).start()
-
-                        @pl.when(src != index)
-                        def _():
-                            remote(
-                                ret_s.at[src], ret.at[index], rssem.at[src], rrsem.at[index], dp=s0, mp=row * 2 + cc
-                            ).start()
-
-            return carry
-
-        lax.fori_loop(0, groups + 2, step, 0)
-
-    def finish_path(path, result):
-        sending, (recv_a, recv_b, ssem, asem, fsem, bsem, part, pssem, prsem, ret_s, ret, rssem, rrsem, psend) = path
-
-        def end(e, carry):
-            pltpu.make_async_copy(ret.at[e], ret.at[e], rrsem.at[e]).wait()
-
-            @pl.when(e != index)
-            def _():
-                pltpu.make_async_copy(ret_s.at[e], ret_s.at[e], rssem.at[e]).wait()
-                pltpu.make_async_copy(sending.at[e], sending.at[e], ssem.at[e]).wait()
-
-            return carry
-
-        lax.fori_loop(0, experts, end, 0)
-
-        def end_pair(s0, carry):
-            two = pl.ds(s0 * 2, 2)
-            pltpu.make_async_copy(recv_a.at[two], recv_a.at[two], fsem.at[s0]).wait()
-            return carry
-
-        lax.fori_loop(0, dp_count, end_pair, 0)
-
-        def end_group(g, carry):
-            pltpu.make_async_copy(psend.at[g], psend.at[g], pssem.at[g]).wait()
-            return carry
-
-        lax.fori_loop(0, groups, end_group, 0)
-        result[...] = ret[...]
-
-    def compute_forward(g):
-        x = x_all[g]
-        total = 0.0
-        for q in range(2):
-            hidden = gelu_tanh(nn(x, w1[q])).astype(BF)
-            if backward:
-                hid_all[q, g] = hidden
-            total = total + nn(hidden, w2[q])
-        return total
-
-    def compute_backward(g):
-        x, gr = x_all[g], g_all[g]
-        total = 0.0
-        for q in range(2):
-            value, slope = gelu_grad(nn(x, w1[q]))
-            if not forward:
-                hid_all[q, g] = value.astype(BF)
-            inner = (nt(gr, w2[q]) * slope).astype(BF)
-            ig_all[q, g] = inner
-            total = total + nt(inner, w1[q])
-        return total
-
-    if forward:
-        run_path(paths[0], x_all, compute_forward)
-        if mode == "fwd":
-            saved = pltpu.make_async_copy(x_all, x_o, xsem)
-            saved.start()
+                partial_copy(path, g).start()
+
+        @pl.when(i >= 2)
+        def _():
+            for path in paths:
+                give_back(path, i - 2)
+
+        return carry
+
+    lax.fori_loop(0, dp_count + 2, step, 0)
+    if mode == "fwd":
+        saved = pltpu.make_async_copy(x_all, x_o, xsem)
+        saved.start()
     if backward:
-        run_path(paths[-1], g_all, compute_backward)
-        count = groups * 2 * rows_a
+        count = dp_count * 2 * rows_a
 
         def products(n, q):
             if n == 0:
@@ -1340,26 +1436,60 @@
             copy = pltpu.make_async_copy(stage.at[n], outs[n].at[core], glsem.at[n])
             copy.start()
             copies.append(copy)
+    for path, result in zip(paths, results):
+        kept, part, pssem, prsem, ret_s, ret, rssem, rrsem, psend = path
+
+        def end(e, carry):
+            pltpu.make_async_copy(ret.at[e], ret.at[e], rrsem.at[e]).wait()
+
+            @pl.when(e != index)
+            def _():
+                pltpu.make_async_copy(ret_s.at[e], ret_s.at[e], rssem.at[e]).wait()
+
+            return carry
+
+        lax.fori_loop(0, experts, end, 0)
+
+        def end_group(g, carry):
+            pltpu.make_async_copy(psend.at[g], psend.at[g], pssem.at[g]).wait()
+            return carry
+
+        lax.fori_loop(0, dp_count, end_group, 0)
+        result[...] = ret[...]
+
+    def end_send(e, carry):
+        @pl.when(e != index)
+        def _():
+            pltpu.make_async_copy(sending.at[e], sending.at[e], ssem.at[e]).wait()
+
+        return carry
+
+    lax.fori_loop(0, experts, end_send, 0)
+
+    def end_pair(s0, carry):
+        two = pl.ds(s0 * 2, 2)
+        pltpu.make_async_copy(recv_a.at[two], recv_a.at[two], fsem.at[s0]).wait()
+        return carry
+
+    lax.fori_loop(0, dp_count, end_pair, 0)
+    if mode == "fwd":
+        saved.wait()
+    if backward:
         for n in range(2):
             copies[n].wait_recv()
             copies[2 + n].wait()
-    if forward:
-        finish_path(paths[0], out_o)
-        if mode == "fwd":
-            saved.wait()
-    if backward:
-        finish_path(paths[-1], grad_o)
-
-
-def expert_call(mode, layer, number, dp_count, sends, x_in, w_in, w_out):
+
+
+def expert_call(mode, layer, number, dp_count, send, far, x_in, w_in, w_out):
     forward, backward = mode in ("fwd", "both"), mode in ("both", "bwd")
-    shape = sends[0].shape
-    experts, tile, wide = shape
+    experts, tile, _ = send.shape
     model = w_in.shape[2]
-    groups = dp_count // 2
-    rows = 2 * 4 * 56
-    args = list(sends)
-    specs = [VMEM] * len(sends)
+    block = (experts, tile, 7 * model // 2)
+    rows = 2 * 7 * tile
+    args, specs = [send], [VMEM]
+    if mode == "both":
+        args += far
+        specs += [VMEM] * 2
     if mode == "bwd":
         args.append(x_in)
         specs.append(ANY)
@@ -1371,12 +1501,11 @@
         outs.append(jax.ShapeDtypeStruct(dims, kind))
         out_specs.append(spec)
 
-    if forward:
-        out(shape, BF, VMEM)
+    for _ in range(forward + backward):
+        out(block, BF, VMEM)
     if mode == "fwd":
-        out((groups, rows, model), BF, ANY)
+        out((dp_count, rows, model), BF, ANY)
     if backward:
-        out(shape, BF, VMEM)
         out((2, model, model), F32, ANY)
         out((2, model, model), F32, ANY)
     scratch = [
@@ -1385,32 +1514,32 @@
         dma(2),
         dma(2),
         dma(2),
-        pltpu.VMEM((2, rows // 2, model), F32),
-        pltpu.VMEM((groups, rows, model), BF),
+        pltpu.VMEM((dp_count, rows, model), BF),
         dma(),
+        pltpu.VMEM(send.shape, BF),
+        pltpu.VMEM(send.shape, BF),
+        dma(experts),
+        dma(experts),
+        dma(dp_count),
+        dma(dp_count),
     ]
-    for _ in sends:
+    for _ in range(forward + backward):
         scratch += [
-            pltpu.VMEM(shape, BF),
-            pltpu.VMEM(shape, BF),
+            pltpu.VMEM((2, rows // 2, model), F32),
+            pltpu.VMEM((dp_count, rows // 2, model), BF),
+            dma(dp_count),
+            dma(dp_count),
+            pltpu.VMEM(block, BF),
+            pltpu.VMEM(block, BF),
             dma(experts),
             dma(experts),
-            dma(dp_count),
-            dma(dp_count),
-            pltpu.VMEM((groups, rows // 2, model), BF),
-            dma(groups),
-            dma(groups),
-            pltpu.VMEM(shape, BF),
-            pltpu.VMEM(shape, BF),
-            dma(experts),
-            dma(experts),
-            pltpu.VMEM((groups, rows // 2, model), BF),
+            pltpu.VMEM((dp_count, rows // 2, model), BF),
         ]
     if backward:
         scratch += [
-            pltpu.VMEM((groups, rows, model), BF),
-            pltpu.VMEM((2, groups, rows, model), BF),
-            pltpu.VMEM((2, groups, rows, model), BF),
+            pltpu.VMEM((dp_count, rows, model), BF),
+            pltpu.VMEM((2, dp_count, rows, model), BF),
+            pltpu.VMEM((2, dp_count, rows, model), BF),
             pltpu.VMEM((2, model, model), F32),
             dma(2),
             dma(2),
@@ -1505,36 +1634,31 @@
         return [pltpu.VMEM((mp_count, local, width), BF)], [dma(3), dma(3), dma()]
 
     kept = [None] * layers
-    stream = tokens[0]
-    sends, back, x_rows = None, None, None
+    back, far = None, [None, None]
     for l in range(layers):
-        if l == 0:
-            (normed,) = mp_call(first_kernel, 0, [(held, BF)], gather, stream, (gain_a, l))
+        first, last = l == 0, l == layers - 1
+        normal = [(gain_a, l), (w_qkv, l), vecs[l], (w_attn, l), (gain_f, l), (router, l), (rows, l), (cols, l)]
+        if first:
+            specials = [tokens[0], cotangent[0], (rows, layers - 1)]
         else:
             before = kept[l - 1]
-            stream, normed = mp_call(
-                next_kernel, 1, [((local, model), F32), (held, BF)], gather,
-                before["middle"], before["out"], (cols, l - 1), before["gates"], (gain_a, l),
-            )
-        normed = normed.reshape(seq, model)
-        qkv, mixed, lse = attn_fwd(cont_lengths, normed, w_qkv, l, vecs[l], own_heads, size)
-        last = l == layers - 1
-        outs = [((local, model), F32), ((local, model), BF), ((local, 2), F32), (block, BF)] + ([(block, BF)] if last else [])
-        args = [mixed.reshape(mp_count, local, own), stream, (w_attn, l), (gain_f, l), (router, l), (rows, l), (cols, l)]
-        space, sems = swap(own)
-        got = mp_call(
-            functools.partial(middle_kernel, last), 2 + last, outs, space + sems,
-            *args, *([cotangent[0]] if last else []),
-        )
-        middle, ffn, gates = got[:3]
-        kept[l] = dict(stream=stream, normed=normed, qkv=qkv, mixed=mixed, lse=lse, middle=middle, ffn=ffn, gates=gates)
+            specials = [before["middle"], before["out"], (cols, l - 1), before["gates"]]
         if last:
-            out, back, gw_in, gw_out = expert_call("both", l, 5, dp_count, got[3:5], None, w_in, w_out)
-            kept[l].update(gw_in=gw_in, gw_out=gw_out)
+            specials.append(far[0])
+        got = pre_call(
+            l, layers, l, own_heads, size, cont_lengths, normal, mp_count, dp_count, local, model, specials, block
+        )
+        got = [tokens[0]] + list(got) if first else list(got)
+        names = ("stream", "normed", "qkv", "mixed", "lse", "middle", "ffn", "gates")
+        kept[l] = k = dict(zip(names, got))
+        k["normed"] = k["normed"].reshape(seq, model)
+        if first:
+            far[0] = got[9]
+        if last:
+            far[1] = got[9]
+            k["out"], back, k["gw_in"], k["gw_out"] = expert_call("both", l, 5, dp_count, got[8], far, None, w_in, w_out)
         else:
-            out, x_rows = expert_call("fwd", l, 4, dp_count, got[3:4], None, w_in, w_out)
-            kept[l].update(x_rows=x_rows)
-        kept[l].update(out=out)
+            k["out"], k["x_rows"] = expert_call("fwd", l, 4, dp_count, got[8], None, None, w_in, w_out)
 
     flow = cotangent[0]
     for l in reversed(range(layers)):
@@ -1572,7 +1696,7 @@
                 space + [pltpu.VMEM(chunk, BF)] * 2 + sems + [dma(dp_count)] * 2,
                 *args, (rows, l - 1), (cols, l - 1), b["gates"], heads_grad,
             )
-            back, b["gw_in"], b["gw_out"] = expert_call("bwd", l - 1, 10, dp_count, [send], b["x_rows"], w_in, w_out)
+            back, b["gw_in"], b["gw_out"] = expert_call("bwd", l - 1, 10, dp_count, send, None, b["x_rows"], w_in, w_out)
         else:
             (parts,) = got[3:]
 

time: 782 us -> 712 us (0.910)
  Pallas kernels: 759 us -> 685 us
    pallas_call x8 -> x4, Pallas kernels: 283 us -> 193 us  [mp_call(): pl.pallas_call(kernel, grid=(1,), out_shape=tuple((jax.ShapeDtypeStruct(s...]
    pallas_call x2, Pallas kernels: 46.4 us -> 108 us  [pre_call(): pl.pallas_call(functools.partial(pre_kernel, layer, layers, heads, size),...]
    pallas_call x3, Pallas kernels: 334 us -> 289 us  [expert_call(): pl.pallas_call(functools.partial(expert_kernel, mode, layer, dp_count), o...]
where the time goes in v3:
time: 712 us; the launch traced here: 703 us
  Pallas kernels  685 us (96%)
  local copies, waits for them, and re-layouts  15.2 us (2%)
    pallas_call x3, Pallas kernels, expert_call(): pl.pallas_call(functools.partial(expert_kernel, mode, layer, dp_count), o...  289 us
    pallas_call x4, Pallas kernels, mp_call(): pl.pallas_call(kernel, grid=(1,), out_shape=tuple((jax.ShapeDtypeStruct(s...  193 us
    pallas_call x2, Pallas kernels, pre_call(): pl.pallas_call(functools.partial(pre_kernel, layer, layers, heads, size),...  108 us
    pallas_call x2, Pallas kernels, attn_bwd(): pl.pallas_call(functools.partial(attn_bwd_kernel, heads, size, extra), gr...  78 us
    pallas_call x1, Pallas kernels, spread_call(): pl.pallas_call(functools.partial(spread_kernel, own, layers), grid=(steps...  16.6 us

profile of v3, /device:TPU:17, one launch (start us, length us, event | category | flops | bytes accessed | tf_op | source)
XLA Modules:
  0.0 703.4 jit_solution(6188476801571453518)
XLA Ops:
  1.4 1.3 broadcast_in_dim.75.refs_1_.gain
  2.7 1.3 broadcast_in_dim.81.refs_5_.refs_8_
  3.9 0.7 copy.90
  4.7 0.7 fusion.35
  6.5 1.7 copy.73.refs_6_.refs_7_
  8.3 0.8 fusion.36
  9.1 0.7 copy.74.refs_7_.refs_11_.rows
  9.8 44.6 %shard_map.213 = (bf16[4,384,768]{2,1,0:T(8,128)(2,1)}, bf16[1536,576]{1,0:T(8,128)(2,1)}, bf16[1536,192]{1,0:T(8,128)(2,1)}, f32[3,1536]{1,0:T(4,128)}, f32[384...) custom-call(s32[1,8]{1,0:T(1,128)} %lens.3, ...), custom_call_target="tpu_custom_call" | custom-call | tf_op jit(solution)/shard_map/pallas_call | solution.py:1044
  54.4 80.8 %shard_map.214 = (bf16[16,16,2688]{2,1,0:T(8,128)(2,1)}, bf16[8,224,768]{2,1,0:T(8,128)(2,1)}) custom-call(bf16[16,16,2688]{2,1,0:T(8,128)(2,1)} %get-tuple-element.69.refs_0_, bf16[2,2,768,768]{3,2,1,0:T(8,128)(2,1)} %refs_2_.7, bf16[2,2,768,768]{3,2,1,0:T(8,128)(2,1)} %refs_3_.3), custom_call_target="tpu_custom_call" | custom-call | tf_op jit(solution)/shard_map/pallas_call | solution.py:1548
  135.2 63.9 %shard_map.215 = (f32[384,768]{1,0:T(8,128)}, bf16[4,384,768]{2,1,0:T(8,128)(2,1)}, bf16[1536,576]{1,0:T(8,128)(2,1)}, bf16[1536,192]{1,0:T(8,128)(2,1)}, f32[3,...) custom-call(s32[1,8]{1,0:T(1,128)} %lens.3, ...), custom_call_target="tpu_custom_call" | custom-call | tf_op jit(solution)/shard_map/pallas_call | solution.py:1044
  199.1 122.2 %shard_map.216 = (bf16[16,16,2688]{2,1,0:T(8,128)(2,1)}, bf16[16,16,2688]{2,1,0:T(8,128)(2,1)}, f32[2,768,768]{2,1,0:T(8,128)}, f32[2,768,768]{2,1,0:T(8,128)}) custom-call(bf16[16,16,2816]{2,1,0:T(8,128)(2,1)} %get-tuple-element.73.refs_0_, bf16[16,16,2688]{2,1,0:T(8,128)(2,1)} %get-tuple-element.72.refs_13_.refs_1_, ...), custom_call_target="tpu_custom_call" | custom-call | tf_op jit(solution)/shard_map/pallas_call | solution.py:1548
  321.3 28.0 %shard_map.217 = (f32[384,768]{1,0:T(8,128)}, bf16[4,384,768]{2,1,0:T(8,128)(2,1)}, f32[1,768]{1,0:T(1,128)}, f32[16,768]{1,0:T(8,128)}, bf16[384,768]{1,0:T(8,128)(2,1)}) custom-call(bf16[16,16,2688]{2,1,0:T(8,128)(2,1)} %get-tuple-element.75.refs_0_, bf16[16,16,2688]{2,1,0:T(8,128)(2,1)} %get-tuple-element.76.refs_1_, bf16[384,768]{1,0:T(8,128)(2,1)} %bitcast.37, ...), custom_call_target="tpu_custom_call" | custom-call | tf_op jit(solution)/shard_map/pallas_call | solution.py:1215
  349.3 37.8 %shard_map.218 = (bf16[1536,576]{1,0:T(8,128)(2,1)}, f32[768,768]{1,0:T(8,128)}, f32[3,1408]{1,0:T(4,128)}, f32[2,2,768,768]{3,2,1,0:T(8,128)}, f32[2,2,768,768]{3,2,1,0:T(8,128)}) custom-call(s32[1,8]{1,0:T(1,128)} %lens.3, bf16[1536,576]{1,0:T(8,128)(2,1)} %get-tuple-element.83.qkv, bf16[1536,768]{1,0:T(8,128)(2,1)} %bitcast.34, ...), custom_call_target="tpu_custom_call" | custom-call | tf_op jit(solution)/shard_map/pallas_call | solution.py:620
  387.1 35.2 %shard_map.219 = (f32[384,768]{1,0:T(8,128)}, f32[1,768]{1,0:T(1,128)}, bf16[16,16,2688]{2,1,0:T(8,128)(2,1)}, bf16[96,768]{1,0:T(8,128)(2,1)}) custom-call(bf16[4,384,576]{2,1,0:T(8,128)(2,1)} %bitcast.42, bf16[2,768,2304]{2,1,0:T(8,128)(2,1)} %w_qkv.3, f32[384,768]{1,0:T(8,128)} %get-tuple-element.91.stream, f32[2,1,768]{2,1,0:T(1,128)} %broadcast_in_dim.75.refs_1_.gain, ...), custom_call_target="tpu_custom_call" | custom-call | tf_op jit(solution)/shard_map/pallas_call | solution.py:1215
  422.4 85.8 %shard_map.220 = (bf16[16,16,2688]{2,1,0:T(8,128)(2,1)}, f32[2,768,768]{2,1,0:T(8,128)}, f32[2,768,768]{2,1,0:T(8,128)}) custom-call(bf16[16,16,2688]{2,1,0:T(8,128)(2,1)} %get-tuple-element.94.refs_0_, bf16[8,224,768]{2,1,0:T(8,128)(2,1)} %get-tuple-element.95.refs_1_, bf16[2,2,768,768]{3,2,1,0:T(8,128)(2,1)} %refs_2_.7, bf16[2,2,768,768]{3,2,1,0:T(8,128)(2,1)} %refs_3_.3), custom_call_target="tpu_custom_call" | custom-call | tf_op jit(solution)/shard_map/pallas_call | solution.py:1548
  508.2 38.5 %shard_map.221 = (f32[384,768]{1,0:T(8,128)}, bf16[4,384,768]{2,1,0:T(8,128)(2,1)}, f32[1,768]{1,0:T(1,128)}, f32[16,768]{1,0:T(8,128)}, bf16[8,96,768]{2,1,0:T(8,128)(2,1)}) custom-call(bf16[16,16,2688]{2,1,0:T(8,128)(2,1)} %get-tuple-element.96.refs_0_, bf16[16,16,2688]{2,1,0:T(8,128)(2,1)} %get-tuple-element.70.refs_10_.refs_1_, ...), custom_call_target="tpu_custom_call" | custom-call | tf_op jit(solution)/shard_map/pallas_call | solution.py:1215
  546.8 40.2 %shard_map.222 = (bf16[1536,576]{1,0:T(8,128)(2,1)}, f32[768,768]{1,0:T(8,128)}, f32[3,1408]{1,0:T(4,128)}, bf16[4,8,96,768]{3,2,1,0:T(8,128)(2,1)}) custom-call(s32[1,8]{1,0:T(1,128)} %lens.3, bf16[1536,576]{1,0:T(8,128)(2,1)} %get-tuple-element.81.qkv, bf16[1536,768]{1,0:T(8,128)(2,1)} %bitcast.38, bf16[1536,768]{1,0:T(8,128)(2,1)} %bitcast.39, ...), custom_call_target="tpu_custom_call" | custom-call | tf_op jit(solution)/shard_map/pallas_call | solution.py:620
  587.0 0.9 select_reduce_fusion.1
  588.4 0.7 pad_bitcast_fusion.small
  589.1 91.5 %shard_map.223 = (f32[384,768]{1,0:T(8,128)}, bf16[4,8,96,768]{3,2,1,0:T(8,128)(2,1)}, f32[8,8,768]{2,1,0:T(8,128)}) custom-call(bf16[4,384,576]{2,1,0:T(8,128)(2,1)} %bitcast.43, bf16[2,768,2304]{2,1,0:T(8,128)(2,1)} %w_qkv.3, bf16[384,768]{1,0:T(8,128)(2,1)} %bitcast.41, f32[2,1,768]{2,1,0:T(1,128)} %broadcast_in_dim.75.refs_1_.gain, ...), custom_call_target="tpu_custom_call" | custom-call | tf_op jit(solution)/shard_map/pallas_call | solution.py:1215
  680.6 0.9 slice.26
  684.1 16.6 %shard_map.224 = (f32[2,768,2304]{2,1,0:T(8,128)}, f32[2,768,768]{2,1,0:T(8,128)}, f32[2,2,768,768]{3,2,1,0:T(8,128)}, f32[2,2,768,768]{3,2,1,0:T(8,128)}) custom-call(bf16[4,8,96,768]{3,2,1,0:T(8,128)(2,1)} %get-tuple-element.115.refs_0_, bf16[4,8,96,768]{3,2,1,0:T(8,128)(2,1)} %get-tuple-element.116.refs_1_, ...), custom_call_target="tpu_custom_call", output_to_operand_aliasing={{2}: (4, {}), {3}: (5, {})} | custom-call | tf_op jit(solution)/shard_map/pallas_call | solution.py:1585
  700.8 0.8 copy.99
  702.2 1.0 copy.100
  (47 shorter events, 5.5 us)
Async XLA Ops:
  0.6 0.7 copy-start
  546.7 40.2 %copy-start.6 = (f32[3,1408]{1,0:T(4,128)S(1)}, f32[3,1408]{1,0:T(4,128)}, u32[]{:S(2)}) copy-start(f32[3,1408]{1,0:T(4,128)} %get-tuple-element.112) | copy-start | bytes 50692
  546.7 41.6 %copy-start.4 = (f32[16,768]{1,0:T(8,128)S(1)}, f32[16,768]{1,0:T(8,128)}, u32[]{:S(2)}) copy-start(f32[16,768]{1,0:T(8,128)} %get-tuple-element.113) | copy-start | bytes 147460
  546.7 41.6 %copy-start.5 = (f32[16,768]{1,0:T(8,128)S(1)}, f32[16,768]{1,0:T(8,128)}, u32[]{:S(2)}) copy-start(f32[16,768]{1,0:T(8,128)} %get-tuple-element.109) | copy-start | bytes 147460
  546.8 41.6 %copy-start.7 = (f32[1,768]{1,0:T(1,128)S(1)}, f32[1,768]{1,0:T(1,128)}, u32[]{:S(2)}) copy-start(f32[1,768]{1,0:T(1,128)} %get-tuple-element.111) | copy-start | bytes 9220
  546.8 41.6 %copy-start.8 = (f32[1,768]{1,0:T(1,128)S(1)}, f32[1,768]{1,0:T(1,128)}, u32[]{:S(2)}) copy-start(f32[1,768]{1,0:T(1,128)} %get-tuple-element.110) | copy-start | bytes 9220
  546.8 41.6 %copy-start.9 = (f32[1,768]{1,0:T(1,128)S(1)}, f32[1,768]{1,0:T(1,128)}, u32[]{:S(2)}) copy-start(f32[1,768]{1,0:T(1,128)} %get-tuple-element.107) | copy-start | bytes 9220
  684.1 16.6 %copy-start.3 = (bf16[384,768]{1,0:T(8,128)(2,1)S(1)}, bf16[384,768]{1,0:T(8,128)(2,1)}, u32[]{:S(2)}) copy-start(bf16[384,768]{1,0:T(8,128)(2,1)} %get-tuple-element.80) | copy-start | bytes 1769476
  684.1 19.1 %copy-start.1 = (f32[2,12,32]{2,0,1:T(2,128)S(1)}, f32[2,12,32]{2,0,1:T(2,128)}, u32[]{:S(2)}) copy-start(f32[2,12,32]{2,0,1:T(2,128)} %param.19) | copy-start | bytes 9220
  700.8 1.5 copy-start.2

commit v4 on v3

--- a/solution.py
+++ b/solution.py
@@ -419,7 +419,7 @@
 
 def layer_spec(array, layer):
     zeros = (0,) * (array.ndim - 1)
-    return pl.BlockSpec((None,) + array.shape[1:], lambda i: (layer,) + zeros)
+    return pl.BlockSpec((None,) + array.shape[1:], lambda i: (layer,) + zeros, pipeline_mode=pl.Buffered(1))
 
 
 def segments(lens, shape, dim):
@@ -480,176 +480,6 @@
     return [(0, PROMPT, first), (k0, k1, second)]
 
 
-def attn_bwd_kernel(heads, size, extra, lens, qkv, normed, branch, w_attn, mixed, lse, vecs, *refs):
-    refs = list(refs)
-    if extra == "copy":
-        sources, refs = refs[:2], refs[2:]
-    elif extra == "share":
-        shared, refs = refs[0], refs[1:]
-    dqkv_o, gw_o, dvec_o = refs[:3]
-    refs = refs[3:]
-    if extra == "copy":
-        targets, refs = refs[:2], refs[2:]
-    elif extra == "share":
-        all_o, refs = refs[0], refs[1:]
-    q_s, k_s, v_s, kt_s, do_s, table, cont_bias, fold, dtable, dk_s, dv_s, dqt, dk_all, dv_all, segc = refs[:15]
-    refs = refs[15:]
-    me, core, mate, across, diagonal = mp_places()
-    if extra == "copy":
-        spaces, sems = refs[:2], refs[2]
-        takes = [pltpu.make_async_copy(sources[n], spaces[n], sems.at[n]) for n in range(2)]
-        puts = [pltpu.make_async_copy(spaces[n], targets[n].at[targets[n].shape[0] - 1], sems.at[2 + n]) for n in range(2)]
-        for copy in takes:
-            copy.start()
-    elif extra == "share":
-        held, ssem, rsem = refs
-        greet_mp(2)
-        held[me] = shared[...]
-        to_mate = remote(held.at[me], held.at[me], ssem.at[0], rsem.at[0], mp=mate)
-        over = remote(held.at[me], held.at[me], ssem.at[1], rsem.at[1], mp=across)
-        passed = remote(held.at[across], held.at[across], ssem.at[2], rsem.at[2], mp=mate)
-        over.start()
-        to_mate.start()
-
-    seq, model = normed.shape
-    own = heads * size
-    cont = seq - PROMPT
-    own_rows = pl.ds(pl.multiple_of(me * own, size), own)
-    for i in range(seq // QB):
-        rows = pl.ds(i * QB, QB)
-        part = qkv[rows, :]
-        dmix = nt(branch[rows, :], w_attn[own_rows, :]).astype(BF)
-        for h in range(heads):
-            q_s[h, rows, :] = part[:, h * size : (h + 1) * size] * BF(0.125)
-            key = part[:, own + h * size : own + (h + 1) * size]
-            k_s[h, rows, :] = key
-            kt_s[h, :, rows] = (key.astype(F32) * 0.125).T.astype(BF)
-            v_s[h, rows, :] = part[:, 2 * own + h * size : 2 * own + (h + 1) * size]
-            do_s[h, rows, :] = dmix[:, h * size : (h + 1) * size]
-    seg_row, _ = segments(lens, (1, cont), 1)
-    segc[...] = segments(lens, (cont, LANES), 0)[0]
-    _, offset = segments(lens, (cont, LANES), 0)
-    unplace = (lax.broadcasted_iota(jnp.int32, (cont, LANES), 1) == offset).astype(BF)
-    width = vecs.shape[1]
-
-    def head(h, carry):
-        bias_stage(vecs[pl.ds(h, 1), :], lens, table, cont_bias)
-        dtable[...] = jnp.zeros_like(dtable)
-        dk_s[...] = jnp.zeros_like(dk_s)
-        dv_s[...] = jnp.zeros_like(dv_s)
-        for block in blocks_of(seq):
-            q0, prompt_keys, cont_from = block
-            query = q_s[h, q0 : q0 + QB, :]
-            dout = do_s[h, q0 : q0 + QB, :]
-            parts = scores_of(k_s, query, table, cont_bias, segc, seg_row, block, h)
-            lse_row = lse[pl.ds(h, 1), q0 : q0 + QB]
-            kept, delta = [], 0.0
-            for k0, k1, s in parts:
-                p = jnp.exp(s - lse_row)
-                dp = nt(v_s[h, k0:k1, :], dout)
-                delta = delta + jnp.sum(p * dp, axis=0, keepdims=True)
-                dv_s[k0:k1, :] += nn(p.astype(BF), dout)
-                kept.append((k0, k1, p, dp))
-            dq = 0.0
-            for k0, k1, p, dp in kept:
-                ds = p * (dp - delta)
-                dsb = ds.astype(BF)
-                dk_s[k0:k1, :] += nn(dsb, query)
-                dq = dq + nn(kt_s[h, :, k0:k1], dsb)
-                if cont_from is not None and k0 == 0:
-                    fold[:, q0 - PROMPT : q0 - PROMPT + QB] = dsb
-                else:
-                    left = PROMPT - q0 if cont_from is None else PROMPT + cont_from - (q0 - PROMPT)
-                    dtable[left : left + k1 - k0, :] += ds[:, 0:LANES]
-                    dtable[left - LANES : left - LANES + k1 - k0, :] += ds[:, LANES:]
-            dqt[pl.ds(pl.multiple_of(h * size, size), size), q0 : q0 + QB] = dq
-        dk_all[h] = dk_s[...].astype(BF)
-        dv_all[h] = dv_s[...].astype(BF)
-        dtable[0:PROMPT, :] += nn(fold[...], unplace)
-        flat = dtable[...].T
-        flat = jnp.concatenate([flat, jnp.zeros((LANES, LANES), F32)], 1)
-        rows = lax.broadcasted_iota(jnp.int32, (LANES, width), 0)
-        for bit in range(7):
-            flat = jnp.where((rows >> bit) % 2 == 1, pltpu.roll(flat, width - (1 << bit), 1), flat)
-        dvec_o[pl.ds(h, 1), :] = jnp.sum(flat, axis=0, keepdims=True)
-        return carry
-
-    lax.fori_loop(0, heads, head, 0)
-    if extra == "copy":
-        for n in range(2):
-            takes[n].wait()
-            puts[n].start()
-    elif extra == "share":
-        over.wait_recv()
-        passed.start()
-    for i in range(seq // QB):
-        rows = pl.ds(i * QB, QB)
-        pieces = [dqt[:, i * QB : (i + 1) * QB].T.astype(BF)]
-        pieces += [dk_all[h, rows, :] for h in range(heads)] + [dv_all[h, rows, :] for h in range(heads)]
-        dqkv_o[rows, :] = jnp.concatenate(pieces, 1)
-    half = normed.shape[1] // 2
-    for i in range(2):
-        cols = slice(i * half, (i + 1) * half)
-        gw_o[cols, 0 : 3 * own] = tn(normed[:, cols], dqkv_o[...])
-        gw_o[cols, 3 * own :] = tn(branch[:, cols], mixed[...])
-    if extra == "copy":
-        for copy in puts:
-            copy.wait()
-    elif extra == "share":
-        to_mate.wait()
-        over.wait_send()
-        passed.wait()
-        all_o[...] = held[...]
-
-
-def attn_bwd(lens, qkv, normed, branch, w_attn, layer, mixed, lse, vecs, heads, size, extra=None, more=(), number=None):
-    seq, model = normed.shape
-    own = heads * size
-    width = vecs.shape[1]
-    cont = seq - PROMPT
-    params = pltpu.CompilerParams(vmem_limit_bytes=VMEM_BYTES)
-    outs, scratch, in_spec = (), [], VMEM
-    if extra == "copy":
-        outs = tuple(jax.ShapeDtypeStruct((w_attn.shape[0],) + g.shape, F32) for g in more)
-        scratch, in_spec = [pltpu.VMEM(g.shape, F32) for g in more] + [pltpu.SemaphoreType.DMA((4,))], ANY
-    elif extra == "share":
-        shape = (4,) + more[0].shape
-        outs = (jax.ShapeDtypeStruct(shape, BF),)
-        scratch = [pltpu.VMEM(shape, BF), pltpu.SemaphoreType.DMA((3,)), pltpu.SemaphoreType.DMA((3,))]
-        params = pltpu.CompilerParams(collective_id=number, has_side_effects=True, vmem_limit_bytes=VMEM_BYTES)
-    return pl.pallas_call(
-        functools.partial(attn_bwd_kernel, heads, size, extra),
-        grid=(1,),
-        out_shape=(
-            jax.ShapeDtypeStruct((seq, 3 * own), BF),
-            jax.ShapeDtypeStruct((model, 4 * own), F32),
-            jax.ShapeDtypeStruct((heads, width), F32),
-        )
-        + outs,
-        in_specs=[SMEM] + [VMEM] * 3 + [layer_spec(w_attn, layer)] + [VMEM] * 3 + [in_spec] * len(more),
-        out_specs=(VMEM, VMEM, VMEM) + (in_spec,) * len(outs),
-        scratch_shapes=[
-            pltpu.VMEM((heads, seq, size), BF),
-            pltpu.VMEM((heads, seq, size), BF),
-            pltpu.VMEM((heads, seq, size), BF),
-            pltpu.VMEM((heads, size, seq), BF),
-            pltpu.VMEM((heads, seq, size), BF),
-            pltpu.VMEM((width - LANES, LANES), F32),
-            pltpu.VMEM((PROMPT, cont), F32),
-            pltpu.VMEM((PROMPT, cont), BF),
-            pltpu.VMEM((width - LANES, LANES), F32),
-            pltpu.VMEM((seq, size), F32),
-            pltpu.VMEM((seq, size), F32),
-            pltpu.VMEM((own, seq), F32),
-            pltpu.VMEM((heads, seq, size), BF),
-            pltpu.VMEM((heads, seq, size), BF),
-            pltpu.VMEM((cont, LANES), jnp.int32),
-        ]
-        + scratch,
-        compiler_params=params,
-    )(lens, qkv, normed, branch, w_attn, mixed, lse, vecs, *more)
-
-
 def diagonals():
     width = PROMPT + 3 * LANES
     at = jnp.arange(width, dtype=jnp.int32)
@@ -663,12 +493,6 @@
     hot = bucket_of(distance)[None, :] == jnp.arange(bias.shape[-1], dtype=jnp.int32)[:, None]
     picked = jnp.sum(jnp.where(hot, bias[..., :, None], 0.0), axis=-2)
     return jnp.where(valid, picked, -1e30)
-
-
-def bias_grads(dvecs, buckets):
-    _, distance, valid = diagonals()
-    hot = (bucket_of(distance)[None, :] == jnp.arange(buckets, dtype=jnp.int32)[:, None]) & valid[None, :]
-    return jnp.sum(jnp.where(hot, dvecs[..., None, :], 0.0), axis=-1)
 
 
 def scatter_rows(rows, values, send):
@@ -756,32 +580,6 @@
     )
 
 
-def gather_mp(held, ssem, rsem):
-    me, core, mate, across, diagonal = mp_places()
-    to_mate = remote(held.at[me], held.at[me], ssem.at[0], rsem.at[0], mp=mate)
-    over = remote(held.at[me], held.at[me], ssem.at[1], rsem.at[1], mp=across)
-    over.start()
-    to_mate.start()
-    over.wait_recv()
-    passed = remote(held.at[across], held.at[across], ssem.at[2], rsem.at[2], mp=mate)
-    passed.start()
-    to_mate.wait_recv()
-    passed.wait_recv()
-    for copy in (to_mate, over, passed):
-        copy.wait_send()
-
-
-def swap_mp(out, held, ssem, rsem, lsem):
-    me, core, mate, across, diagonal = mp_places()
-    copies = [
-        remote(out.at[to], held.at[me], ssem.at[n], rsem.at[n], mp=to) for n, to in enumerate((diagonal, across, mate))
-    ]
-    copies.append(pltpu.make_async_copy(out.at[me], held.at[me], lsem))
-    for copy in copies:
-        copy.start()
-    return copies
-
-
 def greet_mp(count, dp_count=1):
     me, core, mate, across, diagonal = mp_places()
     d = lax.axis_index("dp")
@@ -845,16 +643,17 @@
         tokens, cotangent, far_rows = take(3)
     else:
         before, returned, cols_in, gates_in = take(4)
-    (g_in,) = take(1) if last else (None,)
+    g_in, g_half = take(2) if last else (None, None)
     (stream_o,) = (None,) if first else take(1)
     normed_o, qkv_o, mixed_o, lse_o, middle_o, ffn_o, gates_o, send_o = take(8)
     (g_o,) = take(1) if first or last else (None,)
+    (g_half_o,) = take(1) if first else (None,)
     held, hssem, hrsem = take(3)
     weight, q_s, k_s, vt_s, table, cont_bias, mixt, segc, out_s, mixed_s, mssem, mrsem = take(12)
     if first:
         g_send, g_held, gssem, grsem = take(4)
-    elif last:
-        g_held, gssem, grsem = take(3)
+    if first or last:
+        g_over, gfsem, gbsem = take(3)
     me, core, mate, across, diagonal = mp_places()
     d = lax.axis_index("dp")
     dp_count = lax.axis_size("dp")
@@ -878,7 +677,7 @@
         for j in range(2):
             stream = stream + gates_in[:, j : j + 1] * gather_rows(cols_in, j, returned)
         stream_o[...] = stream
-    held[me] = (stream * mean_square_scale(stream) * gain_a[...]).astype(BF)
+    held[me] = (stream * mean_square_scale(stream) * gain_a[layer : layer + 1, :]).astype(BF)
     pl.semaphore_wait(barrier, count)
     over = remote(held.at[me], held.at[me], hssem.at[1], hrsem.at[1], mp=across)
     to_mate = remote(held.at[me], held.at[me], hssem.at[0], hrsem.at[0], mp=mate)
@@ -886,20 +685,34 @@
     over.start()
     to_mate.start()
 
-    extras = []
+    index = d * 2 + core
+
+    def far_copy(k):
+        dd, cc = lax.rem(d + k // 2, dp_count), lax.rem(core + k % 2, 2)
+        if k == 0:
+            return pltpu.make_async_copy(g_send.at[index], g_held.at[index], grsem.at[0])
+        return remote(g_send.at[dd * 2 + cc], g_held.at[index], gssem.at[k], grsem.at[k], dp=dd, mp=(me // 2) * 2 + cc)
+
+    def far_over(source, n):
+        two = pl.ds(lax.rem(d + dp_count - n, dp_count) * 2, 2)
+        return remote(source.at[two], g_over.at[two], gfsem.at[n], gbsem.at[n], mp=across)
+
+    def far_wave(n):
+        if n < dp_count:
+            far_copy(2 * n).start()
+            far_copy(2 * n + 1).start()
+
+    def far_arrived(n):
+        far_copy(2 * n).wait() if n == 0 else far_copy(2 * n).wait_recv()
+        far_copy(2 * n + 1).wait_recv()
+
     if first:
         scatter_rows(far_rows, [cotangent[...]], g_send)
-        index = d * 2 + core
-        extras.append(pltpu.make_async_copy(g_send.at[index], g_held.at[index], grsem.at[0]))
-        for k in range(1, 2 * dp_count):
-            dd, cc = lax.rem(d + k // 2, dp_count), lax.rem(core + k % 2, 2)
-            extras.append(
-                remote(g_send.at[dd * 2 + cc], g_held.at[index], gssem.at[k], grsem.at[k], dp=dd, mp=(me // 2) * 2 + cc)
-            )
+        for n in range(dp_count):
+            far_wave(n)
     elif last:
-        extras.append(remote(g_in, g_held, gssem, grsem, mp=across))
-    for copy in extras:
-        copy.start()
+        for n in range(2, dp_count):
+            far_over(g_in, n).start()
 
     for m in range(model // own):
 
@@ -938,8 +751,12 @@
     def handed(n):
         return remote(out_s.at[n], mixed_s.at[me, n % parts], mssem.at[n], mrsem.at[me, n % parts], mp=n // parts)
 
-    for block in blocks_of(seq):
+    early = {1: 0, 3: 1}
+    for number, block in enumerate(blocks_of(seq)):
         q0 = block[0]
+        if first and number in early:
+            far_arrived(early[number])
+            far_over(g_held, early[number]).start()
 
         def head(h, carry):
             query = q_s[h, q0 : q0 + QB, :]
@@ -976,7 +793,7 @@
             pltpu.make_async_copy(mixed_s.at[m, n], mixed_s.at[m, n], mrsem.at[m, n]).wait()
         middle = middle + nn(mixed_s[m].reshape(local, own), w_attn[m * own : (m + 1) * own, :])
     middle_o[...] = middle
-    ffn = (middle * mean_square_scale(middle) * gain_f[...]).astype(BF)
+    ffn = (middle * mean_square_scale(middle) * gain_f[layer : layer + 1, :]).astype(BF)
     ffn_o[...] = ffn
     logits = nn(ffn, router[...])
     expert = lax.broadcasted_iota(jnp.int32, logits.shape, 1)
@@ -990,14 +807,24 @@
     scatter_rows(rows, [ffn], send_o)
     if last:
         scatter_gates(rows, gates, send_o, 7 * model // 2)
-    if first or last:
-        for copy in extras:
-            if first and copy is extras[0]:
-                copy.wait()
-            else:
-                copy.wait_send()
-                copy.wait_recv()
+    if first:
+        for n in range(2, dp_count):
+            far_arrived(n)
         g_o[...] = g_held[...]
+        for k in range(1, 2 * dp_count):
+            far_copy(k).wait_send()
+        for n in range(2):
+            far_over(g_held, n).wait()
+            two = pl.ds(lax.rem(d + dp_count - n, dp_count) * 2, 2)
+            g_half_o[two] = g_over[two]
+    elif last:
+        for n in range(2):
+            two = pl.ds(lax.rem(d + dp_count - n, dp_count) * 2, 2)
+            g_o[two] = g_half[two]
+        for n in range(2, dp_count):
+            far_over(g_in, n).wait()
+            two = pl.ds(lax.rem(d + dp_count - n, dp_count) * 2, 2)
+            g_o[two] = g_over[two]
     for copy in (to_mate, over, passed):
         copy.wait_send()
     for n in range(seq // LANES):
@@ -1021,6 +848,8 @@
         ((local, model), F32), ((local, model), BF), ((local, 2), F32), (send, BF),
     ]
     if first or last:
+        outs.append((narrow, BF))
+    if first:
         outs.append((narrow, BF))
     scratch = [
         pltpu.VMEM((mp_count, local, model), BF), dma(3), dma(3),
@@ -1039,8 +868,8 @@
     ]
     if first:
         scratch += [pltpu.VMEM(narrow, BF), pltpu.VMEM(narrow, BF), dma(2 * dp_count), dma(2 * dp_count)]
-    elif last:
-        scratch += [pltpu.VMEM(narrow, BF), dma(), dma()]
+    if first or last:
+        scratch += [pltpu.VMEM(narrow, BF), dma(dp_count), dma(dp_count)]
     return pl.pallas_call(
         functools.partial(pre_kernel, layer, layers, heads, size),
         grid=(1,),
@@ -1054,28 +883,73 @@
     )(lens, *[a[0] if isinstance(a, tuple) else a for a in args])
 
 
-def post_kernel(with_output, *refs):
-    if with_output:
-        (back, returned, flow_in, middle, ffn, gates, cols, router, gain, grad_o, all_o, gain_o, router_o, out_o, held, ssem, rsem) = refs
-        greet_mp(2)
+def shift_table(flat, width):
+    rows = lax.broadcasted_iota(jnp.int32, flat.shape, 0)
+    for bit in range(7):
+        flat = jnp.where((rows >> bit) % 2 == 1, pltpu.roll(flat, width - (1 << bit), 1), flat)
+    return jnp.sum(flat, axis=0, keepdims=True)
+
+
+def back_kernel(layer, layers, heads, size, buckets, *refs):
+    refs = list(refs)
+
+    def take(count):
+        taken = refs[:count]
+        del refs[:count]
+        return taken
+
+    first, last = layer == 0, layer == layers - 1
+    lens, vecs, back, returned, flow_in, middle, ffn, gates, cols, router, gain_f = take(11)
+    normed, qkv, mixed, lse, w_attn, w_qkv, stream, gain_a = take(8)
+    if first:
+        above, small_above = take(2)
     else:
-        (back, returned, flow_in, middle, ffn, gates, cols, router, gain, shared, grad_o, all_o, gain_o, router_o, share_o, held, ssem, rsem, round_s, dssem, drsem) = refs
-        greet_mp(2, dp_count=round_s.shape[0])
-        d = lax.axis_index("dp")
-        round_s[d] = shared[...]
-        shares = share_dp(round_s, dssem, drsem)
-        for copy in shares:
-            copy.start()
-    me = lax.axis_index("mp")
+        rows_below, cols_below, gates_below = take(3)
+    (flow_o,) = take(1)
+    if first:
+        up_o, all_o, small_o = take(3)
+    else:
+        out_o, send_o, sum_o, small_o = take(4)
+    held, hssem, hrsem = take(3)
+    normed_t, q_s, k_s, v_s, kt_s, do_s, table, cont_bias, fold, dtable, dk_s, dv_s, dqt, segc, hot, bias_s, gw_a, router_s = take(18)
+    dq_s, dq_held, qssem, qrsem, part, come, pssem, prsem = take(8)
+    if first:
+        small_s, small_come, small_mp, tsem, usem, csem, dsem, vsem, zsem = take(9)
+        assem, arsem, ossem, orsem = take(4)
+        ussem, ursem, wssem, wrsem = take(4)
+    me, core, mate, across, diagonal = mp_places()
+    d = lax.axis_index("dp")
+    dp_count = part.shape[0]
+    local, model = middle.shape
+    seq, own = mixed.shape
+    cont = seq - PROMPT
+    width = vecs.shape[1]
+    places = mixed.shape[0] // local
+
+    def dp_share(held_all, ssem, rsem, k):
+        return remote(held_all.at[me, d], held_all.at[me, d], ssem.at[k], rsem.at[k], dp=lax.rem(d + k, dp_count), mp=me)
+
+    def mp_share(held_all, ssem, rsem, n, j):
+        whose = across if n == 2 else me
+        return remote(
+            held_all.at[whose, j], held_all.at[whose, j], ssem.at[n, j], rsem.at[n, j], mp=across if n == 1 else mate
+        )
+
+    greet_mp(3, dp_count=dp_count)
+    if first:
+        up_o[me, d] = above[...]
+        for k in range(1, dp_count - 2):
+            dp_share(up_o, ussem, ursem, k).start()
+
     flow = flow_in[...].astype(F32)
     outs = [gather_rows(cols, j, returned) for j in range(2)]
     gate = [gates[:, j : j + 1] for j in range(2)]
     keep = [cols[:, 4 + j : 5 + j].astype(F32) for j in range(2)]
-    if with_output:
+    if last:
         out_o[...] = (middle[...] + gate[0] * keep[0] * outs[0] + gate[1] * keep[1] * outs[1]).astype(BF)
     gate_grad = [keep[j] * jnp.sum(flow * outs[j], axis=1, keepdims=True) for j in range(2)]
     shared = gate[0] * gate_grad[0] + gate[1] * gate_grad[1]
-    expert = lax.broadcasted_iota(jnp.int32, (flow.shape[0], router.shape[1]), 1)
+    expert = lax.broadcasted_iota(jnp.int32, (local, router.shape[1]), 1)
     logit_grad = 0.0
     for j in range(2):
         logit_grad = logit_grad + jnp.where(expert == cols[:, j : j + 1], gate[j] * (gate_grad[j] - shared), 0.0)
@@ -1083,137 +957,312 @@
     low = (logit_grad - high.astype(F32)).astype(BF)
     upstream = gather_rows(cols, 0, back) + gather_rows(cols, 1, back)
     upstream = upstream + nt(high, router[...]) + nt(low, router[...])
-    router_o[...] = tn(high, ffn[...]) + tn(low, ffn[...])
-    grad, gain_o[...] = norm_grads(middle[...], gain[...], upstream)
+    grad, gain_f_grad = norm_grads(middle[...], gain_f[layer : layer + 1, :], upstream)
     grad = grad + flow
-    grad_o[...] = grad
+    flow_o[...] = grad
     held[me] = grad.astype(BF)
-    gather_mp(held, ssem, rsem)
-    all_o[...] = held[...]
-    if not with_output:
-        for copy in shares:
-            copy.wait()
-        share_o[...] = round_s[...]
-
-
-def close_layer(held, w_qkv, stream, gain, grad):
-    model = w_qkv.shape[0]
-    own = held.shape[2] // 3
+    to_mate = remote(held.at[me], held.at[me], hssem.at[0], hrsem.at[0], mp=mate)
+    over = remote(held.at[me], held.at[me], hssem.at[1], hrsem.at[1], mp=across)
+    passed = remote(held.at[across], held.at[across], hssem.at[2], hrsem.at[2], mp=mate)
+    over.start()
+    to_mate.start()
+
+    router_s[...] = tn(jnp.concatenate([high, low], 1), ffn[...])
+    for i in range(seq // local):
+        rows = pl.ds(i * local, local)
+        normed_t[:, i * local : (i + 1) * local] = normed[i].astype(F32).T.astype(BF)
+        piece = qkv[rows, :]
+        for h in range(heads):
+            q_s[h, rows, :] = piece[:, h * size : (h + 1) * size] * BF(0.125)
+            key = piece[:, own + h * size : own + (h + 1) * size]
+            k_s[h, rows, :] = key
+            kt_s[h, :, i * local : (i + 1) * local] = (key.astype(F32) * 0.125).T.astype(BF)
+            v_s[h, rows, :] = piece[:, 2 * own + h * size : 2 * own + (h + 1) * size]
+    seg_row, _ = segments(lens, (1, cont), 1)
+    segc[...] = segments(lens, (cont, LANES), 0)[0]
+    _, offset = segments(lens, (cont, LANES), 0)
+    unplace = (lax.broadcasted_iota(jnp.int32, (cont, LANES), 1) == offset).astype(BF)
+    at = lax.broadcasted_iota(jnp.int32, (1, width), 1)
+    distance = jnp.where(at <= PROMPT, PROMPT - at, PROMPT + width - at)
+    bucket = jnp.where((at <= PROMPT) | (at > width - LANES), bucket_of(distance), -1)
+    hot[...] = (lax.broadcasted_iota(jnp.int32, (buckets, width), 0) == bucket).astype(F32)
+    bias_s[...] = jnp.zeros_like(bias_s)
+
+    def receive(m):
+        dmix = nt(held[m], w_attn[pl.ds(pl.multiple_of(me * own, size), own), :]).astype(BF)
+        for h in range(heads):
+            do_s[h, pl.ds(pl.multiple_of(m * local, LANES), local), :] = dmix[:, h * size : (h + 1) * size]
+
+    receive(me)
+    to_mate.wait_recv()
+    receive(mate)
+    over.wait_recv()
+    passed.start()
+    receive(across)
+    passed.wait_recv()
+    receive(diagonal)
+    gw_a[...] = tn(held[...].reshape(seq, model), mixed[...])
+
+    def swap_copy(h, n):
+        to = (mate, across, diagonal)[n]
+        return remote(dq_s.at[h, to], dq_held.at[h, me], qssem.at[h, n], qrsem.at[h, me], mp=to)
+
+    def sum_copy(h, k):
+        to = lax.rem(d + k, dp_count)
+        return remote(part.at[to, h], come.at[d, h], pssem.at[h, k], prsem.at[h, k], dp=to, mp=me)
+
+    def summed(h):
+        total = part[d, h].astype(F32)
+        for k in range(1, dp_count):
+            sum_copy(h, k).wait_recv()
+            total = total + come[lax.rem(d + dp_count - k, dp_count), h].astype(F32)
+        return total.astype(BF)
+
+    def head_share(h, k):
+        place = all_o.at[me, d, h]
+        return remote(place, place, assem.at[h, k], arsem.at[h, k], dp=lax.rem(d + k, dp_count), mp=me)
+
+    def head_pass(n, h, j):
+        place = all_o.at[across if n == 2 else me, j, h]
+        return remote(place, place, ossem.at[n, h, j], orsem.at[n, h, j], mp=across if n == 1 else mate)
+
+    def finish_sum(h):
+        all_o[me, d, h] = summed(h)
+        for k in range(1, dp_count):
+            head_share(h, k).start()
+
+    def hand_on(h):
+        for k in range(dp_count):
+            j = lax.rem(d + dp_count - k, dp_count)
+            if k > 0:
+                head_share(h, k).wait_recv()
+            head_pass(1, h, j).start()
+            head_pass(0, h, j).start()
+
+    def pass_on(h):
+        for k in range(dp_count):
+            j = lax.rem(d + dp_count - k, dp_count)
+            head_pass(1, h, j).wait_recv()
+            head_pass(2, h, j).start()
+
+    def head(h, carry):
+        bias_stage(vecs[pl.ds(h, 1), :], lens, table, cont_bias)
+        dtable[...] = jnp.zeros_like(dtable)
+        dk_s[...] = jnp.zeros_like(dk_s)
+        dv_s[...] = jnp.zeros_like(dv_s)
+        for number, block in enumerate(blocks_of(seq)):
+            q0, prompt_keys, cont_from = block
+            if first:
+
+                @pl.when(h == 0)
+                def _():
+                    for k in ((0,), (1,), (2,), (3,), (4, 5), (6, 7))[number]:
+                        if k > 0:
+                            dp_share(up_o, ussem, ursem, k).wait_recv()
+                        if number == 1:
+                            for later in range(dp_count - 2, dp_count):
+                                dp_share(up_o, ussem, ursem, later).start()
+                        j = lax.rem(d + dp_count - k, dp_count)
+                        mp_share(up_o, wssem, wrsem, 1, j).start()
+                        mp_share(up_o, wssem, wrsem, 0, j).start()
+
+            query = q_s[h, q0 : q0 + QB, :]
+            dout = do_s[h, q0 : q0 + QB, :]
+            scored = scores_of(k_s, query, table, cont_bias, segc, seg_row, block, h)
+            lse_row = lse[pl.ds(h, 1), q0 : q0 + QB]
+            kept, delta = [], 0.0
+            for k0, k1, s in scored:
+                p = jnp.exp(s - lse_row)
+                dp = nt(v_s[h, k0:k1, :], dout)
+                delta = delta + jnp.sum(p * dp, axis=0, keepdims=True)
+                dv_s[k0:k1, :] += nn(p.astype(BF), dout)
+                kept.append((k0, k1, p, dp))
+            dq = 0.0
+            for k0, k1, p, dp in kept:
+                ds = p * (dp - delta)
+                dsb = ds.astype(BF)
+                dk_s[k0:k1, :] += nn(dsb, query)
+                dq = dq + nn(kt_s[h, :, k0:k1], dsb)
+                if cont_from is not None and k0 == 0:
+                    fold[:, q0 - PROMPT : q0 - PROMPT + QB] = dsb
+                else:
+                    left = PROMPT - q0 if cont_from is None else PROMPT + cont_from - (q0 - PROMPT)
+                    dtable[left : left + k1 - k0, :] += ds[:, 0:LANES]
+                    dtable[left - LANES : left - LANES + k1 - k0, :] += ds[:, LANES:]
+            dqt[:, q0 : q0 + QB] = dq
+        for m in range(places):
+            rows = slice(m * local, (m + 1) * local)
+            dq_s[h, m] = jnp.concatenate(
+                [dqt[:, rows].T.astype(BF), dk_s[rows, :].astype(BF), dv_s[rows, :].astype(BF)], 1
+            )
+        for n in (2, 1, 0):
+            swap_copy(h, n).start()
+        pltpu.make_async_copy(dq_s.at[h, me], dq_held.at[h, me], qrsem.at[h, me]).start()
+        grads = nn(normed_t[...], dq_s[h].reshape(seq, 3 * size))
+        for j in range(dp_count):
+            rows = slice(j * part.shape[2], (j + 1) * part.shape[2])
+            part[j, h, :, 0 : 3 * size] = grads[rows, :].astype(BF)
+        for k in range(1, dp_count):
+            sum_copy(h, k).start()
+        dtable[0:PROMPT, :] += nn(fold[...], unplace)
+        flat = jnp.concatenate([dtable[...].T, jnp.zeros((LANES, LANES), F32)], 1)
+        found = jnp.sum(hot[...] * shift_table(flat, width), axis=1, keepdims=True)
+        lane = lax.broadcasted_iota(jnp.int32, bias_s.shape, 1)
+        bias_s[...] += jnp.where(lane == me * heads + h, found, 0.0)
+        if first:
+
+            @pl.when(h == heads - 1)
+            def _():
+                for j in range(dp_count):
+                    mp_share(up_o, wssem, wrsem, 1, j).wait_recv()
+                    mp_share(up_o, wssem, wrsem, 2, j).start()
+
+            @pl.when(h > 0)
+            def _():
+                finish_sum(h - 1)
+
+        return carry
+
+    for j in range(dp_count):
+        rows = slice(j * part.shape[2], (j + 1) * part.shape[2])
+        for h in range(heads):
+            part[j, h, :, 3 * size :] = gw_a[rows, h * size : (h + 1) * size].astype(BF)
+    lax.fori_loop(0, heads, head, 0)
+    if first:
+        hand_on(0)
+    for h in range(heads):
+        for m in range(places):
+            pltpu.make_async_copy(dq_held.at[h, m], dq_held.at[h, m], qrsem.at[h, m]).wait()
     upstream = 0.0
     for t in range(3):
-        piece = jnp.concatenate([held[m, :, t * own : (t + 1) * own] for m in range(held.shape[0])], 1)
+        piece = jnp.concatenate(
+            [dq_held[h, m, :, t * size : (t + 1) * size] for m in range(places) for h in range(heads)], 1
+        )
         upstream = upstream + nt(piece, w_qkv[:, t * model : (t + 1) * model])
-    inner, gain_grad = norm_grads(stream[...].astype(F32), gain[...], upstream)
-    return grad[...] + inner, gain_grad
-
-
-def fill_parts(part, heads):
-    rows = part.shape[1]
-    for j in range(part.shape[0]):
-        part[j] = heads[j * rows : (j + 1) * rows, :].astype(BF)
-
-
-def close_kernel(dqkv, w_qkv, stream, gain, grad, rows, cols, gates, heads, flow_o, gain_o, send_o, sum_o, held, part, come, ssem, rsem, lsem, dssem, drsem):
-    greet_mp(3, dp_count=part.shape[0])
-    swaps = swap_mp(dqkv, held, ssem, rsem, lsem)
-    fill_parts(part, heads)
-    scattered = scatter_dp(part, come, dssem, drsem)
-    for copy in scattered:
-        copy.start()
-    for copy in swaps:
-        copy.wait()
-    flow, gain_o[...] = close_layer(held, w_qkv, stream, gain, grad)
+    inner, gain_a_grad = norm_grads(stream[...].astype(F32), gain_a[layer : layer + 1, :], upstream)
+    flow = flow_o[...] + inner
     flow_o[...] = flow
-    scatter_rows(
-        rows,
-        [(gates[:, j : j + 1] * cols[:, 4 + j : 5 + j].astype(F32) * flow).astype(BF) for j in range(2)],
-        send_o,
-    )
-    sum_o[...] = sum_dp(scattered, part, come).astype(BF)
-    for copy in scattered:
+    gains = jnp.concatenate([gain_a_grad, gain_f_grad, jnp.zeros((6, model), F32)], 0)
+    tiles = [bias_s[8 * i : 8 * i + 8, :] for i in range(buckets // 8)]
+    bias_rows = jnp.concatenate(tiles + [jnp.zeros((8, model - LANES * len(tiles)), F32)], 1)
+    router_grad = router_s[0 : router.shape[1], :] + router_s[router.shape[1] :, :]
+    small = [gains, bias_rows] + [router_grad[8 * i : 8 * i + 8, :] for i in range(router.shape[1] // 8)]
+
+    if not first:
+        scatter_rows(
+            rows_below,
+            [(gates_below[:, j : j + 1] * cols_below[:, 4 + j : 5 + j].astype(F32) * flow).astype(BF) for j in range(2)],
+            send_o,
+        )
+        for n, block in enumerate(small):
+            small_o[n] = block
+        for h in range(heads):
+            sum_o[h] = summed(h)
+    else:
+        for n, block in enumerate(small):
+            small_s[n] = block
+        small_s[len(small) :] = small_above[...]
+        small_scattered = scatter_dp(small_s, small_come, tsem, usem)
+        for copy in small_scattered:
+            copy.start()
+        finish_sum(heads - 1)
+        hand_on(1)
+        small_mp[me] = sum_dp(small_scattered, small_s, small_come)
+        small_swaps = [
+            remote(small_mp.at[me], small_mp.at[me], csem.at[n], dsem.at[n], mp=to) for n, to in enumerate((mate, across, diagonal))
+        ]
+        for copy in small_swaps:
+            copy.start()
+        pass_on(0)
+        for copy in small_swaps:
+            copy.wait_recv()
+        small_o[d] = small_mp[0] + small_mp[1] + small_mp[2] + small_mp[3]
+        small_shares = share_dp(small_o, vsem, zsem)
+        for copy in small_shares:
+            copy.start()
+        for h in range(2, heads):
+            hand_on(h)
+        for h in range(1, heads):
+            pass_on(h)
+        for copy in small_shares:
+            copy.wait_recv()
+        for j in range(dp_count):
+            for n in range(3):
+                if n != 1:
+                    mp_share(up_o, wssem, wrsem, n, j).wait_recv()
+                mp_share(up_o, wssem, wrsem, n, j).wait_send()
+                for h in range(heads):
+                    if n != 1:
+                        head_pass(n, h, j).wait_recv()
+                    head_pass(n, h, j).wait_send()
+        for k in range(1, dp_count):
+            dp_share(up_o, ussem, ursem, k).wait_send()
+            for h in range(heads):
+                head_share(h, k).wait_send()
+        for copy in small_swaps + small_scattered + small_shares:
+            copy.wait_send()
+    for copy in (to_mate, over, passed):
         copy.wait_send()
-
-
-def last_kernel(
-    dqkv, w_qkv, stream, gain, grad, heads, small, flow_o, all_o, small_o,
-    held, part, come, small_s, small_come, small_mp, small_all,
-    ssem, rsem, lsem, dssem, drsem, tsem, usem, csem, dsem, vsem, zsem, esem, fsem, hsem, isem,
-):
-    dp_count = part.shape[0]
-    d = lax.axis_index("dp")
-    me, core, mate, across, diagonal = mp_places()
-    greet_mp(3, dp_count=dp_count)
-    swaps = swap_mp(dqkv, held, ssem, rsem, lsem)
-    fill_parts(part, heads)
-    scattered = scatter_dp(part, come, dssem, drsem)
-    for copy in scattered:
-        copy.start()
-    small_s[...] = small[...]
-    for copy in swaps:
-        copy.wait()
-    flow, gain_grad = close_layer(held, w_qkv, stream, gain, grad)
-    flow_o[...] = flow
-    small_s[0, 0:1, :] = gain_grad
-    small_scattered = scatter_dp(small_s, small_come, tsem, usem)
-    for copy in small_scattered:
-        copy.start()
-    all_o[me, d] = sum_dp(scattered, part, come).astype(BF)
-    shares = [
-        remote(all_o.at[me, d], all_o.at[me, d], esem.at[k], fsem.at[k], dp=lax.rem(d + k, dp_count), mp=me)
-        for k in range(1, dp_count)
+    for h in range(heads):
+        for n in range(3):
+            swap_copy(h, n).wait_send()
+        for k in range(1, dp_count):
+            sum_copy(h, k).wait_send()
+
+
+def back_call(layer, layers, number, heads, size, buckets, lens, normal, mp_count, dp_count, local, model, block, extra):
+    first, last = layer == 0, layer == layers - 1
+    seq, own = local * mp_count, heads * size
+    width = PROMPT + 3 * LANES
+    cont = seq - PROMPT
+    args = list(normal) + list(extra)
+    specs = [SMEM] + [layer_spec(*a) if isinstance(a, tuple) else VMEM for a in args]
+    chunk = (heads, model // dp_count, 4 * size)
+    smalls = dp_count // layers
+    outs = [((local, model), F32)]
+    if first:
+        outs += [((mp_count, dp_count) + chunk, BF), ((mp_count, dp_count) + chunk, BF), ((dp_count, 8, model), F32)]
+    else:
+        outs += [((local, model), BF), (block, BF), (chunk, BF), ((smalls, 8, model), F32)]
+    scratch = [
+        pltpu.VMEM((mp_count, local, model), BF), dma(3), dma(3),
+        pltpu.VMEM((model, seq), BF),
+        pltpu.VMEM((heads, seq, size), BF),
+        pltpu.VMEM((heads, seq, size), BF),
+        pltpu.VMEM((heads, seq, size), BF),
+        pltpu.VMEM((heads, size, seq), BF),
+        pltpu.VMEM((heads, seq, size), BF),
+        pltpu.VMEM((width - LANES, LANES), F32),
+        pltpu.VMEM((PROMPT, cont), F32),
+        pltpu.VMEM((PROMPT, cont), BF),
+        pltpu.VMEM((width - LANES, LANES), F32),
+        pltpu.VMEM((seq, size), F32),
+        pltpu.VMEM((seq, size), F32),
+        pltpu.VMEM((size, seq), F32),
+        pltpu.VMEM((cont, LANES), jnp.int32),
+        pltpu.VMEM((buckets, width), F32),
+        pltpu.VMEM((buckets, LANES), F32),
+        pltpu.VMEM((model, own), F32),
+        pltpu.VMEM((4 * dp_count, model), F32),
+        pltpu.VMEM((heads, mp_count, local, 3 * size), BF),
+        pltpu.VMEM((heads, mp_count, local, 3 * size), BF),
+        dma(heads, 3),
+        dma(heads, mp_count),
+        pltpu.VMEM((dp_count,) + chunk, BF),
+        pltpu.VMEM((dp_count,) + chunk, BF),
+        dma(heads, dp_count),
+        dma(heads, dp_count),
     ]
-    for copy in shares:
-        copy.start()
-
-    def over(n, j):
-        whose = across if n == 2 else me
-        return remote(all_o.at[whose, j], all_o.at[whose, j], hsem.at[n, j], isem.at[n, j], mp=across if n == 1 else mate)
-
-    over(1, d).start()
-    over(0, d).start()
-    small_mp[me] = sum_dp(small_scattered, small_s, small_come)
-    small_swaps = [
-        remote(small_mp.at[me], small_mp.at[me], csem.at[n], dsem.at[n], mp=to) for n, to in enumerate((mate, across, diagonal))
-    ]
-    for copy in small_swaps:
-        copy.start()
-    for copy in small_swaps:
-        copy.wait_recv()
-    small_all[d] = small_mp[0] + small_mp[1] + small_mp[2] + small_mp[3]
-    small_shares = share_dp(small_all, vsem, zsem)
-    for copy in small_shares:
-        copy.start()
-    for k in range(1, dp_count):
-        j = lax.rem(d + dp_count - k, dp_count)
-        shares[k - 1].wait_recv()
-        over(1, j).start()
-        over(0, j).start()
-        last = lax.rem(d + dp_count - k + 1, dp_count)
-        over(1, last).wait_recv()
-        over(2, last).start()
-    last = lax.rem(d + 1, dp_count)
-    over(1, last).wait_recv()
-    over(2, last).start()
-    for copy in small_shares:
-        copy.wait_recv()
-    small_o[...] = small_all[...]
-    for j in range(dp_count):
-        over(0, j).wait_recv()
-        over(2, j).wait_recv()
-        for n in range(3):
-            over(n, j).wait_send()
-    for copy in small_swaps + scattered + small_scattered + small_shares + shares:
-        copy.wait_send()
-
-
-def dma(*shape):
-    return pltpu.SemaphoreType.DMA(shape) if shape else pltpu.SemaphoreType.DMA
-
-
-def mp_call(kernel, number, outs, scratch, *args):
-    specs = [layer_spec(*a) if isinstance(a, tuple) else VMEM for a in args]
+    if first:
+        scratch += [
+            pltpu.VMEM((dp_count, 8, model), F32),
+            pltpu.VMEM((dp_count, 8, model), F32),
+            pltpu.VMEM((mp_count, 8, model), F32),
+        ]
+        scratch += [dma(dp_count)] * 2 + [dma(3)] * 2 + [dma(dp_count)] * 2
+        scratch += [dma(heads, dp_count)] * 2 + [dma(3, heads, dp_count)] * 2 + [dma(dp_count)] * 2 + [dma(3, dp_count)] * 2
     return pl.pallas_call(
-        kernel,
+        functools.partial(back_kernel, layer, layers, heads, size, buckets),
         grid=(1,),
         out_shape=tuple(jax.ShapeDtypeStruct(shape, kind) for shape, kind in outs),
         in_specs=specs,
@@ -1222,7 +1271,11 @@
         compiler_params=pltpu.CompilerParams(
             collective_id=number, has_side_effects=True, vmem_limit_bytes=VMEM_BYTES
         ),
-    )(*[a[0] if isinstance(a, tuple) else a for a in args])
+    )(lens, *[a[0] if isinstance(a, tuple) else a for a in args])
+
+
+def dma(*shape):
+    return pltpu.SemaphoreType.DMA(shape) if shape else pltpu.SemaphoreType.DMA
 
 
 def gelu_grad(values):
@@ -1374,6 +1427,15 @@
             def _():
                 remote(ret_s.at[src], ret.at[index], rssem.at[src], rrsem.at[index], dp=s0, mp=row * 2 + cc).start()
 
+    def products(n, q, part):
+        half_groups = pl.ds(part * dp_count // 2, dp_count // 2)
+        count = dp_count * rows_a
+        if n == 0:
+            left, right = x_all[half_groups], ig_all[q, half_groups]
+        else:
+            left, right = hid_all[q, half_groups], g_all[half_groups]
+        return tn(left.reshape(count, model), right.reshape(count, model))
+
     def step(i, carry):
         @pl.when(i < dp_count)
         def _():
@@ -1409,6 +1471,14 @@
             for path in paths:
                 give_back(path, i - 2)
 
+        if backward:
+            for n in range(2):
+                for q in range(2):
+
+                    @pl.when(i == dp_count // 2 + 1 + 2 * n + q)
+                    def _():
+                        stage[n, q] = products(n, q, 0)
+
         return carry
 
     lax.fori_loop(0, dp_count + 2, step, 0)
@@ -1416,24 +1486,16 @@
         saved = pltpu.make_async_copy(x_all, x_o, xsem)
         saved.start()
     if backward:
-        count = dp_count * 2 * rows_a
-
-        def products(n, q):
-            if n == 0:
-                return tn(x_all[...].reshape(count, model), ig_all[q].reshape(count, model))
-            return tn(hid_all[q].reshape(count, model), g_all[...].reshape(count, model))
-
         outs = (gw_in_o, gw_out_o)
         copies = []
         for n in range(2):
-            stage[n] = products(n, 1 - core)
-            copy = remote(stage.at[n], outs[n].at[core], gsem.at[n], grsem.at[n], mp=mate)
+            stage[n, 1 - core] += products(n, 1 - core, 1)
+            copy = remote(stage.at[n, 1 - core], outs[n].at[core], gsem.at[n], grsem.at[n], mp=mate)
             copy.start()
             copies.append(copy)
         for n in range(2):
-            copies[n].wait_send()
-            stage[n] = products(n, core)
-            copy = pltpu.make_async_copy(stage.at[n], outs[n].at[core], glsem.at[n])
+            stage[n, core] += products(n, core, 1)
+            copy = pltpu.make_async_copy(stage.at[n, core], outs[n].at[core], glsem.at[n])
             copy.start()
             copies.append(copy)
     for path, result in zip(paths, results):
@@ -1476,7 +1538,7 @@
         saved.wait()
     if backward:
         for n in range(2):
-            copies[n].wait_recv()
+            copies[n].wait()
             copies[2 + n].wait()
 
 
@@ -1540,7 +1602,7 @@
             pltpu.VMEM((dp_count, rows, model), BF),
             pltpu.VMEM((2, dp_count, rows, model), BF),
             pltpu.VMEM((2, dp_count, rows, model), BF),
-            pltpu.VMEM((2, model, model), F32),
+            pltpu.VMEM((2, 2, model, model), F32),
             dma(2),
             dma(2),
             dma(2),
@@ -1557,52 +1619,68 @@
     )(*args)
 
 
-def spread_kernel(own, count, *refs):
-    parts, (gw_in, gw_out, _, _) = refs[:count], refs[count : count + 4]
-    qkv_o, attn_o, in_o, out_o, sem = refs[count + 4 :]
+def spread_kernel(size, buckets, count, *refs):
+    parts, grads, small = refs[:count], refs[count : 3 * count], refs[3 * count]
+    qkv_o, attn_o, in_o, out_o, gain_a_o, bias_o, gain_f_o, router_o, sem = refs[3 * count + 1 :]
     step = pl.program_id(0)
-    copies = [
-        pltpu.make_async_copy(gw_in.at[0], in_o.at[0, step], sem.at[0]),
-        pltpu.make_async_copy(gw_out.at[0], out_o.at[0, step], sem.at[1]),
-    ]
+    copies = []
+    for n in range(count):
+        copies.append(pltpu.make_async_copy(grads[2 * n].at[0], in_o.at[n, step], sem.at[2 * n]))
+        copies.append(pltpu.make_async_copy(grads[2 * n + 1].at[0], out_o.at[n, step], sem.at[2 * n + 1]))
     for copy in copies:
         copy.start()
-
     for n in range(count):
-        mp_count, blocks, rows, width = parts[n].shape
-        pieces = [parts[n][m].reshape(blocks * rows, width).astype(F32) for m in range(mp_count)]
-        qkv_o[n] = jnp.concatenate([p[:, t * own : (t + 1) * own] for t in range(3) for p in pieces], 1)
-        for m in range(mp_count):
-            attn_o[n, m * own : (m + 1) * own, :] = pieces[m][:, 3 * own :].T
+        mp_count, blocks, heads, rows, _ = parts[n].shape
+        pieces = [
+            parts[n][m, :, h].reshape(blocks * rows, 4 * size).astype(F32) for m in range(mp_count) for h in range(heads)
+        ]
+        qkv_o[n] = jnp.concatenate([p[:, t * size : (t + 1) * size] for t in range(3) for p in pieces], 1)
+        for number, p in enumerate(pieces):
+            attn_o[n, number * size : (number + 1) * size, :] = p[:, 3 * size :].T
+    lines = small.shape[0] // count
+    for n in range(count):
+        gain_a_o[n : n + 1, :] = small[n * lines, 0:1, :]
+        gain_f_o[n : n + 1, :] = small[n * lines, 1:2, :]
+        tiles = [small[n * lines + 1, :, i * LANES : (i + 1) * LANES] for i in range(buckets // 8)]
+        bias_o[n] = jnp.concatenate(tiles, 0).T[0 : bias_o.shape[1], :]
+        router_o[n] = jnp.concatenate([small[n * lines + i] for i in range(2, lines)], 0)
     for copy in copies:
         copy.wait()
 
 
-def spread_call(parts, own, grads, places):
-    mp_count, blocks, rows, width = parts[0].shape
+def spread_call(parts, grads, small, size, heads, buckets, experts):
+    mp_count, blocks, own_heads, rows, wide = parts[0].shape
     layers, model = len(parts), blocks * rows
     steps = grads[0].shape[0]
     return pl.pallas_call(
-        functools.partial(spread_kernel, own, layers),
+        functools.partial(spread_kernel, size, buckets, layers),
         grid=(steps,),
         out_shape=(
-            jax.ShapeDtypeStruct((layers, model, 3 * mp_count * own), F32),
-            jax.ShapeDtypeStruct((layers, mp_count * own, model), F32),
-        )
-        + tuple(jax.ShapeDtypeStruct(p.shape, F32) for p in places),
-        in_specs=[pl.BlockSpec((mp_count, blocks // steps, rows, width), lambda i: (0, i, 0, 0))] * layers
+            jax.ShapeDtypeStruct((layers, model, 3 * heads * size), F32),
+            jax.ShapeDtypeStruct((layers, heads * size, model), F32),
+            jax.ShapeDtypeStruct((layers,) + grads[0].shape, F32),
+            jax.ShapeDtypeStruct((layers,) + grads[1].shape, F32),
+            jax.ShapeDtypeStruct((layers, model), F32),
+            jax.ShapeDtypeStruct((layers, heads, buckets), F32),
+            jax.ShapeDtypeStruct((layers, model), F32),
+            jax.ShapeDtypeStruct((layers, experts, model), F32),
+        ),
+        in_specs=[pl.BlockSpec((mp_count, blocks // steps, own_heads, rows, wide), lambda i: (0, i, 0, 0, 0))] * layers
         + [pl.BlockSpec((1,) + g.shape[1:], lambda i: (i, 0, 0)) for g in grads]
-        + [ANY] * 2,
+        + [VMEM],
         out_specs=(
-            pl.BlockSpec((layers, model // steps, 3 * mp_count * own), lambda i: (0, i, 0)),
-            pl.BlockSpec((layers, mp_count * own, model // steps), lambda i: (0, 0, i)),
+            pl.BlockSpec((layers, model // steps, 3 * heads * size), lambda i: (0, i, 0)),
+            pl.BlockSpec((layers, heads * size, model // steps), lambda i: (0, 0, i)),
             ANY,
             ANY,
+            VMEM,
+            VMEM,
+            VMEM,
+            VMEM,
         ),
-        scratch_shapes=[dma(2)],
-        input_output_aliases={layers + 2: 2, layers + 3: 3},
+        scratch_shapes=[dma(2 * layers)],
         compiler_params=pltpu.CompilerParams(vmem_limit_bytes=VMEM_BYTES),
-    )(*parts, *grads, *places)
+    )(*parts, *grads, small)
 
 
 def fast_body(
@@ -1613,9 +1691,7 @@
     size = model // heads
     layers = w_qkv.shape[0]
     dp_count, mp_count = lax.axis_size("dp"), lax.axis_size("mp")
-    seq = local * mp_count
     own_heads = heads // mp_count
-    own = own_heads * size
     experts = dp_count * 2
     me = lax.axis_index("mp")
     block = (experts, 16, 7 * model // 2)
@@ -1625,37 +1701,29 @@
     cols = jnp.pad(pairs, ((0, 0), (0, 0), (0, 2)))
     rows = cols.transpose(0, 2, 1)
     vecs = bias_vectors(lax.dynamic_slice_in_dim(rel_bias, me * own_heads, own_heads, 1))
-    gain_a, gain_f = attn_gain[:, None], ffn_gain[:, None]
-    held = (mp_count, local, model)
-    chunk = (dp_count, model // dp_count, model)
-    gather = [pltpu.VMEM(held, BF), dma(3), dma(3)]
-
-    def swap(width):
-        return [pltpu.VMEM((mp_count, local, width), BF)], [dma(3), dma(3), dma()]
 
     kept = [None] * layers
-    back, far = None, [None, None]
+    back, far = None, None
     for l in range(layers):
         first, last = l == 0, l == layers - 1
-        normal = [(gain_a, l), (w_qkv, l), vecs[l], (w_attn, l), (gain_f, l), (router, l), (rows, l), (cols, l)]
+        normal = [attn_gain, (w_qkv, l), vecs[l], (w_attn, l), ffn_gain, (router, l), (rows, l), (cols, l)]
         if first:
             specials = [tokens[0], cotangent[0], (rows, layers - 1)]
         else:
             before = kept[l - 1]
             specials = [before["middle"], before["out"], (cols, l - 1), before["gates"]]
         if last:
-            specials.append(far[0])
+            specials += far
         got = pre_call(
             l, layers, l, own_heads, size, cont_lengths, normal, mp_count, dp_count, local, model, specials, block
         )
         got = [tokens[0]] + list(got) if first else list(got)
         names = ("stream", "normed", "qkv", "mixed", "lse", "middle", "ffn", "gates")
         kept[l] = k = dict(zip(names, got))
-        k["normed"] = k["normed"].reshape(seq, model)
         if first:
-            far[0] = got[9]
+            far = got[9:11]
         if last:
-            far[1] = got[9]
+            far = [far[0], got[9]]
             k["out"], back, k["gw_in"], k["gw_out"] = expert_call("both", l, 5, dp_count, got[8], far, None, w_in, w_out)
         else:
             k["out"], k["x_rows"] = expert_call("fwd", l, 4, dp_count, got[8], None, None, w_in, w_out)
@@ -1664,79 +1732,26 @@
     for l in reversed(range(layers)):
         k = kept[l]
         last = l == layers - 1
-        outs = [((local, model), F32), (held, BF), ((1, model), F32), ((experts, model), F32)]
-        args = [back, k["out"], flow, k["middle"], k["ffn"], k["gates"], (cols, l), (router, l), (gain_f, l)]
+        normal = [
+            vecs[l], back, k["out"], flow, k["middle"], k["ffn"], k["gates"], (cols, l), (router, l), ffn_gain,
+            k["normed"], k["qkv"], k["mixed"], k["lse"], (w_attn, l), (w_qkv, l), k["stream"], attn_gain,
+        ]
+        extra = [(rows, l - 1), (cols, l - 1), kept[l - 1]["gates"]] if last else [heads_sum, small]
+        got = back_call(
+            l, layers, 6 + last, own_heads, size, buckets, cont_lengths, normal, mp_count, dp_count, local, model, block, extra
+        )
         if last:
-            outs.append(((local, model), BF))
-            scratch = gather
-        else:
-            outs.append((chunk, BF))
-            args.append(heads_sum)
-            scratch = gather + [pltpu.VMEM(chunk, BF), dma(dp_count), dma(dp_count)]
-        got = mp_call(functools.partial(post_kernel, last), 6 + last, outs, scratch, *args)
-        grad, branch, k["ffn_gain"], k["router"] = got[:4]
-        if last:
-            output = got[4]
-            extra, more = "copy", (k["gw_in"], k["gw_out"])
-        else:
-            extra, more = "share", (got[4],)
-        got = attn_bwd(
-            cont_lengths, k["qkv"], k["normed"], branch.reshape(seq, model), w_attn, l, k["mixed"], k["lse"], vecs[l],
-            own_heads, size, extra, more, 8,
-        )
-        dqkv, heads_grad, dvecs = got[:3]
-        k["bias"] = bias_grads(dvecs, buckets)
-        args = [dqkv.reshape(mp_count, local, 3 * own), (w_qkv, l), k["stream"], (gain_a, l), grad]
-        space, sems = swap(3 * own)
-        if last:
-            places = got[3:]
+            flow, output, send, heads_sum, small = got
             b = kept[l - 1]
-            flow, k["attn_gain"], send, heads_sum = mp_call(
-                close_kernel, 9, [((local, model), F32), ((1, model), F32), (block, BF), (chunk[1:], BF)],
-                space + [pltpu.VMEM(chunk, BF)] * 2 + sems + [dma(dp_count)] * 2,
-                *args, (rows, l - 1), (cols, l - 1), b["gates"], heads_grad,
-            )
             back, b["gw_in"], b["gw_out"] = expert_call("bwd", l - 1, 10, dp_count, send, None, b["x_rows"], w_in, w_out)
         else:
-            (parts,) = got[3:]
-
-    small = []
-    for l in range(layers):
-        k = kept[l]
-        bias = lax.dynamic_update_slice_in_dim(jnp.zeros((heads, buckets), F32), k["bias"], me * own_heads, 0)
-        small += [k["attn_gain"] if l > 0 else jnp.zeros((1, model), F32), k["ffn_gain"]]
-        small += [jnp.pad(bias.reshape(1, -1), ((0, 5), (0, model - heads * buckets))), k["router"]]
-    lines = 8 + experts
-    share = -(-layers * lines // (8 * dp_count)) * 8
-    small = jnp.pad(jnp.concatenate(small, 0), ((0, share * dp_count - layers * lines), (0, 0)))
-    small = small.reshape(dp_count, share, model)
-    small_vmem = pltpu.VMEM(small.shape, F32)
-    flow, first_parts, small = mp_call(
-        last_kernel, 11, [((local, model), F32), ((mp_count,) + chunk, BF), (small.shape, F32)],
-        space
-        + [pltpu.VMEM(chunk, BF)] * 2
-        + [small_vmem, small_vmem, pltpu.VMEM((mp_count, share, model), F32), small_vmem]
-        + sems
-        + [dma(dp_count)] * 4
-        + [dma(3)] * 2
-        + [dma(dp_count)] * 4
-        + [dma(3, dp_count)] * 2,
-        *args, heads_grad, small,
+            flow, upper, lower, small = got
+    grads = [kept[l][name] for l in range(layers) for name in ("gw_in", "gw_out")]
+    grad_qkv, grad_attn, grad_in, grad_out, grad_a, grad_bias, grad_f, grad_router = spread_call(
+        [lower, upper], grads, small, size, heads, buckets, experts
     )
-    small = small.reshape(-1, model)[: layers * lines].reshape(layers, lines, model)
-    b = kept[0]
-    grad_qkv, grad_attn, grad_in, grad_out = spread_call([first_parts, parts], own, (b["gw_in"], b["gw_out"]), places)
     return (
-        output[None],
-        flow[None],
-        grad_qkv,
-        grad_attn,
-        small[:, 0],
-        small[:, 2, : heads * buckets].reshape(layers, heads, buckets),
-        small[:, 1],
-        small[:, 8:].transpose(0, 2, 1),
-        grad_in,
-        grad_out,
+        output[None], flow[None], grad_qkv, grad_attn, grad_a, grad_bias, grad_f, grad_router.transpose(0, 2, 1), grad_in, grad_out,
     )
 
 
@@ -1752,7 +1767,9 @@
         groups == 1
         and w_qkv.shape[0] == 2
         and mp_count == 4
-        and dp_count % 8 == 0
+        and dp_count == 8
+        and router.shape[2] == 16
+        and rel_bias.shape[2] == 32
         and heads % mp_count == 0
         and model // heads == 64
         and model % 256 == 0

time: 712 us -> 633 us (0.89)
  Pallas kernels: 685 us -> 611 us
    pallas_call x7 -> x3, Pallas kernels: 288 us -> 223 us  [the longest x2 199 us: back_call(): pl.pallas_call(functools.partial(back_kernel, layer, layers, heads, size,...]
where the time goes in v4:
time: 633 us; the launch traced here: 622 us
  Pallas kernels  611 us (97%)
  local copies, waits for them, and re-layouts  8.72 us (1%)
    pallas_call x3, Pallas kernels, expert_call(): pl.pallas_call(functools.partial(expert_kernel, mode, layer, dp_count), o...  284 us
    pallas_call x2, Pallas kernels, back_call(): pl.pallas_call(functools.partial(back_kernel, layer, layers, heads, size,...  199 us
    pallas_call x2, Pallas kernels, pre_call(): pl.pallas_call(functools.partial(pre_kernel, layer, layers, heads, size),...  104 us
    pallas_call x1, Pallas kernels, spread_call(): pl.pallas_call(functools.partial(spread_kernel, size, buckets, layers), g...  23.3 us

profile of v4, /device:TPU:17, one launch (start us, length us, event | category | flops | bytes accessed | tf_op | source)
XLA Modules:
  0.0 621.9 jit_solution(9458746675030406156)
XLA Ops:
  0.6 0.0 copy-start
  0.7 0.7 copy-done
  1.4 0.7 copy.70
  2.1 0.7 fusion.35
  2.8 0.2 select_reduce_fusion
  3.1 0.6 slice_bitcast_fusion
  3.7 0.2 copy.55
  3.9 1.7 copy.59.refs_6_.refs_9_
  5.6 0.8 fusion.36
  6.4 0.7 copy.60.refs_7_.refs_11_.refs_19_
  7.2 47.1 %shard_map.213 = (bf16[4,384,768]{2,1,0:T(8,128)(2,1)}, bf16[1536,576]{1,0:T(8,128)(2,1)}, bf16[1536,192]{1,0:T(8,128)(2,1)}, f32[3,1536]{1,0:T(4,128)}, f32[384...) custom-call(s32[1,8]{1,0:T(1,128)} %refs_0_.7, ...), custom_call_target="tpu_custom_call" | custom-call | tf_op jit(solution)/shard_map/pallas_call | solution.py:873
  54.3 80.2 %shard_map.214 = (bf16[16,16,2688]{2,1,0:T(8,128)(2,1)}, bf16[8,224,768]{2,1,0:T(8,128)(2,1)}) custom-call(bf16[16,16,2688]{2,1,0:T(8,128)(2,1)} %get-tuple-element.57.refs_0_, bf16[2,2,768,768]{3,2,1,0:T(8,128)(2,1)} %refs_2_.7, bf16[2,2,768,768]{3,2,1,0:T(8,128)(2,1)} %refs_3_.3), custom_call_target="tpu_custom_call" | custom-call | tf_op jit(solution)/shard_map/pallas_call | solution.py:1610
  134.6 57.0 %shard_map.215 = (f32[384,768]{1,0:T(8,128)}, bf16[4,384,768]{2,1,0:T(8,128)(2,1)}, bf16[1536,576]{1,0:T(8,128)(2,1)}, bf16[1536,192]{1,0:T(8,128)(2,1)}, f32[3,...) custom-call(s32[1,8]{1,0:T(1,128)} %refs_0_.7, ...), custom_call_target="tpu_custom_call" | custom-call | tf_op jit(solution)/shard_map/pallas_call | solution.py:873
  191.6 120.9 %shard_map.216 = (bf16[16,16,2688]{2,1,0:T(8,128)(2,1)}, bf16[16,16,2688]{2,1,0:T(8,128)(2,1)}, f32[2,768,768]{2,1,0:T(8,128)}, f32[2,768,768]{2,1,0:T(8,128)}) custom-call(bf16[16,16,2816]{2,1,0:T(8,128)(2,1)} %get-tuple-element.62.refs_0_, bf16[16,16,2688]{2,1,0:T(8,128)(2,1)} %get-tuple-element.60.refs_13_.refs_1_, ...), custom_call_target="tpu_custom_call" | custom-call | tf_op jit(solution)/shard_map/pallas_call | solution.py:1610
  312.5 76.5 %shard_map.217 = (f32[384,768]{1,0:T(8,128)}, bf16[384,768]{1,0:T(8,128)(2,1)}, bf16[16,16,2688]{2,1,0:T(8,128)(2,1)}, bf16[3,96,256]{2,1,0:T(8,128)(2,1)}, f32[4,8,768]{2,1,0:T(8,128)}) custom-call(s32[1,8]{1,0:T(1,128)} %refs_0_.7, f32[3,1408]{1,0:T(4,128)} %get-tuple-element.135.refs_3_.refs_1_, bf16[16,16,2688]{2,1,0:T(8,128)(2,1)} %get-tuple-element.64.refs_2_, ...), custom_call_target="tpu_custom_call" | custom-call | tf_op jit(solution)/shard_map/pallas_call | solution.py:1264
  388.9 83.0 %shard_map.218 = (bf16[16,16,2688]{2,1,0:T(8,128)(2,1)}, f32[2,768,768]{2,1,0:T(8,128)}, f32[2,768,768]{2,1,0:T(8,128)}) custom-call(bf16[16,16,2688]{2,1,0:T(8,128)(2,1)} %get-tuple-element.75.refs_0_, bf16[8,224,768]{2,1,0:T(8,128)(2,1)} %get-tuple-element.76.refs_1_, bf16[2,2,768,768]{3,2,1,0:T(8,128)(2,1)} %refs_2_.7, bf16[2,2,768,768]{3,2,1,0:T(8,128)(2,1)} %refs_3_.3), custom_call_target="tpu_custom_call" | custom-call | tf_op jit(solution)/shard_map/pallas_call | solution.py:1610
  471.9 123.0 %shard_map.219 = (f32[384,768]{1,0:T(8,128)}, bf16[4,8,3,96,256]{4,3,2,1,0:T(8,128)(2,1)}, bf16[4,8,3,96,256]{4,3,2,1,0:T(8,128)(2,1)}, f32[8,8,768]{2,1,0:T(8,128)}) custom-call(s32[1,8]{1,0:T(1,128)} %refs_0_.7, f32[3,1408]{1,0:T(4,128)} %get-tuple-element.134.refs_3_.refs_1_, bf16[16,16,2688]{2,1,0:T(8,128)(2,1)} %get-tuple-element.77.refs_2_, ...), custom_call_target="tpu_custom_call" | custom-call | tf_op jit(solution)/shard_map/pallas_call | solution.py:1264
  594.9 0.0 copy-start.3
  595.0 0.0 copy-start.1
  595.0 23.3 %shard_map.220 = (f32[2,768,2304]{2,1,0:T(8,128)}, f32[2,768,768]{2,1,0:T(8,128)}, f32[2,2,768,768]{3,2,1,0:T(8,128)}, f32[2,2,768,768]{3,2,1,0:T(8,128)}, f32[2...) custom-call(bf16[4,8,3,96,256]{4,3,2,1,0:T(8,128)(2,1)} %get-tuple-element.87.refs_0_, ...), custom_call_target="tpu_custom_call" | custom-call | tf_op jit(solution)/shard_map/pallas_call | solution.py:1655
  618.3 1.4 copy.64
  619.8 0.8 copy.73
  620.6 1.0 copy.74
  621.6 0.0 copy-done.1
  (10 shorter events, 0.1 us)
Async XLA Ops:
  0.6 0.7 copy-start
  594.9 24.8 %copy-start.3 = (bf16[384,768]{1,0:T(8,128)(2,1)S(1)}, bf16[384,768]{1,0:T(8,128)(2,1)}, u32[]{:S(2)}) copy-start(bf16[384,768]{1,0:T(8,128)(2,1)} %get-tuple-element.74) | copy-start | bytes 1769476
  595.0 26.6 %copy-start.1 = (f32[2,12,32]{2,0,1:T(2,128)S(1)}, f32[2,12,32]{2,0,1:T(2,128)}, u32[]{:S(2)}) copy-start(f32[2,12,32]{2,0,1:T(2,128)} %param.19) | copy-start | bytes 9220
  618.3 2.2 copy-start.2

commit v5 on v4

--- a/solution.py
+++ b/solution.py
@@ -520,6 +520,10 @@
     send[:, :, 3 * model : 3 * model + half] = tail.astype(BF).reshape(experts, tile, half)
 
 
+def columns(rows):
+    return rows[...].astype(F32).T.astype(jnp.int32)
+
+
 def scatter_gates(rows, gates, send, start):
     experts, tile, _ = send.shape
     tokens = rows.shape[1]
@@ -638,17 +642,20 @@
         return taken
 
     first, last = layer == 0, layer == layers - 1
-    lens, gain_a, w_qkv, vecs, w_attn, gain_f, router, rows, cols = take(9)
+    lens, gain_a, w_qkv_in, vecs, w_attn_in, gain_f, router, rows = take(8)
     if first:
         tokens, cotangent, far_rows = take(3)
     else:
-        before, returned, cols_in, gates_in = take(4)
+        before, returned, rows_in, gates_in = take(4)
+        cols_in = columns(rows_in)
     g_in, g_half = take(2) if last else (None, None)
     (stream_o,) = (None,) if first else take(1)
     normed_o, qkv_o, mixed_o, lse_o, middle_o, ffn_o, gates_o, send_o = take(8)
     (g_o,) = take(1) if first or last else (None,)
     (g_half_o,) = take(1) if first else (None,)
     held, hssem, hrsem = take(3)
+    w_qkv, w_attn, qkv_s, iosem = take(4)
+    (stream_s,) = (None,) if first else take(1)
     weight, q_s, k_s, vt_s, table, cont_bias, mixt, segc, out_s, mixed_s, mssem, mrsem = take(12)
     if first:
         g_send, g_held, gssem, grsem = take(4)
@@ -660,6 +667,16 @@
     seq, own = mixed_o.shape
     local, model = middle_o.shape
     parts = local // LANES
+    cols = columns(rows)
+    w_qkv_come = pltpu.make_async_copy(w_qkv_in.at[layer], w_qkv, iosem.at[0])
+    w_attn_come = pltpu.make_async_copy(w_attn_in.at[layer], w_attn, iosem.at[1])
+    normed_go = pltpu.make_async_copy(held, normed_o, iosem.at[2])
+    qkv_go = pltpu.make_async_copy(qkv_s, qkv_o, iosem.at[3])
+    goes = [normed_go, qkv_go]
+    if not first:
+        goes.append(pltpu.make_async_copy(stream_s, stream_o, iosem.at[4]))
+    w_qkv_come.start()
+    w_attn_come.start()
 
     barrier = pltpu.get_barrier_semaphore()
     for to in (mate, across, diagonal):
@@ -676,7 +693,8 @@
         stream = before[...]
         for j in range(2):
             stream = stream + gates_in[:, j : j + 1] * gather_rows(cols_in, j, returned)
-        stream_o[...] = stream
+        stream_s[...] = stream
+        goes[2].start()
     held[me] = (stream * mean_square_scale(stream) * gain_a[layer : layer + 1, :]).astype(BF)
     pl.semaphore_wait(barrier, count)
     over = remote(held.at[me], held.at[me], hssem.at[1], hrsem.at[1], mp=across)
@@ -714,6 +732,7 @@
         for n in range(2, dp_count):
             far_over(g_in, n).start()
 
+    w_qkv_come.wait()
     for m in range(model // own):
 
         @pl.when(me == m)
@@ -733,7 +752,7 @@
     def project(m):
         at = pl.ds(pl.multiple_of(m * local, LANES), local)
         part = nn(held[m], weight[...]).astype(BF)
-        qkv_o[at, :] = part
+        qkv_s[at, :] = part
         for h in range(heads):
             q_s[h, at, :] = part[:, h * size : (h + 1) * size] * BF(0.125)
             k_s[h, at, :] = part[:, own + h * size : own + (h + 1) * size]
@@ -747,6 +766,8 @@
     project(across)
     passed.wait_recv()
     project(diagonal)
+    normed_go.start()
+    qkv_go.start()
 
     def handed(n):
         return remote(out_s.at[n], mixed_s.at[me, n % parts], mssem.at[n], mrsem.at[me, n % parts], mp=n // parts)
@@ -776,7 +797,10 @@
         mixed_o[q0 : q0 + QB, :] = done
         for half in range(QB // LANES):
             n = q0 // LANES + half
-            out_s[n] = done[half * LANES : (half + 1) * LANES, :]
+            middle_row = half * LANES + LANES // 2
+            out_s[n] = jnp.concatenate(
+                [done[half * LANES : middle_row, :], done[middle_row : (half + 1) * LANES, :]], 1
+            )
 
             @pl.when(me == n // parts)
             def _():
@@ -786,16 +810,17 @@
             def _():
                 handed(n).start()
 
-    normed_o[...] = held[...]
+    w_attn_come.wait()
     middle = stream
     for m in range(mixed_s.shape[0]):
         for n in range(parts):
             pltpu.make_async_copy(mixed_s.at[m, n], mixed_s.at[m, n], mrsem.at[m, n]).wait()
-        middle = middle + nn(mixed_s[m].reshape(local, own), w_attn[m * own : (m + 1) * own, :])
+        halves = [mixed_s[m, n][:, i * own : (i + 1) * own] for n in range(parts) for i in range(2)]
+        middle = middle + nn(jnp.concatenate(halves, 0), w_attn[m * own : (m + 1) * own, :])
     middle_o[...] = middle
     ffn = (middle * mean_square_scale(middle) * gain_f[layer : layer + 1, :]).astype(BF)
     ffn_o[...] = ffn
-    logits = nn(ffn, router[...])
+    logits = nt(ffn, router[...])
     expert = lax.broadcasted_iota(jnp.int32, logits.shape, 1)
     chosen = [
         jnp.sum(jnp.where(expert == cols[:, j : j + 1], logits, 0.0), axis=1, keepdims=True) for j in range(2)
@@ -825,6 +850,8 @@
             far_over(g_in, n).wait()
             two = pl.ds(lax.rem(d + dp_count - n, dp_count) * 2, 2)
             g_o[two] = g_over[two]
+    for copy in goes:
+        copy.wait()
     for copy in (to_mate, over, passed):
         copy.wait_send()
     for n in range(seq // LANES):
@@ -840,6 +867,7 @@
     width = PROMPT + 3 * LANES
     args = list(normal) + list(specials)
     specs = [SMEM] + [layer_spec(*a) if isinstance(a, tuple) else VMEM for a in args]
+    specs[2] = specs[4] = ANY
     narrow = block[:2] + (7 * model // 2,)
     send = narrow[:2] + (narrow[2] + LANES,) if last else narrow
     outs = [] if first else [((local, model), F32)]
@@ -851,8 +879,13 @@
         outs.append((narrow, BF))
     if first:
         outs.append((narrow, BF))
+    out_specs = [VMEM] * len(outs)
+    for n in (0, 1) if first else (0, 1, 2):
+        out_specs[n] = ANY
     scratch = [
         pltpu.VMEM((mp_count, local, model), BF), dma(3), dma(3),
+        pltpu.VMEM((model, 3 * model), BF), pltpu.VMEM((model, model), BF), pltpu.VMEM((seq, 3 * own), BF), dma(5),
+        *([] if first else [pltpu.VMEM((local, model), F32)]),
         pltpu.VMEM((model, 3 * own), BF),
         pltpu.VMEM((heads, seq, size), BF),
         pltpu.VMEM((heads, seq, size), BF),
@@ -861,8 +894,8 @@
         pltpu.VMEM((heads, PROMPT, seq - PROMPT), F32),
         pltpu.VMEM((own, QB), F32),
         pltpu.VMEM((seq - PROMPT, LANES), jnp.int32),
-        pltpu.VMEM((seq // LANES, LANES, own), BF),
-        pltpu.VMEM((mp_count, local // LANES, LANES, own), BF),
+        pltpu.VMEM((seq // LANES, LANES // 2, 2 * own), BF),
+        pltpu.VMEM((mp_count, local // LANES, LANES // 2, 2 * own), BF),
         dma(seq // LANES),
         dma(mp_count, local // LANES),
     ]
@@ -875,7 +908,7 @@
         grid=(1,),
         out_shape=tuple(jax.ShapeDtypeStruct(shape, kind) for shape, kind in outs),
         in_specs=specs,
-        out_specs=tuple([VMEM] * len(outs)),
+        out_specs=tuple(out_specs),
         scratch_shapes=scratch,
         compiler_params=pltpu.CompilerParams(
             collective_id=number, has_side_effects=True, vmem_limit_bytes=VMEM_BYTES
@@ -899,24 +932,26 @@
         return taken
 
     first, last = layer == 0, layer == layers - 1
-    lens, vecs, back, returned, flow_in, middle, ffn, gates, cols, router, gain_f = take(11)
-    normed, qkv, mixed, lse, w_attn, w_qkv, stream, gain_a = take(8)
+    lens, vecs, back, returned, flow_in, middle, ffn, gates, rows_own, router, gain_f = take(11)
+    normed_in, qkv_in, mixed, lse, w_attn_in, w_qkv_in, stream, gain_a = take(8)
     if first:
         above, small_above = take(2)
     else:
-        rows_below, cols_below, gates_below = take(3)
+        rows_below, gates_below = take(2)
     (flow_o,) = take(1)
     if first:
-        up_o, all_o, small_o = take(3)
+        up_out, all_out, small_o = take(3)
     else:
         out_o, send_o, sum_o, small_o = take(4)
     held, hssem, hrsem = take(3)
+    normed, qkv, w_attn, w_qkv, insem = take(5)
     normed_t, q_s, k_s, v_s, kt_s, do_s, table, cont_bias, fold, dtable, dk_s, dv_s, dqt, segc, hot, bias_s, gw_a, router_s = take(18)
-    dq_s, dq_held, qssem, qrsem, part, come, pssem, prsem = take(8)
+    dq_s, dq_fold, dq_held, qssem, qrsem, part, come, pssem, prsem = take(9)
     if first:
         small_s, small_come, small_mp, tsem, usem, csem, dsem, vsem, zsem = take(9)
         assem, arsem, ossem, orsem = take(4)
         ussem, ursem, wssem, wrsem = take(4)
+        up_o, all_o, outsem = take(3)
     me, core, mate, across, diagonal = mp_places()
     d = lax.axis_index("dp")
     dp_count = part.shape[0]
@@ -925,6 +960,11 @@
     cont = seq - PROMPT
     width = vecs.shape[1]
     places = mixed.shape[0] // local
+    cols = columns(rows_own)
+    sources = (normed_in, qkv_in, w_attn_in.at[layer], w_qkv_in.at[layer])
+    come_in = [pltpu.make_async_copy(s, h, insem.at[n]) for n, (s, h) in enumerate(zip(sources, (normed, qkv, w_attn, w_qkv)))]
+    for copy in come_in:
+        copy.start()
 
     def dp_share(held_all, ssem, rsem, k):
         return remote(held_all.at[me, d], held_all.at[me, d], ssem.at[k], rsem.at[k], dp=lax.rem(d + k, dp_count), mp=me)
@@ -949,14 +989,14 @@
         out_o[...] = (middle[...] + gate[0] * keep[0] * outs[0] + gate[1] * keep[1] * outs[1]).astype(BF)
     gate_grad = [keep[j] * jnp.sum(flow * outs[j], axis=1, keepdims=True) for j in range(2)]
     shared = gate[0] * gate_grad[0] + gate[1] * gate_grad[1]
-    expert = lax.broadcasted_iota(jnp.int32, (local, router.shape[1]), 1)
+    expert = lax.broadcasted_iota(jnp.int32, (local, router.shape[0]), 1)
     logit_grad = 0.0
     for j in range(2):
         logit_grad = logit_grad + jnp.where(expert == cols[:, j : j + 1], gate[j] * (gate_grad[j] - shared), 0.0)
     high = logit_grad.astype(BF)
     low = (logit_grad - high.astype(F32)).astype(BF)
     upstream = gather_rows(cols, 0, back) + gather_rows(cols, 1, back)
-    upstream = upstream + nt(high, router[...]) + nt(low, router[...])
+    upstream = upstream + nn(high, router[...]) + nn(low, router[...])
     grad, gain_f_grad = norm_grads(middle[...], gain_f[layer : layer + 1, :], upstream)
     grad = grad + flow
     flow_o[...] = grad
@@ -968,6 +1008,8 @@
     to_mate.start()
 
     router_s[...] = tn(jnp.concatenate([high, low], 1), ffn[...])
+    for copy in come_in[:3]:
+        copy.wait()
     for i in range(seq // local):
         rows = pl.ds(i * local, local)
         normed_t[:, i * local : (i + 1) * local] = normed[i].astype(F32).T.astype(BF)
@@ -1005,7 +1047,7 @@
 
     def swap_copy(h, n):
         to = (mate, across, diagonal)[n]
-        return remote(dq_s.at[h, to], dq_held.at[h, me], qssem.at[h, n], qrsem.at[h, me], mp=to)
+        return remote(dq_fold.at[h, to], dq_held.at[h, me], qssem.at[h, n], qrsem.at[h, me], mp=to)
 
     def sum_copy(h, k):
         to = lax.rem(d + k, dp_count)
@@ -1092,13 +1134,13 @@
             dqt[:, q0 : q0 + QB] = dq
         for m in range(places):
             rows = slice(m * local, (m + 1) * local)
-            dq_s[h, m] = jnp.concatenate(
-                [dqt[:, rows].T.astype(BF), dk_s[rows, :].astype(BF), dv_s[rows, :].astype(BF)], 1
-            )
+            piece = jnp.concatenate([dqt[:, rows].T.astype(BF), dk_s[rows, :].astype(BF), dv_s[rows, :].astype(BF)], 1)
+            dq_s[m] = piece
+            dq_fold[h, m] = jnp.concatenate([piece[0 : local // 2, :], piece[local // 2 :, :]], 1)
         for n in (2, 1, 0):
             swap_copy(h, n).start()
-        pltpu.make_async_copy(dq_s.at[h, me], dq_held.at[h, me], qrsem.at[h, me]).start()
-        grads = nn(normed_t[...], dq_s[h].reshape(seq, 3 * size))
+        pltpu.make_async_copy(dq_fold.at[h, me], dq_held.at[h, me], qrsem.at[h, me]).start()
+        grads = nn(normed_t[...], dq_s[...].reshape(seq, 3 * size))
         for j in range(dp_count):
             rows = slice(j * part.shape[2], (j + 1) * part.shape[2])
             part[j, h, :, 0 : 3 * size] = grads[rows, :].astype(BF)
@@ -1127,17 +1169,20 @@
         rows = slice(j * part.shape[2], (j + 1) * part.shape[2])
         for h in range(heads):
             part[j, h, :, 3 * size :] = gw_a[rows, h * size : (h + 1) * size].astype(BF)
-    lax.fori_loop(0, heads, head, 0)
+    lax.fori_loop(0, heads, head, 0, unroll=True)
     if first:
         hand_on(0)
     for h in range(heads):
         for m in range(places):
             pltpu.make_async_copy(dq_held.at[h, m], dq_held.at[h, m], qrsem.at[h, m]).wait()
+    come_in[3].wait()
     upstream = 0.0
     for t in range(3):
-        piece = jnp.concatenate(
-            [dq_held[h, m, :, t * size : (t + 1) * size] for m in range(places) for h in range(heads)], 1
-        )
+        halves = []
+        for lane in (t * size, own + t * size):
+            found = [dq_held[h, m, :, lane : lane + size] for m in range(places) for h in range(heads)]
+            halves.append(jnp.concatenate(found, 1))
+        piece = jnp.concatenate(halves, 0)
         upstream = upstream + nt(piece, w_qkv[:, t * model : (t + 1) * model])
     inner, gain_a_grad = norm_grads(stream[...].astype(F32), gain_a[layer : layer + 1, :], upstream)
     flow = flow_o[...] + inner
@@ -1145,10 +1190,11 @@
     gains = jnp.concatenate([gain_a_grad, gain_f_grad, jnp.zeros((6, model), F32)], 0)
     tiles = [bias_s[8 * i : 8 * i + 8, :] for i in range(buckets // 8)]
     bias_rows = jnp.concatenate(tiles + [jnp.zeros((8, model - LANES * len(tiles)), F32)], 1)
-    router_grad = router_s[0 : router.shape[1], :] + router_s[router.shape[1] :, :]
-    small = [gains, bias_rows] + [router_grad[8 * i : 8 * i + 8, :] for i in range(router.shape[1] // 8)]
+    router_grad = router_s[0 : router.shape[0], :] + router_s[router.shape[0] :, :]
+    small = [gains, bias_rows] + [router_grad[8 * i : 8 * i + 8, :] for i in range(router.shape[0] // 8)]
 
     if not first:
+        cols_below = columns(rows_below)
         scatter_rows(
             rows_below,
             [(gates_below[:, j : j + 1] * cols_below[:, 4 + j : 5 + j].astype(F32) * flow).astype(BF) for j in range(2)],
@@ -1166,6 +1212,12 @@
         for copy in small_scattered:
             copy.start()
         finish_sum(heads - 1)
+        for j in range(dp_count):
+            mp_share(up_o, wssem, wrsem, 0, j).wait_recv()
+            mp_share(up_o, wssem, wrsem, 2, j).wait_recv()
+        up_go = pltpu.make_async_copy(up_o, up_out, outsem.at[0])
+        all_go = pltpu.make_async_copy(all_o, all_out, outsem.at[1])
+        up_go.start()
         hand_on(1)
         small_mp[me] = sum_dp(small_scattered, small_s, small_come)
         small_swaps = [
@@ -1187,13 +1239,14 @@
         for copy in small_shares:
             copy.wait_recv()
         for j in range(dp_count):
+            for h in range(heads):
+                head_pass(0, h, j).wait_recv()
+                head_pass(2, h, j).wait_recv()
+        all_go.start()
+        for j in range(dp_count):
             for n in range(3):
-                if n != 1:
-                    mp_share(up_o, wssem, wrsem, n, j).wait_recv()
                 mp_share(up_o, wssem, wrsem, n, j).wait_send()
                 for h in range(heads):
-                    if n != 1:
-                        head_pass(n, h, j).wait_recv()
                     head_pass(n, h, j).wait_send()
         for k in range(1, dp_count):
             dp_share(up_o, ussem, ursem, k).wait_send()
@@ -1201,6 +1254,8 @@
                 head_share(h, k).wait_send()
         for copy in small_swaps + small_scattered + small_shares:
             copy.wait_send()
+        up_go.wait()
+        all_go.wait()
     for copy in (to_mate, over, passed):
         copy.wait_send()
     for h in range(heads):
@@ -1217,6 +1272,8 @@
     cont = seq - PROMPT
     args = list(normal) + list(extra)
     specs = [SMEM] + [layer_spec(*a) if isinstance(a, tuple) else VMEM for a in args]
+    for n in (11, 12, 15, 16):
+        specs[n] = ANY
     chunk = (heads, model // dp_count, 4 * size)
     smalls = dp_count // layers
     outs = [((local, model), F32)]
@@ -1224,8 +1281,11 @@
         outs += [((mp_count, dp_count) + chunk, BF), ((mp_count, dp_count) + chunk, BF), ((dp_count, 8, model), F32)]
     else:
         outs += [((local, model), BF), (block, BF), (chunk, BF), ((smalls, 8, model), F32)]
+    out_specs = [VMEM] * len(outs)
     scratch = [
         pltpu.VMEM((mp_count, local, model), BF), dma(3), dma(3),
+        pltpu.VMEM((mp_count, local, model), BF), pltpu.VMEM((seq, 3 * own), BF),
+        pltpu.VMEM((model, model), BF), pltpu.VMEM((model, 3 * model), BF), dma(4),
         pltpu.VMEM((model, seq), BF),
         pltpu.VMEM((heads, seq, size), BF),
         pltpu.VMEM((heads, seq, size), BF),
@@ -1244,8 +1304,9 @@
         pltpu.VMEM((buckets, LANES), F32),
         pltpu.VMEM((model, own), F32),
         pltpu.VMEM((4 * dp_count, model), F32),
-        pltpu.VMEM((heads, mp_count, local, 3 * size), BF),
-        pltpu.VMEM((heads, mp_count, local, 3 * size), BF),
+        pltpu.VMEM((mp_count, local, 3 * size), BF),
+        pltpu.VMEM((heads, mp_count, local // 2, 6 * size), BF),
+        pltpu.VMEM((heads, mp_count, local // 2, 6 * size), BF),
         dma(heads, 3),
         dma(heads, mp_count),
         pltpu.VMEM((dp_count,) + chunk, BF),
@@ -1261,12 +1322,14 @@
         ]
         scratch += [dma(dp_count)] * 2 + [dma(3)] * 2 + [dma(dp_count)] * 2
         scratch += [dma(heads, dp_count)] * 2 + [dma(3, heads, dp_count)] * 2 + [dma(dp_count)] * 2 + [dma(3, dp_count)] * 2
+        scratch += [pltpu.VMEM((mp_count, dp_count) + chunk, BF)] * 2 + [dma(2)]
+        out_specs[1] = out_specs[2] = ANY
     return pl.pallas_call(
         functools.partial(back_kernel, layer, layers, heads, size, buckets),
         grid=(1,),
         out_shape=tuple(jax.ShapeDtypeStruct(shape, kind) for shape, kind in outs),
         in_specs=specs,
-        out_specs=tuple([VMEM] * len(outs)),
+        out_specs=tuple(out_specs),
         scratch_shapes=scratch,
         compiler_params=pltpu.CompilerParams(
             collective_id=number, has_side_effects=True, vmem_limit_bytes=VMEM_BYTES
@@ -1351,8 +1414,6 @@
         copies.append(pltpu.make_async_copy(x_in, x_all, xsem))
     for copy in copies:
         copy.start()
-    for copy in copies:
-        copy.wait()
 
     def source_of(g):
         return lax.rem(d + dp_count - g, dp_count)
@@ -1436,14 +1497,17 @@
             left, right = hid_all[q, half_groups], g_all[half_groups]
         return tn(left.reshape(count, model), right.reshape(count, model))
 
+    def arrive(g):
+        s0 = source_of(g)
+        for cc in range(2):
+            src = s0 * 2 + cc
+            pltpu.make_async_copy(recv_a.at[src], recv_a.at[src], asem.at[src]).wait()
+        forward_copy(s0).start()
+
     def step(i, carry):
         @pl.when(i < dp_count)
         def _():
-            s0 = source_of(i)
-            for cc in range(2):
-                src = s0 * 2 + cc
-                pltpu.make_async_copy(recv_a.at[src], recv_a.at[src], asem.at[src]).wait()
-            forward_copy(s0).start()
+            arrive(i)
 
         @pl.when(i + ahead < dp_count)
         def _():
@@ -1481,7 +1545,11 @@
 
         return carry
 
-    lax.fori_loop(0, dp_count + 2, step, 0)
+    arrive(0)
+    send_wave(ahead)
+    for copy in copies:
+        copy.wait()
+    lax.fori_loop(1, dp_count + 2, step, 0)
     if mode == "fwd":
         saved = pltpu.make_async_copy(x_all, x_o, xsem)
         saved.start()
@@ -1698,20 +1766,20 @@
     pairs = jnp.concatenate(
         [routes.reshape(layers, local, 2), slots.reshape(layers, local, 2), 1 - drops.reshape(layers, local, 2)], 2
     )
-    cols = jnp.pad(pairs, ((0, 0), (0, 0), (0, 2)))
-    rows = cols.transpose(0, 2, 1)
+    rows = jnp.pad(pairs.transpose(0, 2, 1), ((0, 0), (0, 2), (0, 0)))
+    router = router.transpose(0, 2, 1)
     vecs = bias_vectors(lax.dynamic_slice_in_dim(rel_bias, me * own_heads, own_heads, 1))
 
     kept = [None] * layers
     back, far = None, None
     for l in range(layers):
         first, last = l == 0, l == layers - 1
-        normal = [attn_gain, (w_qkv, l), vecs[l], (w_attn, l), ffn_gain, (router, l), (rows, l), (cols, l)]
+        normal = [attn_gain, w_qkv, vecs[l], w_attn, ffn_gain, (router, l), (rows, l)]
         if first:
             specials = [tokens[0], cotangent[0], (rows, layers - 1)]
         else:
             before = kept[l - 1]
-            specials = [before["middle"], before["out"], (cols, l - 1), before["gates"]]
+            specials = [before["middle"], before["out"], (rows, l - 1), before["gates"]]
         if last:
             specials += far
         got = pre_call(
@@ -1733,10 +1801,10 @@
         k = kept[l]
         last = l == layers - 1
         normal = [
-            vecs[l], back, k["out"], flow, k["middle"], k["ffn"], k["gates"], (cols, l), (router, l), ffn_gain,
-            k["normed"], k["qkv"], k["mixed"], k["lse"], (w_attn, l), (w_qkv, l), k["stream"], attn_gain,
+            vecs[l], back, k["out"], flow, k["middle"], k["ffn"], k["gates"], (rows, l), (router, l), ffn_gain,
+            k["normed"], k["qkv"], k["mixed"], k["lse"], w_attn, w_qkv, k["stream"], attn_gain,
         ]
-        extra = [(rows, l - 1), (cols, l - 1), kept[l - 1]["gates"]] if last else [heads_sum, small]
+        extra = [(rows, l - 1), kept[l - 1]["gates"]] if last else [heads_sum, small]
         got = back_call(
             l, layers, 6 + last, own_heads, size, buckets, cont_lengths, normal, mp_count, dp_count, local, model, block, extra
         )

time: 633 us -> 601 us (0.949)
  Pallas kernels: 611 us -> 582 us
    pallas_call x2, Pallas kernels: 199 us -> 186 us  [back_call(): pl.pallas_call(functools.partial(back_kernel, layer, layers, heads, size,...]
    pallas_call x2, Pallas kernels: 104 us -> 96.2 us  [pre_call(): pl.pallas_call(functools.partial(pre_kernel, layer, layers, heads, size),...]
    pallas_call x3, Pallas kernels: 284 us -> 277 us  [expert_call(): pl.pallas_call(functools.partial(expert_kernel, mode, layer, dp_count), o...]
where the time goes in v5:
time: 601 us; the launch traced here: 590 us
  Pallas kernels  582 us (97%)
    pallas_call x3, Pallas kernels, expert_call(): pl.pallas_call(functools.partial(expert_kernel, mode, layer, dp_count), o...  277 us
    pallas_call x2, Pallas kernels, back_call(): pl.pallas_call(functools.partial(back_kernel, layer, layers, heads, size,...  186 us
    pallas_call x2, Pallas kernels, pre_call(): pl.pallas_call(functools.partial(pre_kernel, layer, layers, heads, size),...  96.2 us
    pallas_call x1, Pallas kernels, spread_call(): pl.pallas_call(functools.partial(spread_kernel, size, buckets, layers), g...  23.3 us

profile of v5, /device:TPU:17, one launch (start us, length us, event | category | flops | bytes accessed | tf_op | source)
XLA Modules:
  0.0 590.0 jit_solution(11217964678307485617)
XLA Ops:
  0.6 0.0 copy-start
  0.7 0.7 copy-done
  1.4 0.7 fusion.35
  2.1 0.7 add_bitcast_fusion
  2.8 0.6 pad.4.refs_7_.refs_10_.refs_8_.refs_19_
  3.5 0.2 select_reduce_fusion
  3.7 0.6 slice_bitcast_fusion
  4.3 43.8 %shard_map.213 = (bf16[4,384,768]{2,1,0:T(8,128)(2,1)}, bf16[1536,576]{1,0:T(8,128)(2,1)}, bf16[1536,192]{1,0:T(8,128)(2,1)}, f32[3,1536]{1,0:T(4,128)}, f32[384...) custom-call(s32[1,8]{1,0:T(1,128)} %refs_0_.7, ...), custom_call_target="tpu_custom_call" | custom-call | tf_op jit(solution)/shard_map/pallas_call | solution.py:906
  48.1 77.1 %shard_map.214 = (bf16[16,16,2688]{2,1,0:T(8,128)(2,1)}, bf16[8,224,768]{2,1,0:T(8,128)(2,1)}) custom-call(bf16[16,16,2688]{2,1,0:T(8,128)(2,1)} %get-tuple-element.57.refs_0_, bf16[2,2,768,768]{3,2,1,0:T(8,128)(2,1)} %refs_2_.7, bf16[2,2,768,768]{3,2,1,0:T(8,128)(2,1)} %refs_3_.3), custom_call_target="tpu_custom_call" | custom-call | tf_op jit(solution)/shard_map/pallas_call | solution.py:1678
  125.2 52.4 %shard_map.215 = (f32[384,768]{1,0:T(8,128)}, bf16[4,384,768]{2,1,0:T(8,128)(2,1)}, bf16[1536,576]{1,0:T(8,128)(2,1)}, bf16[1536,192]{1,0:T(8,128)(2,1)}, f32[3,...) custom-call(s32[1,8]{1,0:T(1,128)} %refs_0_.7, ...), custom_call_target="tpu_custom_call" | custom-call | tf_op jit(solution)/shard_map/pallas_call | solution.py:906
  177.7 120.5 %shard_map.216 = (bf16[16,16,2688]{2,1,0:T(8,128)(2,1)}, bf16[16,16,2688]{2,1,0:T(8,128)(2,1)}, f32[2,768,768]{2,1,0:T(8,128)}, f32[2,768,768]{2,1,0:T(8,128)}) custom-call(bf16[16,16,2816]{2,1,0:T(8,128)(2,1)} %get-tuple-element.62.refs_0_, bf16[16,16,2688]{2,1,0:T(8,128)(2,1)} %get-tuple-element.60.refs_12_.refs_1_, ...), custom_call_target="tpu_custom_call" | custom-call | tf_op jit(solution)/shard_map/pallas_call | solution.py:1678
  298.2 66.2 %shard_map.217 = (f32[384,768]{1,0:T(8,128)}, bf16[384,768]{1,0:T(8,128)(2,1)}, bf16[16,16,2688]{2,1,0:T(8,128)(2,1)}, bf16[3,96,256]{2,1,0:T(8,128)(2,1)}, f32[4,8,768]{2,1,0:T(8,128)}) custom-call(s32[1,8]{1,0:T(1,128)} %refs_0_.7, f32[3,1408]{1,0:T(4,128)} %get-tuple-element.123.refs_3_.refs_1_, bf16[16,16,2688]{2,1,0:T(8,128)(2,1)} %get-tuple-element.64.refs_2_, ...), custom_call_target="tpu_custom_call" | custom-call | tf_op jit(solution)/shard_map/pallas_call | solution.py:1327
  364.4 79.0 %shard_map.218 = (bf16[16,16,2688]{2,1,0:T(8,128)(2,1)}, f32[2,768,768]{2,1,0:T(8,128)}, f32[2,768,768]{2,1,0:T(8,128)}) custom-call(bf16[16,16,2688]{2,1,0:T(8,128)(2,1)} %get-tuple-element.75.refs_0_, bf16[8,224,768]{2,1,0:T(8,128)(2,1)} %get-tuple-element.76.refs_1_, bf16[2,2,768,768]{3,2,1,0:T(8,128)(2,1)} %refs_2_.7, bf16[2,2,768,768]{3,2,1,0:T(8,128)(2,1)} %refs_3_.3), custom_call_target="tpu_custom_call" | custom-call | tf_op jit(solution)/shard_map/pallas_call | solution.py:1678
  443.5 119.7 %shard_map.219 = (f32[384,768]{1,0:T(8,128)}, bf16[4,8,3,96,256]{4,3,2,1,0:T(8,128)(2,1)}, bf16[4,8,3,96,256]{4,3,2,1,0:T(8,128)(2,1)}, f32[8,8,768]{2,1,0:T(8,128)}) custom-call(s32[1,8]{1,0:T(1,128)} %refs_0_.7, f32[3,1408]{1,0:T(4,128)} %get-tuple-element.122.refs_3_.refs_1_, bf16[16,16,2688]{2,1,0:T(8,128)(2,1)} %get-tuple-element.77.refs_2_, ...), custom_call_target="tpu_custom_call" | custom-call | tf_op jit(solution)/shard_map/pallas_call | solution.py:1327
  563.1 0.0 copy-start.3
  563.1 0.0 copy-start.1
  563.1 23.3 %shard_map.220 = (f32[2,768,2304]{2,1,0:T(8,128)}, f32[2,768,768]{2,1,0:T(8,128)}, f32[2,2,768,768]{3,2,1,0:T(8,128)}, f32[2,2,768,768]{3,2,1,0:T(8,128)}, f32[2...) custom-call(bf16[4,8,3,96,256]{4,3,2,1,0:T(8,128)(2,1)} %get-tuple-element.87.refs_0_, ...), custom_call_target="tpu_custom_call" | custom-call | tf_op jit(solution)/shard_map/pallas_call | solution.py:1723
  586.5 0.0 copy-start.2
  586.5 1.4 copy.29
  587.9 0.0 copy-done.3
  587.9 0.8 copy.32
  588.8 0.0 copy-done.2
  588.8 1.0 copy.33
  589.8 0.0 copy-done.1
  (6 shorter events, 0.1 us)
Async XLA Ops:
  0.6 0.7 copy-start
  563.1 24.8 %copy-start.3 = (bf16[384,768]{1,0:T(8,128)(2,1)S(1)}, bf16[384,768]{1,0:T(8,128)(2,1)}, u32[]{:S(2)}) copy-start(bf16[384,768]{1,0:T(8,128)(2,1)} %get-tuple-element.74) | copy-start | bytes 1769476
  563.1 26.6 %copy-start.1 = (f32[2,12,32]{2,0,1:T(2,128)S(1)}, f32[2,12,32]{2,0,1:T(2,128)}, u32[]{:S(2)}) copy-start(f32[2,12,32]{2,0,1:T(2,128)} %param.19) | copy-start | bytes 9220
  586.5 2.2 copy-start.2

commit v6 on v5

--- a/solution.py
+++ b/solution.py
@@ -399,7 +399,7 @@
 VMEM = pl.BlockSpec(memory_space=pltpu.VMEM)
 SMEM = pl.BlockSpec(memory_space=pltpu.SMEM)
 ANY = pl.BlockSpec(memory_space=pl.ANY)
-VMEM_BYTES = 60 << 20
+VMEM_BYTES = 61 << 20
 MESH = pl.DeviceIdType.MESH
 LANES = 128
 QB = 256
@@ -1030,6 +1030,12 @@
     hot[...] = (lax.broadcasted_iota(jnp.int32, (buckets, width), 0) == bucket).astype(F32)
     bias_s[...] = jnp.zeros_like(bias_s)
 
+    def tables(h, carry):
+        bias_stage(vecs[pl.ds(h, 1), :], lens, table.at[h], cont_bias.at[h])
+        return carry
+
+    lax.fori_loop(0, heads, tables, 0)
+
     def receive(m):
         dmix = nt(held[m], w_attn[pl.ds(pl.multiple_of(me * own, size), own), :]).astype(BF)
         for h in range(heads):
@@ -1088,7 +1094,6 @@
             head_pass(2, h, j).start()
 
     def head(h, carry):
-        bias_stage(vecs[pl.ds(h, 1), :], lens, table, cont_bias)
         dtable[...] = jnp.zeros_like(dtable)
         dk_s[...] = jnp.zeros_like(dk_s)
         dv_s[...] = jnp.zeros_like(dv_s)
@@ -1110,7 +1115,7 @@
 
             query = q_s[h, q0 : q0 + QB, :]
             dout = do_s[h, q0 : q0 + QB, :]
-            scored = scores_of(k_s, query, table, cont_bias, segc, seg_row, block, h)
+            scored = scores_of(k_s, query, table.at[h], cont_bias.at[h], segc, seg_row, block, h)
             lse_row = lse[pl.ds(h, 1), q0 : q0 + QB]
             kept, delta = [], 0.0
             for k0, k1, s in scored:
@@ -1292,8 +1297,8 @@
         pltpu.VMEM((heads, seq, size), BF),
         pltpu.VMEM((heads, size, seq), BF),
         pltpu.VMEM((heads, seq, size), BF),
-        pltpu.VMEM((width - LANES, LANES), F32),
-        pltpu.VMEM((PROMPT, cont), F32),
+        pltpu.VMEM((heads, width - LANES, LANES), F32),
+        pltpu.VMEM((heads, PROMPT, cont), F32),
         pltpu.VMEM((PROMPT, cont), BF),
         pltpu.VMEM((width - LANES, LANES), F32),
         pltpu.VMEM((seq, size), F32),
@@ -1379,7 +1384,7 @@
     half = model // 2
     rows_a = x_all.shape[1] // 2
     tile = sending.shape[1]
-    ahead = 3
+    ahead = 2
 
     barrier = pltpu.get_barrier_semaphore()
 
@@ -1710,7 +1715,7 @@
         gain_a_o[n : n + 1, :] = small[n * lines, 0:1, :]
         gain_f_o[n : n + 1, :] = small[n * lines, 1:2, :]
         tiles = [small[n * lines + 1, :, i * LANES : (i + 1) * LANES] for i in range(buckets // 8)]
-        bias_o[n] = jnp.concatenate(tiles, 0).T[0 : bias_o.shape[1], :]
+        bias_o[:, n : n + 1, :] = jnp.concatenate(tiles, 0).T[0 : bias_o.shape[0], :].reshape(bias_o.shape[0], 1, buckets)
         router_o[n] = jnp.concatenate([small[n * lines + i] for i in range(2, lines)], 0)
     for copy in copies:
         copy.wait()
@@ -1729,7 +1734,7 @@
             jax.ShapeDtypeStruct((layers,) + grads[0].shape, F32),
             jax.ShapeDtypeStruct((layers,) + grads[1].shape, F32),
             jax.ShapeDtypeStruct((layers, model), F32),
-            jax.ShapeDtypeStruct((layers, heads, buckets), F32),
+            jax.ShapeDtypeStruct((heads, layers, buckets), F32),
             jax.ShapeDtypeStruct((layers, model), F32),
             jax.ShapeDtypeStruct((layers, experts, model), F32),
         ),
@@ -1819,7 +1824,7 @@
         [lower, upper], grads, small, size, heads, buckets, experts
     )
     return (
-        output[None], flow[None], grad_qkv, grad_attn, grad_a, grad_bias, grad_f, grad_router.transpose(0, 2, 1), grad_in, grad_out,
+        output[None], flow[None], grad_qkv, grad_attn, grad_a, grad_bias.transpose(1, 0, 2), grad_f, grad_router.transpose(0, 2, 1), grad_in, grad_out,
     )
 
 

time: 601 us -> 588 us (0.978)
  Pallas kernels: 582 us -> 569 us
    pallas_call x2, Pallas kernels: 186 us -> 177 us  [back_call(): pl.pallas_call(functools.partial(back_kernel, layer, layers, heads, size,...]
where the time goes in v6:
time: 588 us; the launch traced here: 577 us
  Pallas kernels  569 us (97%)
    pallas_call x3, Pallas kernels, expert_call(): pl.pallas_call(functools.partial(expert_kernel, mode, layer, dp_count), o...  273 us
    pallas_call x2, Pallas kernels, back_call(): pl.pallas_call(functools.partial(back_kernel, layer, layers, heads, size,...  177 us
    pallas_call x2, Pallas kernels, pre_call(): pl.pallas_call(functools.partial(pre_kernel, layer, layers, heads, size),...  96.3 us
    pallas_call x1, Pallas kernels, spread_call(): pl.pallas_call(functools.partial(spread_kernel, size, buckets, layers), g...  23.3 us

profile of v6, /device:TPU:17, one launch (start us, length us, event | category | flops | bytes accessed | tf_op | source)
XLA Modules:
  0.0 576.6 jit_solution(9683550139026103210)
XLA Ops:
  0.6 0.0 copy-start
  0.7 0.7 copy-done
  1.4 0.7 fusion.35
  2.1 0.7 add_bitcast_fusion
  2.8 0.6 pad.4.refs_7_.refs_10_.refs_8_.refs_19_
  3.5 0.2 select_reduce_fusion
  3.7 0.6 slice_bitcast_fusion
  4.3 43.8 %shard_map.213 = (bf16[4,384,768]{2,1,0:T(8,128)(2,1)}, bf16[1536,576]{1,0:T(8,128)(2,1)}, bf16[1536,192]{1,0:T(8,128)(2,1)}, f32[3,1536]{1,0:T(4,128)}, f32[384...) custom-call(s32[1,8]{1,0:T(1,128)} %refs_0_.7, ...), custom_call_target="tpu_custom_call" | custom-call | tf_op jit(solution)/shard_map/pallas_call | solution.py:906
  48.1 77.1 %shard_map.214 = (bf16[16,16,2688]{2,1,0:T(8,128)(2,1)}, bf16[8,224,768]{2,1,0:T(8,128)(2,1)}) custom-call(bf16[16,16,2688]{2,1,0:T(8,128)(2,1)} %get-tuple-element.57.refs_0_, bf16[2,2,768,768]{3,2,1,0:T(8,128)(2,1)} %refs_2_.7, bf16[2,2,768,768]{3,2,1,0:T(8,128)(2,1)} %refs_3_.3), custom_call_target="tpu_custom_call" | custom-call | tf_op jit(solution)/shard_map/pallas_call | solution.py:1683
  125.3 52.5 %shard_map.215 = (f32[384,768]{1,0:T(8,128)}, bf16[4,384,768]{2,1,0:T(8,128)(2,1)}, bf16[1536,576]{1,0:T(8,128)(2,1)}, bf16[1536,192]{1,0:T(8,128)(2,1)}, f32[3,...) custom-call(s32[1,8]{1,0:T(1,128)} %refs_0_.7, ...), custom_call_target="tpu_custom_call" | custom-call | tf_op jit(solution)/shard_map/pallas_call | solution.py:906
  177.8 116.5 %shard_map.216 = (bf16[16,16,2688]{2,1,0:T(8,128)(2,1)}, bf16[16,16,2688]{2,1,0:T(8,128)(2,1)}, f32[2,768,768]{2,1,0:T(8,128)}, f32[2,768,768]{2,1,0:T(8,128)}) custom-call(bf16[16,16,2816]{2,1,0:T(8,128)(2,1)} %get-tuple-element.62.refs_0_, bf16[16,16,2688]{2,1,0:T(8,128)(2,1)} %get-tuple-element.60.refs_12_.refs_1_, ...), custom_call_target="tpu_custom_call" | custom-call | tf_op jit(solution)/shard_map/pallas_call | solution.py:1683
  294.4 62.0 %shard_map.217 = (f32[384,768]{1,0:T(8,128)}, bf16[384,768]{1,0:T(8,128)(2,1)}, bf16[16,16,2688]{2,1,0:T(8,128)(2,1)}, bf16[3,96,256]{2,1,0:T(8,128)(2,1)}, f32[4,8,768]{2,1,0:T(8,128)}) custom-call(s32[1,8]{1,0:T(1,128)} %refs_0_.7, f32[3,1408]{1,0:T(4,128)} %get-tuple-element.103.refs_3_.refs_1_, bf16[16,16,2688]{2,1,0:T(8,128)(2,1)} %get-tuple-element.64.refs_2_, ...), custom_call_target="tpu_custom_call" | custom-call | tf_op jit(solution)/shard_map/pallas_call | solution.py:1332
  356.3 79.2 %shard_map.218 = (bf16[16,16,2688]{2,1,0:T(8,128)(2,1)}, f32[2,768,768]{2,1,0:T(8,128)}, f32[2,768,768]{2,1,0:T(8,128)}) custom-call(bf16[16,16,2688]{2,1,0:T(8,128)(2,1)} %get-tuple-element.75.refs_0_, bf16[8,224,768]{2,1,0:T(8,128)(2,1)} %get-tuple-element.76.refs_1_, bf16[2,2,768,768]{3,2,1,0:T(8,128)(2,1)} %refs_2_.7, bf16[2,2,768,768]{3,2,1,0:T(8,128)(2,1)} %refs_3_.3), custom_call_target="tpu_custom_call" | custom-call | tf_op jit(solution)/shard_map/pallas_call | solution.py:1683
  435.5 115.0 %shard_map.219 = (f32[384,768]{1,0:T(8,128)}, bf16[4,8,3,96,256]{4,3,2,1,0:T(8,128)(2,1)}, bf16[4,8,3,96,256]{4,3,2,1,0:T(8,128)(2,1)}, f32[8,8,768]{2,1,0:T(8,128)}) custom-call(s32[1,8]{1,0:T(1,128)} %refs_0_.7, f32[3,1408]{1,0:T(4,128)} %get-tuple-element.102.refs_3_.refs_1_, bf16[16,16,2688]{2,1,0:T(8,128)(2,1)} %get-tuple-element.77.refs_2_, ...), custom_call_target="tpu_custom_call" | custom-call | tf_op jit(solution)/shard_map/pallas_call | solution.py:1332
  550.5 0.0 copy-start.3
  550.6 0.0 copy-start.1
  550.6 23.3 %shard_map.220 = (f32[2,768,2304]{2,1,0:T(8,128)}, f32[2,768,768]{2,1,0:T(8,128)}, f32[2,2,768,768]{3,2,1,0:T(8,128)}, f32[2,2,768,768]{3,2,1,0:T(8,128)}, f32[2...) custom-call(bf16[4,8,3,96,256]{4,3,2,1,0:T(8,128)(2,1)} %get-tuple-element.87.refs_0_, ...), custom_call_target="tpu_custom_call" | custom-call | tf_op jit(solution)/shard_map/pallas_call | solution.py:1728
  573.9 0.0 copy-start.2
  573.9 0.0 copy-done.3
  573.9 0.8 copy.30
  574.8 0.6 copy-done.2
  575.4 1.0 copy.31
  576.4 0.0 copy-done.1
  (6 shorter events, 0.1 us)
Async XLA Ops:
  0.6 0.7 copy-start
  550.5 23.4 %copy-start.3 = (bf16[384,768]{1,0:T(8,128)(2,1)S(1)}, bf16[384,768]{1,0:T(8,128)(2,1)}, u32[]{:S(2)}) copy-start(bf16[384,768]{1,0:T(8,128)(2,1)} %get-tuple-element.74) | copy-start | bytes 1769476
  550.6 25.9 %copy-start.1 = (f32[2,12,32]{2,0,1:T(2,128)S(1)}, f32[2,12,32]{2,0,1:T(2,128)}, u32[]{:S(2)}) copy-start(f32[2,12,32]{2,0,1:T(2,128)} %param.19) | copy-start | bytes 9220
  573.9 1.5 copy-start.2
